TPU v7x, 256 devices: a whole 4x4x8 slice. The times are simulated.
256 devices in a mesh: group: 8 (over y, core), expert: 32 (over x, z).
Axes of the slice: x: 4, y: 4, z: 8, core: 2. Of those that a mesh axis runs over, the one named last changes fastest.
Arguments:
- tokens: bfloat16 [5120, 3584], P(('group', 'expert')), may hold values from -6 to 6
- expert_ids: int32 [5120, 8], P(('group', 'expert')), may hold values from 0 to 127, all different within a row; in each aligned block of 20 rows (0 to 19, 20 to 39, ...) at most 2 rows name the same one
- route_weights: float32 [5120, 8], P(('group', 'expert')), may hold values from 0.1 to 1
- w_gate: bfloat16 [8, 32, 3584, 512], P('group', 'expert'), may hold values from -0.09375 to 0.09375
- w_up: bfloat16 [8, 32, 3584, 512], P('group', 'expert'), may hold values from -0.09375 to 0.09375
- w_down: bfloat16 [8, 32, 512, 3584], P('group', 'expert'), may hold values from -0.1875 to 0.1875
Outputs:
- mixed: bfloat16 [5120, 3584], P(('group', 'expert'))
Inputs may be any that keep to these rules, and one draw needn't show every extreme that they name: `expert_ids`: each row names 8 different experts. Within the tokens of one device (aligned blocks of 20 rows) no expert is named by more than 2 rows, a bound that some block reaches.
All inputs are finite; a program needn't handle non-finite values.
Results may differ from a plain program's by a relative error of at most 0.0065.
Values may be sent and summed in bfloat16 or wider, within the bound.
No kernel may reach another device: no remote copies, remote signals or barrier semaphores. Data moves between devices by JAX's collectives and lax.ppermute only.
A program may use at most 64 MiB of HBM per device.

v0:
```python
import jax
import jax.numpy as jnp
from jax import lax
from jax.sharding import PartitionSpec as P


def on_device(tokens, expert_ids, route_weights, w_gate, w_up, w_down):
    groups = lax.axis_size("group")
    members = lax.axis_size("expert")
    pairs = groups // 2
    experts = pairs * members
    tok_rows, features = tokens.shape
    top_count = expert_ids.shape[1]
    capacity = max(2, (3 * tok_rows * top_count + 2 * experts - 1) // (2 * experts))
    entries = tok_rows * top_count
    flat_ids = expert_ids.reshape(entries)
    one_hot = (flat_ids[:, None] == jnp.arange(experts, dtype=jnp.int32)[None, :]).astype(
        jnp.float32
    )
    order = jnp.arange(entries, dtype=jnp.int32)
    earlier = (order[:, None] > order[None, :]).astype(jnp.float32)
    before = jnp.dot(earlier, one_hot, precision=lax.Precision.HIGHEST)
    slot_index = jnp.sum(before * one_hot, axis=1).astype(jnp.int32)
    target = flat_ids * capacity + slot_index
    token_index = order // top_count
    source_row = jnp.zeros((experts * capacity,), jnp.int32).at[target].set(token_index)
    filled = jnp.zeros((experts * capacity,), jnp.bool_).at[target].set(True)
    outgoing = jnp.where(filled[:, None], tokens[source_row], jnp.zeros((), tokens.dtype))
    outgoing = outgoing.reshape(pairs, members, capacity, features)
    gate_cols = w_gate[0, 0]
    up_cols = w_up[0, 0]
    down_rows = w_down[0, 0]
    doubled = jnp.repeat(outgoing, 2, axis=0)
    received = lax.all_to_all(doubled, "group", split_axis=0, concat_axis=0, tiled=True)
    arrived_rows = lax.all_to_all(received, "expert", split_axis=1, concat_axis=1, tiled=True)
    item_count = arrived_rows.shape[0]
    row_block = arrived_rows.reshape(-1, features)
    gate_act = jnp.dot(row_block, gate_cols, preferred_element_type=jnp.float32)
    up_act = jnp.dot(row_block, up_cols, preferred_element_type=jnp.float32)
    hidden = (jax.nn.silu(gate_act) * up_act).astype(jnp.bfloat16)
    partial_value = jnp.dot(hidden, down_rows, preferred_element_type=jnp.float32).astype(
        jnp.bfloat16
    )
    partial_value = partial_value.reshape(item_count, members, capacity, features)
    returned = lax.all_to_all(partial_value, "expert", split_axis=1, concat_axis=1, tiled=True)
    arrived = lax.all_to_all(returned, "group", split_axis=0, concat_axis=0, tiled=True)
    pair_parts = arrived.reshape(pairs, 2, members, capacity, features)
    outputs = (pair_parts[:, 0].astype(jnp.float32) + pair_parts[:, 1].astype(jnp.float32)).astype(
        jnp.bfloat16
    )
    outputs = outputs.reshape(experts * capacity, features)
    gathered = outputs[target].astype(jnp.float32) * route_weights.reshape(entries)[:, None]
    mixed = jnp.sum(gathered.reshape(tok_rows, top_count, features), axis=1)
    return mixed.astype(jnp.bfloat16)


def solution(mesh):
    return jax.shard_map(
        on_device,
        mesh=mesh,
        in_specs=(
            P(("group", "expert"), None),
            P(("group", "expert"), None),
            P(("group", "expert"), None),
            P("group", "expert", None, None),
            P("group", "expert", None, None),
            P("group", "expert", None, None),
        ),
        out_specs=P(("group", "expert"), None),
        check_vma=False,
    )
```

profile of v0, /device:TPU:8, one launch (start us, length us, event | category | flops | bytes accessed | tf_op | source)
XLA Modules:
  0.0 359.5 jit_solution(10869463383821203295)
XLA Ops:
  0.7 0.8 copy.31
  2.1 1.1 scatter_custom_fusion.1
  3.3 1.7 gather_fusion
  5.0 1.7 gather.9
  6.7 1.1 scatter_custom_fusion
  8.0 3.3 broadcast_select_fusion
  11.3 3.7 %broadcast_in_dim.39 = bf16[4,2,32,2,3584]{4,3,2,1,0:T(2,128)(2,1)} broadcast(bf16[4,32,2,3584]{3,2,1,0:T(2,128)(2,1)S(1)} %broadcast_select_fusion), dimensions={0,2,3,4} | broadcast | bytes 5505024 | tf_op jit(solution)/shard_map/broadcast_in_dim | solution.py:33
  14.9 48.9 %all_to_all.20 = bf16[8,32,2,3584]{3,2,1,0:T(2,128)(2,1)S(1)} all-to-all(bf16[8,32,2,3584]{3,2,1,0:T(2,128)(2,1)} %bitcast.34), channel_id=1, replica_groups=mesh['group'=8,'expert'=32] {'group'}, dimensions={0} | all-to-all | bytes 7340032 | tf_op jit(solution)/shard_map/all_to_all | solution.py:34
  63.9 3.8 %copy.32 = bf16[8,32,2,3584]{3,2,0,1:T(2,128)(2,1)S(1)} copy(bf16[8,32,2,3584]{3,2,1,0:T(2,128)(2,1)S(1)} %all_to_all.20) | data formatting | bytes 7340032 | tf_op jit(solution)/shard_map/all_to_all | solution.py:34
  67.7 95.1 %all_to_all.21 = bf16[8,32,2,3584]{3,2,0,1:T(2,128)(2,1)S(1)} all-to-all(bf16[8,32,2,3584]{3,2,0,1:T(2,128)(2,1)S(1)} %copy.32), channel_id=1, replica_groups=mesh['group'=8,'expert'=32] {'expert'}, dimensions={1} | all-to-all | bytes 7340032 | tf_op jit(solution)/shard_map/all_to_all | solution.py:35
  162.8 4.7 %copy.33 = bf16[8,32,2,3584]{3,2,1,0:T(2,128)(2,1)} copy(bf16[8,32,2,3584]{3,2,0,1:T(2,128)(2,1)S(1)} %all_to_all.21) | data formatting | bytes 7340032 | tf_op jit(solution)/shard_map/all_to_all | solution.py:35
  167.4 8.4 %reshape.72 = bf16[512,3584]{1,0:T(8,128)(2,1)} reshape(bf16[8,32,2,3584]{3,2,1,0:T(2,128)(2,1)} %copy.33) | data formatting | bytes 7340032 | tf_op jit(solution)/shard_map/reshape | solution.py:37
  175.8 5.2 %fusion.3 = f32[512,512]{1,0:T(8,128)S(1)} fusion(bf16[512,3584]{1,0:T(8,128)(2,1)} %reshape.72, bf16[1,1,3584,512]{3,2,1,0:T(8,128)(2,1)} %param.9), kind=kOutput, calls=%fused_computation.8 | convolution fusion | flops 1879048192 | bytes 8388608 | tf_op jit(solution)/shard_map/dot_general | solution.py:38
  181.0 10.1 %convolution_convert_fusion = bf16[512,3584]{1,0:T(8,128)(2,1)} fusion(bf16[1,1,512,3584]{3,2,1,0:T(8,128)(2,1)} %param.11, bf16[512,3584]{1,0:T(8,128)(2,1)} %reshape.72, bf16[1,1,3584,512]{3,2,1,0:T(8,128)(2,1)} %param.10, f32[512,512]{1,0:T(8,128)S(1)} %fusion.3), kind=kOutput, calls=%fused_computation.4 | convolution fusion | flops 3761504256 | bytes 15728640 | tf_op jit(solution)/shard_map/dot_general | solution.py:41
  191.1 8.1 %reshape.73 = bf16[8,32,2,3584]{3,2,1,0:T(2,128)(2,1)} reshape(bf16[512,3584]{1,0:T(8,128)(2,1)} %convolution_convert_fusion) | data formatting | bytes 7340032 | tf_op jit(solution)/shard_map/reshape | solution.py:44
  199.3 5.8 %copy.34 = bf16[8,32,2,3584]{3,2,0,1:T(2,128)(2,1)S(1)} copy(bf16[8,32,2,3584]{3,2,1,0:T(2,128)(2,1)} %reshape.73) | data formatting | bytes 7340032 | tf_op jit(solution)/shard_map/reshape | solution.py:44
  205.1 88.9 %all_to_all.22 = bf16[8,32,2,3584]{3,2,0,1:T(2,128)(2,1)S(1)} all-to-all(bf16[8,32,2,3584]{3,2,0,1:T(2,128)(2,1)S(1)} %copy.34), channel_id=1, replica_groups=mesh['group'=8,'expert'=32] {'expert'}, dimensions={1} | all-to-all | bytes 7340032 | tf_op jit(solution)/shard_map/all_to_all | solution.py:45
  294.0 4.7 %copy.35 = bf16[8,32,2,3584]{3,2,1,0:T(2,128)(2,1)} copy(bf16[8,32,2,3584]{3,2,0,1:T(2,128)(2,1)S(1)} %all_to_all.22) | data formatting | bytes 7340032 | tf_op jit(solution)/shard_map/all_to_all | solution.py:45
  298.6 6.0 %all-to-all-start.3 = ((bf16[8,32,2,3584]{3,2,1,0:T(2,128)(2,1)}), bf16[8,32,2,3584]{3,2,1,0:T(2,128)(2,1)}, u32[]{:S(2)}, u32[]{:S(2)}) async-start(bf16[8,32,2,3584]{3,2,1,0:T(2,128)(2,1)} %copy.35), calls=%async_computation.3 | async-start | bytes 7340032 | tf_op jit(solution)/shard_map/all_to_all | solution.py:46
  304.7 42.6 %all-to-all-done.3 = bf16[8,32,2,3584]{3,2,1,0:T(2,128)(2,1)} async-done(((bf16[8,32,2,3584]{3,2,1,0:T(2,128)(2,1)}), bf16[8,32,2,3584]{3,2,1,0:T(2,128)(2,1)}, u32[]{:S(2)}, u32[]{:S(2)}) %all-to-all-start.3) | async-done | bytes 3670048 | tf_op jit(solution)/shard_map/all_to_all | solution.py:46
  347.3 5.2 %add_convert_fusion = bf16[4,1,32,2,3584]{4,3,2,0,1:T(2,128)(2,1)} fusion(bf16[4,2,32,2,3584]{4,3,2,1,0:T(2,128)(2,1)} %bitcast.6), kind=kLoop, calls=%fused_computation.10 | loop fusion | flops 3670016 | bytes 5505024 | tf_op jit(solution)/shard_map/convert_element_type | solution.py:48
  352.5 4.1 %convert_element_type.55 = bf16[256,3584]{1,0:T(8,128)(2,1)S(1)} reshape(bf16[4,1,32,2,3584]{4,3,2,0,1:T(2,128)(2,1)} %add_convert_fusion) | data formatting | bytes 3670016 | tf_op jit(solution)/shard_map/convert_element_type | solution.py:48
  356.6 1.3 gather_fusion.1
  357.9 1.6 fusion.5
  (18 shorter events, 1.6 us)
Async XLA Ops:
  0.0 3.3 copy-start
  298.6 6.0 %copy-start.1 = (f32[20,8]{0,1:T(8,128)S(1)}, f32[20,8]{0,1:T(8,128)}, u32[]{:S(2)}) copy-start(f32[20,8]{0,1:T(8,128)} %param.8) | copy-start | bytes 1924
  298.6 48.7 %all-to-all-start.3 = ((bf16[8,32,2,3584]{3,2,1,0:T(2,128)(2,1)}), bf16[8,32,2,3584]{3,2,1,0:T(2,128)(2,1)}, u32[]{:S(2)}, u32[]{:S(2)}) async-start(bf16[8,32,2,3584]{3,2,1,0:T(2,128)(2,1)} %copy.35), calls=%async_computation.3 | async-start | bytes 7340032 | tf_op jit(solution)/shard_map/all_to_all | solution.py:46
where the time goes:
time: 362 us; the launch traced here: 359 us
  blocking collectives  233 us (64%)
  local copies, waits for them, and re-layouts  51.4 us (14%)
  waiting for transfers between devices  42.6 us (12%)
  matrix products  15.6 us (4%)
  other arithmetic  10.8 us (3%)
  starting transfers between devices  5.97 us (2%)
    all_to_all x1, blocking collectives, on_device(): lax.all_to_all(received, 'expert', split_axis=1, concat_axis=1, tiled=True)  95.1 us
    all_to_all x1, blocking collectives, on_device(): lax.all_to_all(partial_value, 'expert', split_axis=1, concat_axis=1, tile...  88.9 us
    all_to_all x1, blocking collectives, on_device(): lax.all_to_all(doubled, 'group', split_axis=0, concat_axis=0, tiled=True)  48.9 us
    all_to_all x1, waiting for transfers between devices, on_device(): lax.all_to_all(returned, 'group', split_axis=0, concat_axis=0, tiled=True)  42.6 us
    reshape x2, local copies, waits for them, and re-layouts, on_device(): partial_value.reshape(item_count, members, capacity, features)  14 us
    dot_general x1, matrix products, on_device(): jnp.dot(hidden, down_rows, preferred_element_type=jnp.float32)  10.1 us
    reshape x1, local copies, waits for them, and re-layouts, on_device(): row_block = arrived_rows.reshape(-1, features)  8.4 us
  transfers between devices with their start and end apart: 1, of which 1 were waited for; matrix products, arithmetic and copies ran while one was open for 0% of the time, Pallas kernels for 0%

commit v1 on v0

v1 whole, which is shorter than its diff:
```python
import functools

import jax
import jax.numpy as jnp
from jax import lax
from jax.experimental import pallas as pl
from jax.experimental.pallas import tpu as pltpu
from jax.sharding import Mesh, PartitionSpec as P

F32, BF16 = jnp.float32, jnp.bfloat16
SLOTS = 2
AXES = ("y", "core", "x", "z")


def slot_parts(ids, experts):
    tokens, top = ids.shape
    lane = lax.broadcasted_iota(jnp.int32, (tokens, experts * SLOTS), 1)
    named = [ids[:, k : k + 1] == lane // SLOTS for k in range(top)]
    hits = functools.reduce(jnp.logical_or, named)
    before = lax.broadcasted_iota(jnp.int32, (tokens, tokens), 1) < lax.broadcasted_iota(jnp.int32, (tokens, tokens), 0)
    rank = jnp.dot(before.astype(F32), hits.astype(F32), preferred_element_type=F32)
    here = rank == (lane % SLOTS).astype(F32)
    return named, hits & here, here


def pick_kernel(ids_ref, tokens_ref, out_ref):
    experts = out_ref.shape[0]
    unused, chosen, also_unused = slot_parts(ids_ref[...], experts)
    rows = lax.dot_general(
        chosen.astype(F32).astype(BF16), tokens_ref[...], (((0,), (0,)), ((), ())), preferred_element_type=F32
    )
    out_ref[...] = rows.astype(BF16).reshape(out_ref.shape)


def mix_kernel(ids_ref, weights_ref, rows_ref, out_ref):
    tokens = ids_ref.shape[0]
    experts, slots, features = rows_ref.shape
    named, unused, here = slot_parts(ids_ref[...], experts)
    weights = weights_ref[...]
    table = jnp.zeros(here.shape, F32)
    for k, hit in enumerate(named):
        table = table + jnp.where(hit & here, weights[:, k : k + 1], 0.0)
    high = table.astype(BF16)
    rest = table - high.astype(F32)
    mid = rest.astype(BF16)
    low = (rest - mid.astype(F32)).astype(BF16)
    rows = rows_ref[...].reshape(experts * slots, features)
    total = jnp.dot(high, rows, preferred_element_type=F32)
    total += jnp.dot(mid, rows, preferred_element_type=F32)
    total += jnp.dot(low, rows, preferred_element_type=F32)
    out_ref[...] = total.astype(BF16)


def expert_kernel(steps, mine_ref, peer_ref, gate_ref, up_ref, down_ref, mine_out, peer_out, gate_acc, up_acc, hidden):
    step = pl.program_id(0)
    half = gate_acc.shape[0] // 2

    @pl.when(step == 0)
    def _():
        gate_acc[...] = jnp.zeros_like(gate_acc)
        up_acc[...] = jnp.zeros_like(up_acc)

    @pl.when(step < steps)
    def _():
        for at, ref in ((0, mine_ref), (half, peer_ref)):
            rows = ref[...].reshape(half, ref.shape[2])
            gate_acc[at : at + half] += jnp.dot(rows, gate_ref[...], preferred_element_type=F32)
            up_acc[at : at + half] += jnp.dot(rows, up_ref[...], preferred_element_type=F32)

    @pl.when(step == steps)
    def _():
        gate = gate_acc[...]
        hidden[...] = (gate / (1.0 + jnp.exp(-gate)) * up_acc[...]).astype(BF16)

    @pl.when(step >= steps)
    def _():
        for at, ref in ((0, mine_out), (half, peer_out)):
            part = jnp.dot(hidden[at : at + half], down_ref[...], preferred_element_type=F32)
            ref[...] = part.astype(BF16).reshape(ref.shape)


def run_expert(mine, peer, gate, up, down):
    experts, slots, features = mine.shape
    units = gate.shape[1]
    steps = 4
    wide = features // steps
    first = lambda i: jnp.minimum(i, steps - 1)
    second = lambda i: jnp.maximum(i - steps, 0)
    rows_spec = pl.BlockSpec((experts, slots, wide), lambda i: (0, 0, first(i)))
    out_spec = pl.BlockSpec((experts, slots, wide), lambda i: (0, 0, second(i)))
    rows = experts * slots * 2
    return pl.pallas_call(
        functools.partial(expert_kernel, steps),
        grid=(2 * steps,),
        in_specs=[
            rows_spec,
            rows_spec,
            pl.BlockSpec((wide, units), lambda i: (first(i), 0)),
            pl.BlockSpec((wide, units), lambda i: (first(i), 0)),
            pl.BlockSpec((units, wide), lambda i: (0, second(i))),
        ],
        out_specs=[out_spec, out_spec],
        out_shape=[jax.ShapeDtypeStruct(mine.shape, BF16)] * 2,
        scratch_shapes=[
            pltpu.VMEM((rows, units), F32),
            pltpu.VMEM((rows, units), F32),
            pltpu.VMEM((rows, units), BF16),
        ],
        compiler_params=pltpu.CompilerParams(vmem_limit_bytes=40 << 20),
        cost_estimate=pl.CostEstimate(flops=6 * rows * features * units, bytes_accessed=20 << 20, transcendentals=rows * units),
    )(mine, peer, gate, up, down)


def on_device(tokens, expert_ids, route_weights, w_gate, w_up, w_down):
    features = tokens.shape[1]
    experts = lax.axis_size("y") * lax.axis_size("x") * lax.axis_size("z")
    swap = [(0, 1), (1, 0)]
    outgoing = pl.pallas_call(
        pick_kernel, out_shape=jax.ShapeDtypeStruct((experts, SLOTS, features), BF16),
        compiler_params=pltpu.CompilerParams(vmem_limit_bytes=40 << 20),
    )(expert_ids, tokens)
    mine = lax.all_to_all(outgoing, ("y", "x", "z"), 0, 0, tiled=True)
    peer = lax.ppermute(mine, "core", swap)
    mine_part, peer_part = run_expert(mine, peer, w_gate[0, 0], w_up[0, 0], w_down[0, 0])
    other_part = lax.ppermute(peer_part, "core", swap)
    total = (mine_part.astype(F32) + other_part.astype(F32)).astype(BF16)
    returned = lax.all_to_all(total, ("y", "x", "z"), 0, 0, tiled=True)
    return pl.pallas_call(
        mix_kernel, out_shape=jax.ShapeDtypeStruct(tokens.shape, BF16),
        compiler_params=pltpu.CompilerParams(vmem_limit_bytes=40 << 20),
    )(expert_ids, route_weights, returned)


def solution(mesh):
    groups, members = mesh.devices.shape
    fine = Mesh(mesh.devices.reshape(groups // 2, 2, 4, members // 4), AXES)
    rows = P(AXES, None)
    weights = P(("y", "core"), ("x", "z"), None, None)
    return jax.shard_map(
        on_device, mesh=fine, in_specs=(rows, rows, rows, weights, weights, weights), out_specs=rows, check_vma=False
    )
```

time: 362 us -> 147 us (0.41)
  blocking collectives: 233 us -> 61.7 us
  local copies, waits for them, and re-layouts: 51.4 us -> 1.78 us
  matrix products: 15.6 us -> 0 us
  Pallas kernels: 0 us -> 14.1 us
  waiting for transfers between devices: 42.6 us -> 54.2 us
  other arithmetic: 10.8 us -> 3.13 us
    all_to_all x3 -> x1, blocking collectives: 233 us -> 61.7 us  [on_device(): mine = lax.all_to_all(outgoing, ('y', 'x', 'z'), 0, 0, tiled=True)]
    reshape x3 -> x0, local copies, waits for them, and re-layouts: 22.4 us -> none  [the longest x2 14 us: on_device(): partial_value.reshape(item_count, members, capacity, features)]
    dot_general x3 -> x0, matrix products: 15.6 us -> none  [the longest x1 10.1 us: on_device(): jnp.dot(hidden, down_rows, preferred_element_type=jnp.float32)]
    pallas_call x0 -> x3, Pallas kernels: none -> 14.1 us  [the longest x1 11.3 us: run_expert(): pl.pallas_call(functools.partial(expert_kernel, steps), grid=(2 * steps,)...]
    all_to_all x3 -> x0, local copies, waits for them, and re-layouts: 13.1 us -> none  [the longest x1 4.66 us: on_device(): lax.all_to_all(partial_value, 'expert', split_axis=1, concat_axis=1, tile...]
    ppermute x0 -> x2, waiting for transfers between devices: none -> 7.43 us  [the longest x1 3.78 us: on_device(): peer = lax.ppermute(mine, 'core', swap)]
    gather x3 -> x0, local copies, waits for them, and re-layouts: 4.68 us -> none  [the longest x2 3.41 us: on_device(): tokens[source_row]]
    all_to_all x1, waiting for transfers between devices: 42.6 us -> 46.8 us  [on_device(): returned = lax.all_to_all(total, ('y', 'x', 'z'), 0, 0, tiled=True)]
  transfers between devices with their start and end apart: 1 -> 3, of which waited for: 1 -> 3; matrix products, arithmetic and copies ran while one was open for 0% -> 0% of each run, Pallas kernels for 0% -> 0%
where the time goes in v1:
time: 147 us; the launch traced here: 144 us
  blocking collectives  61.7 us (42%)
  waiting for transfers between devices  54.2 us (37%)
  Pallas kernels  14.1 us (10%)
  starting transfers between devices  9.1 us (6%)
  other arithmetic  3.13 us (2%)
  local copies, waits for them, and re-layouts  1.78 us (1%)
    all_to_all x1, blocking collectives, on_device(): mine = lax.all_to_all(outgoing, ('y', 'x', 'z'), 0, 0, tiled=True)  61.7 us
    all_to_all x1, waiting for transfers between devices, on_device(): returned = lax.all_to_all(total, ('y', 'x', 'z'), 0, 0, tiled=True)  46.8 us
    pallas_call x1, Pallas kernels, run_expert(): pl.pallas_call(functools.partial(expert_kernel, steps), grid=(2 * steps,)...  11.3 us
    all_to_all x1, starting transfers between devices, on_device(): returned = lax.all_to_all(total, ('y', 'x', 'z'), 0, 0, tiled=True)  8.87 us
    ppermute x1, waiting for transfers between devices, on_device(): peer = lax.ppermute(mine, 'core', swap)  3.78 us
    ppermute x1, waiting for transfers between devices, on_device(): other_part = lax.ppermute(peer_part, 'core', swap)  3.64 us
    convert_element_type x1, other arithmetic, on_device(): total = (mine_part.astype(F32) + other_part.astype(F32)).astype(BF16)  3.13 us
  transfers between devices with their start and end apart: 3, of which 3 were waited for; matrix products, arithmetic and copies ran while one was open for 0% of the time, Pallas kernels for 0%

profile of v1, /device:TPU:8, one launch (start us, length us, event | category | flops | bytes accessed | tf_op | source)
XLA Modules:
  0.0 144.1 jit_solution(16828706306093944620)
XLA Ops:
  0.0 0.8 copy.8.ids_ref
  0.8 0.0 copy-start
  0.8 0.9 copy-done
  1.7 0.9 shard_map.64
  2.6 0.0 copy-start.1
  2.6 61.7 %all_to_all.10.mine_ref = bf16[128,2,3584]{2,1,0:T(2,128)(2,1)S(1)} all-to-all(bf16[128,2,3584]{2,1,0:T(2,128)(2,1)S(1)} %shard_map.64), channel_id=1, replica_groups=mesh['y'=4,'core'=2,'x'=4,'z'=8] {'y','x','z'}, dimensions={0} | all-to-all | bytes 3670016 | tf_op jit(solution)/shard_map/all_to_all | solution.py:122
  64.3 0.0 collective-permute-start
  64.3 3.8 %collective-permute-done.peer_ref = bf16[128,2,3584]{2,1,0:T(2,128)(2,1)S(1)} collective-permute-done((bf16[128,2,3584]{2,1,0:T(2,128)(2,1)S(1)}, bf16[128,2,3584]{2,1,0:T(2,128)(2,1)S(1)}, u32[]{:S(2)}, u32[]{:S(2)}) %collective-permute-start) | collective-permute-done | bytes 1835040 | tf_op jit(solution)/shard_map/ppermute | solution.py:123
  68.1 0.0 copy-done.1
  68.1 11.3 %shard_map.65 = (bf16[128,2,3584]{2,1,0:T(2,128)(2,1)S(1)}, bf16[128,2,3584]{2,1,0:T(2,128)(2,1)S(1)}) custom-call(bf16[128,2,3584]{2,1,0:T(2,128)(2,1)S(1)} %all_to_all.10.mine_ref, bf16[128,2,3584]{2,1,0:T(2,128)(2,1)S(1)} %collective-permute-done.peer_ref, bf16[3584,512]{1,0:T(8,128)(2,1)S(1)} %bitcast.3, bf16[3584,512]{1,0:T(8,128)(2,1)} %bitcast.4, ...), custom_call_target="tpu_custom_call" | custom-call | flops 5637144576 | bytes 20971520 | tf_op jit(solution)/shard_map/pallas_call | solution.py:92
  79.4 0.2 collective-permute-start.1
  79.6 3.6 %collective-permute-done.1 = bf16[128,2,3584]{2,1,0:T(2,128)(2,1)S(1)} collective-permute-done((bf16[128,2,3584]{2,1,0:T(2,128)(2,1)S(1)}, bf16[128,2,3584]{2,1,0:T(2,128)(2,1)S(1)}, u32[]{:S(2)}, u32[]{:S(2)}) %collective-permute-start.1) | collective-permute-done | bytes 1835040 | tf_op jit(solution)/shard_map/ppermute | solution.py:125
  83.3 3.1 %add_convert_fusion = bf16[128,2,3584]{2,1,0:T(2,128)(2,1)} fusion(bf16[128,2,3584]{2,1,0:T(2,128)(2,1)S(1)} %collective-permute-done.1, bf16[128,2,3584]{2,1,0:T(2,128)(2,1)S(1)} %get-tuple-element.7), kind=kLoop, calls=%fused_computation | loop fusion | flops 3670016 | bytes 5505024 | tf_op jit(solution)/shard_map/convert_element_type | solution.py:126
  86.4 0.0 copy-start.2
  86.4 8.9 %all-to-all-start.1 = ((bf16[128,2,3584]{2,1,0:T(2,128)(2,1)}), bf16[128,2,3584]{2,1,0:T(2,128)(2,1)S(1)}, u32[]{:S(2)}, u32[]{:S(2)}) async-start(bf16[128,2,3584]{2,1,0:T(2,128)(2,1)} %add_convert_fusion), calls=%async_computation.1 | async-start | bytes 3670016 | tf_op jit(solution)/shard_map/all_to_all | solution.py:127
  95.3 0.0 copy-done.2
  95.3 0.1 copy.9.weights_ref
  95.4 46.8 %all-to-all-done.1.rows_ref = bf16[128,2,3584]{2,1,0:T(2,128)(2,1)S(1)} async-done(((bf16[128,2,3584]{2,1,0:T(2,128)(2,1)}), bf16[128,2,3584]{2,1,0:T(2,128)(2,1)S(1)}, u32[]{:S(2)}, u32[]{:S(2)}) %all-to-all-start.1) | async-done | bytes 1835040 | tf_op jit(solution)/shard_map/all_to_all | solution.py:127
  142.2 1.9 %shard_map.66 = bf16[20,3584]{1,0:T(8,128)(2,1)} custom-call(s32[20,8]{1,0:T(8,128)S(1)} %copy.8.ids_ref, f32[20,8]{1,0:T(8,128)S(1)} %copy.9.weights_ref, bf16[128,2,3584]{2,1,0:T(2,128)(2,1)S(1)} %all-to-all-done.1.rows_ref), custom_call_target="tpu_custom_call" | custom-call | tf_op jit(solution)/shard_map/pallas_call | solution.py:128
Async XLA Ops:
  0.8 0.9 copy-start
  2.6 65.5 %copy-start.1 = (bf16[1,1,3584,512]{3,2,1,0:T(8,128)(2,1)S(1)}, bf16[1,1,3584,512]{3,2,1,0:T(8,128)(2,1)}, u32[]{:S(2)}) copy-start(bf16[1,1,3584,512]{3,2,1,0:T(8,128)(2,1)} %param.9) | copy-start | bytes 11010052
  64.3 3.8 %collective-permute-start = (bf16[128,2,3584]{2,1,0:T(2,128)(2,1)S(1)}, bf16[128,2,3584]{2,1,0:T(2,128)(2,1)S(1)}, u32[]{:S(2)}, u32[]{:S(2)}) collective-permute-start(bf16[128,2,3584]{2,1,0:T(2,128)(2,1)S(1)} %all_to_all.10.mine_ref), channel_id=1, source_target_pairs={{0,32},{32,0},{1,33},{33,1},{2,34},{34,2},{3,35},{35,3},{4,36},{36... | collective-permute-start | bytes 5505032 | tf_op jit(solution)/shard_map/ppermute | solution.py:123
  79.4 3.9 %collective-permute-start.1 = (bf16[128,2,3584]{2,1,0:T(2,128)(2,1)S(1)}, bf16[128,2,3584]{2,1,0:T(2,128)(2,1)S(1)}, u32[]{:S(2)}, u32[]{:S(2)}) collective-permute-start(bf16[128,2,3584]{2,1,0:T(2,128)(2,1)S(1)} %get-tuple-element.8), channel_id=1, source_target_pairs={{0,32},{32,0},{1,33},{33,1},{2,34},{34,2},{3,35},{35,3},{4,36},{36... | collective-permute-start | bytes 5505032 | tf_op jit(solution)/shard_map/ppermute | solution.py:125
  86.4 8.9 %copy-start.2 = (f32[20,8]{0,1:T(8,128)S(1)}, f32[20,8]{0,1:T(8,128)}, u32[]{:S(2)}) copy-start(f32[20,8]{0,1:T(8,128)} %param.8) | copy-start | bytes 1924
  86.4 55.7 %all-to-all-start.1 = ((bf16[128,2,3584]{2,1,0:T(2,128)(2,1)}), bf16[128,2,3584]{2,1,0:T(2,128)(2,1)S(1)}, u32[]{:S(2)}, u32[]{:S(2)}) async-start(bf16[128,2,3584]{2,1,0:T(2,128)(2,1)} %add_convert_fusion), calls=%async_computation.1 | async-start | bytes 3670016 | tf_op jit(solution)/shard_map/all_to_all | solution.py:127

commit v2 on v0

v2 whole, which is shorter than its diff:
```python
import functools

import jax
import jax.numpy as jnp
from jax import lax
from jax.experimental import pallas as pl
from jax.experimental.pallas import tpu as pltpu
from jax.sharding import Mesh, PartitionSpec as P

F32, BF16 = jnp.float32, jnp.bfloat16
SLOTS = 2
AXES = ("y", "core", "x", "z")
PLANE = ("x", "y")
EXTRA = 128


def params(mib):
    return pltpu.CompilerParams(vmem_limit_bytes=mib << 20)


def pack_kernel(tokens_ref, ids_ref, weights_ref, out_ref):
    features = tokens_ref.shape[1]
    top = ids_ref.shape[1]
    weights = weights_ref[...]
    high = weights.astype(BF16)
    rest = weights - high.astype(F32)
    mid = rest.astype(BF16)
    low = (rest - mid.astype(F32)).astype(BF16)
    column = lax.broadcasted_iota(jnp.int32, (top, EXTRA), 1)
    row = lax.broadcasted_iota(jnp.int32, (top, EXTRA), 0)
    extra = jnp.zeros((tokens_ref.shape[0], EXTRA), F32)
    for place, piece in enumerate((ids_ref[...].astype(F32).astype(BF16), high, mid, low)):
        spread = (column == row + place * top).astype(F32).astype(BF16)
        extra += jnp.dot(piece, spread, preferred_element_type=F32)
    out_ref[:, :features] = tokens_ref[...]
    out_ref[:, features:] = extra.astype(BF16)


def slot_parts(extra, z, top, chips):
    tokens = extra.shape[0]
    lane = lax.broadcasted_iota(jnp.int32, (tokens, chips * SLOTS), 1)
    chip = lane // SLOTS
    expert = ((chip % 4) * 32 + (chip // 4) * 8 + z).astype(F32)
    named = [extra[:, k : k + 1] == expert for k in range(top)]
    hits = functools.reduce(jnp.logical_or, named)
    before = lax.broadcasted_iota(jnp.int32, (tokens, tokens), 1) < lax.broadcasted_iota(jnp.int32, (tokens, tokens), 0)
    rank = jnp.dot(before.astype(F32), hits.astype(F32), preferred_element_type=F32)
    here = rank == (lane % SLOTS).astype(F32)
    return named, hits, here


def pick_kernel(top, count, z_ref, *refs):
    blocks, out_ref = refs[:count], refs[-1]
    chips, unused, slots, features = out_ref.shape
    for b, block in enumerate(blocks):
        unused, hits, here = slot_parts(block[:, features:].astype(F32), z_ref[0], top, chips)
        chosen = (hits & here).astype(F32).astype(BF16)
        rows = lax.dot_general(chosen, block[:, :features], (((0,), (0,)), ((), ())), preferred_element_type=F32)
        out_ref[:, b] = rows.astype(BF16).reshape(chips, slots, features)


def pick(z, blocks, chips, top, after=()):
    features = blocks[0].shape[1] - EXTRA
    vmem = pl.BlockSpec(memory_space=pltpu.VMEM)
    return pl.pallas_call(
        functools.partial(pick_kernel, top, len(blocks)),
        in_specs=[pl.BlockSpec(memory_space=pltpu.SMEM)] + [vmem] * len(blocks) + [pl.BlockSpec(memory_space=pl.ANY)] * len(after),
        out_shape=jax.ShapeDtypeStruct((chips, len(blocks), SLOTS, features), BF16),
        compiler_params=params(16),
    )(z, *blocks, *after)


def block_mix(z, block, rows, top):
    chips, slots, features = rows.shape
    extra = block[:, features:].astype(F32)
    named, unused, here = slot_parts(extra, z, top, chips)
    rows = rows.reshape(chips * slots, features)
    total = jnp.zeros((extra.shape[0], features), F32)
    for part in (1, 2, 3):
        table = jnp.zeros(here.shape, F32)
        for k, hit in enumerate(named):
            at = part * top + k
            table = table + jnp.where(hit & here, extra[:, at : at + 1], 0.0)
        total += jnp.dot(table.astype(BF16), rows, preferred_element_type=F32)
    return total


def far_mix_kernel(top, z_ref, *refs):
    count = (len(refs) - 1) // 2
    blocks, rows_ref, outs = refs[:count], refs[count], refs[count + 1 :]
    for b in range(count):
        outs[b][...] = block_mix(z_ref[0], blocks[b], rows_ref[:, b], top).astype(BF16)


def far_mix(z, blocks, rows, top):
    vmem = pl.BlockSpec(memory_space=pltpu.VMEM)
    out = jax.ShapeDtypeStruct((blocks[0].shape[0], rows.shape[-1]), BF16)
    return pl.pallas_call(
        functools.partial(far_mix_kernel, top),
        in_specs=[pl.BlockSpec(memory_space=pltpu.SMEM)] + [vmem] * (len(blocks) + 1),
        out_shape=[out] * len(blocks),
        compiler_params=params(16),
    )(z, *blocks, rows)


def near_mix_kernel(top, z_ref, own, left1, right1, left2, right2, rows_ref, add_left, add_right, add_far, out0, out1, out2, out3, out4):
    z = z_ref[0]
    out3[...] = (block_mix(z, left2, rows_ref[:, 3], top) + add_left[...].astype(F32) + add_far[...].astype(F32)).astype(BF16)
    out4[...] = (block_mix(z, right2, rows_ref[:, 4], top) + add_right[...].astype(F32)).astype(BF16)
    out1[...] = block_mix(z, left1, rows_ref[:, 1], top).astype(BF16)
    out2[...] = block_mix(z, right1, rows_ref[:, 2], top).astype(BF16)
    out0[...] = block_mix(z, own, rows_ref[:, 0], top)


def near_mix(z, blocks, rows, adds, top):
    vmem = pl.BlockSpec(memory_space=pltpu.VMEM)
    shape = (blocks[0].shape[0], rows.shape[-1])
    return pl.pallas_call(
        functools.partial(near_mix_kernel, top),
        in_specs=[pl.BlockSpec(memory_space=pltpu.SMEM)] + [vmem] * (len(blocks) + 4),
        out_shape=[jax.ShapeDtypeStruct(shape, F32)] + [jax.ShapeDtypeStruct(shape, BF16)] * 4,
        compiler_params=params(16),
    )(z, *blocks, rows, *adds)


def join_kernel(mine_ref, other_ref, *refs):
    refs[-1][...] = (mine_ref[...].astype(F32) + other_ref[...].astype(F32)).astype(BF16)


def join(mine, other, after=()):
    vmem = pl.BlockSpec(memory_space=pltpu.VMEM)
    return pl.pallas_call(
        join_kernel,
        in_specs=[vmem] * 2 + [pl.BlockSpec(memory_space=pl.ANY)] * len(after),
        out_shape=jax.ShapeDtypeStruct(mine.shape, BF16),
        compiler_params=params(16),
    )(mine, other, *after)


def sum_kernel(own, *refs):
    total = own[...]
    for ref in refs[:-1]:
        total = total + ref[...].astype(F32)
    refs[-1][...] = total.astype(BF16)


def expert_kernel(mine_ref, peer_ref, gate_ref, up_ref, down_ref, mine_out, peer_out, rows, hidden):
    half = rows.shape[0] // 2
    features = rows.shape[1]
    units = hidden.shape[1]
    rows[:half] = mine_ref[...].reshape(half, features)
    rows[half:] = peer_ref[...].reshape(half, features)
    wide = 256

    def first(n, carry):
        cols = pl.ds(pl.multiple_of(n * wide, wide), wide)
        gate = jnp.dot(rows[...], gate_ref[:, cols], preferred_element_type=F32)
        up = jnp.dot(rows[...], up_ref[:, cols], preferred_element_type=F32)
        hidden[:, cols] = (gate / (1.0 + jnp.exp(-gate)) * up).astype(BF16)
        return carry

    lax.fori_loop(0, units // wide, first, 0)

    def second(n, carry):
        cols = pl.ds(pl.multiple_of(n * 512, 512), 512)
        part = jnp.dot(hidden[...], down_ref[:, cols], preferred_element_type=F32).astype(BF16)
        lead = mine_out.shape[:-1]
        mine_out[:, :, :, cols] = part[:half].reshape(*lead, 512)
        peer_out[:, :, :, cols] = part[half:].reshape(*lead, 512)
        return carry

    lax.fori_loop(0, features // 512, second, 0)


def run_expert(mine, peer, gate, up, down):
    features, units = gate.shape
    rows = 2 * mine.size // features
    vmem = pl.BlockSpec(memory_space=pltpu.VMEM)
    return pl.pallas_call(
        expert_kernel,
        in_specs=[vmem] * 5,
        out_shape=[jax.ShapeDtypeStruct(mine.shape, BF16)] * 2,
        scratch_shapes=[pltpu.VMEM((rows, features), BF16), pltpu.VMEM((rows, units), BF16)],
        compiler_params=params(30),
        cost_estimate=pl.CostEstimate(flops=6 * rows * features * units, bytes_accessed=16 << 20, transcendentals=rows * units),
    )(mine, peer, gate, up, down)


def on_device(tokens, expert_ids, route_weights, w_gate, w_up, w_down):
    top = expert_ids.shape[1]
    chips = lax.axis_size("x") * lax.axis_size("y")
    ring = lax.axis_size("z")
    z = lax.axis_index("z").astype(jnp.int32).reshape(1)
    gate, up, down = w_gate[0, 0], w_up[0, 0], w_down[0, 0]

    def along(value, by):
        return lax.ppermute(value, "z", [(i, (i + by) % ring) for i in range(ring)])

    def swap(value):
        return lax.ppermute(value, "core", [(0, 1), (1, 0)])

    def plane(value):
        return lax.all_to_all(value, PLANE, 0, 0, tiled=True)

    own = pl.pallas_call(
        pack_kernel,
        out_shape=jax.ShapeDtypeStruct((tokens.shape[0], tokens.shape[1] + EXTRA), BF16),
    )(tokens, expert_ids, route_weights)
    left1, right1, left2, right2 = along(own, 1), along(own, -1), along(own, 2), along(own, -2)
    left3, right3, opposite = along(left2, 1), along(right2, -1), along(left2, 2)
    near, far = [own, left1, right1, left2, right2], [left3, right3, opposite]

    near_mine = plane(pick(z, near, chips, top))
    far_mine = plane(pick(z, far, chips, top, [near_mine]))
    near_parts = run_expert(near_mine, swap(near_mine), gate, up, down)
    far_parts = run_expert(far_mine, swap(far_mine), gate, up, down)

    far_rows = plane(join(far_parts[0], swap(far_parts[1])))
    far_left, far_right, far_opposite = far_mix(z, far, far_rows, top)
    adds = [along(far_left, -1), along(far_right, 1), along(far_opposite, -2)]
    near_rows = plane(join(near_parts[0], swap(near_parts[1]), [far_left]))
    mix0, mix1, mix2, mix3, mix4 = near_mix(z, near, near_rows, adds, top)
    arrived = [along(mix1, -1), along(mix2, 1), along(mix3, -2), along(mix4, 2)]
    return pl.pallas_call(sum_kernel, out_shape=jax.ShapeDtypeStruct(tokens.shape, BF16))(mix0, *arrived)


def solution(mesh):
    groups, members = mesh.devices.shape
    fine = Mesh(mesh.devices.reshape(groups // 2, 2, 4, members // 4), AXES)
    rows = P(AXES, None)
    weights = P(("y", "core"), ("x", "z"), None, None)
    return jax.shard_map(
        on_device, mesh=fine, in_specs=(rows, rows, rows, weights, weights, weights), out_specs=rows, check_vma=False
    )
```

time: 362 us -> 151 us (0.42)
  blocking collectives: 233 us -> 16.7 us
  local copies, waits for them, and re-layouts: 51.4 us -> 11.4 us
  starting transfers between devices: 5.97 us -> 42.2 us
  Pallas kernels: 0 us -> 23.2 us
  matrix products: 15.6 us -> 0 us
  waiting for transfers between devices: 42.6 us -> 54.1 us
  other arithmetic: 10.8 us -> 0 us
    all_to_all x3 -> x1, blocking collectives: 233 us -> 16.7 us  [plane(): return lax.all_to_all(value, PLANE, 0, 0, tiled=True)]
    ppermute x0 -> x18, waiting for transfers between devices: none -> 37.7 us  [the longest x14 35.6 us: along(): return lax.ppermute(value, 'z', [(i, (i + by) % ring) for i in range(ring)])]
    all_to_all x1 -> x3, waiting for transfers between devices: 42.6 us -> 16.4 us  [plane(): return lax.all_to_all(value, PLANE, 0, 0, tiled=True)]
    ppermute x0 -> x18, starting transfers between devices: none -> 24.8 us  [the longest x14 23.9 us: along(): return lax.ppermute(value, 'z', [(i, (i + by) % ring) for i in range(ring)])]
    pallas_call x0 -> x10, Pallas kernels: none -> 23.2 us  [the longest x2 9.25 us: run_expert(): pl.pallas_call(expert_kernel, in_specs=[vmem] * 5, out_shape=[jax.ShapeDt...]
    reshape x3 -> x0, local copies, waits for them, and re-layouts: 22.4 us -> none  [the longest x2 14 us: on_device(): partial_value.reshape(item_count, members, capacity, features)]
    dot_general x3 -> x0, matrix products: 15.6 us -> none  [the longest x1 10.1 us: on_device(): jnp.dot(hidden, down_rows, preferred_element_type=jnp.float32)]
    all_to_all x3 -> x0, local copies, waits for them, and re-layouts: 13.1 us -> none  [the longest x1 4.66 us: on_device(): lax.all_to_all(partial_value, 'expert', split_axis=1, concat_axis=1, tile...]
  transfers between devices with their start and end apart: 1 -> 21, of which waited for: 1 -> 15; matrix products, arithmetic and copies ran while one was open for 0% -> 0% of each run, Pallas kernels for 0% -> 8%
where the time goes in v2:
time: 151 us; the launch traced here: 148 us
  waiting for transfers between devices  54.1 us (36%)
  starting transfers between devices  42.2 us (28%)
  Pallas kernels  23.2 us (15%)
  blocking collectives  16.7 us (11%)
  local copies, waits for them, and re-layouts  11.4 us (8%)
    ppermute x14, waiting for transfers between devices, along(): return lax.ppermute(value, 'z', [(i, (i + by) % ring) for i in range(ring)])  35.6 us
    ppermute x14, starting transfers between devices, along(): return lax.ppermute(value, 'z', [(i, (i + by) % ring) for i in range(ring)])  23.9 us
    all_to_all x3, starting transfers between devices, plane(): return lax.all_to_all(value, PLANE, 0, 0, tiled=True)  17.4 us
    all_to_all x1, blocking collectives, plane(): return lax.all_to_all(value, PLANE, 0, 0, tiled=True)  16.7 us
    all_to_all x3, waiting for transfers between devices, plane(): return lax.all_to_all(value, PLANE, 0, 0, tiled=True)  16.4 us
    unnamed x40, local copies, waits for them, and re-layouts  11.4 us
    pallas_call x2, Pallas kernels, run_expert(): pl.pallas_call(expert_kernel, in_specs=[vmem] * 5, out_shape=[jax.ShapeDt...  9.25 us
    pallas_call x2, Pallas kernels, pick(): pl.pallas_call(functools.partial(pick_kernel, top, len(blocks)), in_specs...  4.35 us
  transfers between devices with their start and end apart: 21, of which 15 were waited for; matrix products, arithmetic and copies ran while one was open for 0% of the time, Pallas kernels for 8%

profile of v2, /device:TPU:8, one launch (start us, length us, event | category | flops | bytes accessed | tf_op | source)
XLA Modules:
  0.0 147.8 jit_solution(8697936610396980089)
XLA Ops:
  4.5 3.3 %collective-permute-start.2 = (bf16[20,3712]{1,0:T(8,128)(2,1)}, bf16[20,3712]{1,0:T(8,128)(2,1)S(1)}, u32[]{:S(2)}, u32[]{:S(2)}) collective-permute-start(bf16[20,3712]{1,0:T(8,128)(2,1)} %shard_map.64.refs_0_.own), channel_id=1, source_target_pairs={{0,2},{1,3},{2,4},{3,5},{4,6},{5,7},{6,0},{7,1},{8,10},{9,11},{10,... | collective-permute-start | bytes 445448 | tf_op jit(solution)/shard_map/ppermute | solution.py:197
  7.7 3.0 %collective-permute-start.3 = (bf16[20,3712]{1,0:T(8,128)(2,1)}, bf16[20,3712]{1,0:T(8,128)(2,1)S(1)}, u32[]{:S(2)}, u32[]{:S(2)}) collective-permute-start(bf16[20,3712]{1,0:T(8,128)(2,1)} %shard_map.64.refs_0_.own), channel_id=1, source_target_pairs={{0,6},{1,7},{2,0},{3,1},{4,2},{5,3},{6,4},{7,5},{8,14},{9,15},{10,... | collective-permute-start | bytes 445448 | tf_op jit(solution)/shard_map/ppermute | solution.py:197
  11.8 2.2 %collective-permute-start.1 = (bf16[20,3712]{1,0:T(8,128)(2,1)}, bf16[20,3712]{1,0:T(8,128)(2,1)S(1)}, u32[]{:S(2)}, u32[]{:S(2)}) collective-permute-start(bf16[20,3712]{1,0:T(8,128)(2,1)} %shard_map.64.refs_0_.own), channel_id=1, source_target_pairs={{0,7},{1,0},{2,1},{3,2},{4,3},{5,4},{6,5},{7,6},{8,15},{9,8},{10,9... | collective-permute-start | bytes 445448 | tf_op jit(solution)/shard_map/ppermute | solution.py:197
  14.0 5.1 %collective-permute-done.2.refs_3_.left2 = bf16[20,3712]{1,0:T(8,128)(2,1)S(1)} collective-permute-done((bf16[20,3712]{1,0:T(8,128)(2,1)}, bf16[20,3712]{1,0:T(8,128)(2,1)S(1)}, u32[]{:S(2)}, u32[]{:S(2)}) %collective-permute-start.2) | collective-permute-done | bytes 148512 | tf_op jit(solution)/shard_map/ppermute | solution.py:197
  24.8 2.5 %shard_map.65 = bf16[16,5,2,3584]{3,2,1,0:T(2,128)(2,1)} custom-call(s32[1]{0:T(128)} %bitcast.z_ref, bf16[20,3712]{1,0:T(8,128)(2,1)S(1)} %copy-done.4, bf16[20,3712]{1,0:T(8,128)(2,1)S(1)} %collective-permute-done.refs_1_.left1, bf16[20,3712]{1,0:T(8,128)(2,1)S(1)} %collective-permute-done.1.refs_2_.right1, ...), custom_call_target="tpu_custom_call" | custom-call | tf_op jit(solution)/shard_map/pallas_call | solution.py:65
  27.4 7.4 %all-to-all-start = ((bf16[16,5,2,3584]{3,2,1,0:T(2,128)(2,1)}), bf16[16,5,2,3584]{3,2,1,0:T(2,128)(2,1)S(1)}, u32[]{:S(2)}, u32[]{:S(2)}) async-start(bf16[16,5,2,3584]{3,2,1,0:T(2,128)(2,1)} %shard_map.65), calls=%async_computation | async-start | bytes 2293760 | tf_op jit(solution)/shard_map/all_to_all | solution.py:203
  35.8 3.8 %collective-permute-start.8 = (bf16[20,3712]{1,0:T(8,128)(2,1)S(1)}, bf16[20,3712]{1,0:T(8,128)(2,1)S(1)}, u32[]{:S(2)}, u32[]{:S(2)}) collective-permute-start(bf16[20,3712]{1,0:T(8,128)(2,1)S(1)} %collective-permute-done.2.refs_3_.left2), channel_id=1, source_target_pairs={{0,2},{1,3},{2,4},{3,5},{4,6},{5,7},{6,0},{7,1},{8,10},{9,11},{10,... | collective-permute-start | bytes 445448 | tf_op jit(solution)/shard_map/ppermute | solution.py:197
  39.6 5.3 %collective-permute-done.6.refs_0_ = bf16[20,3712]{1,0:T(8,128)(2,1)S(1)} collective-permute-done((bf16[20,3712]{1,0:T(8,128)(2,1)S(1)}, bf16[20,3712]{1,0:T(8,128)(2,1)S(1)}, u32[]{:S(2)}, u32[]{:S(2)}) %collective-permute-start.6) | collective-permute-done | bytes 148512 | tf_op jit(solution)/shard_map/ppermute | solution.py:197
  45.0 3.5 %collective-permute-done.8.refs_2_ = bf16[20,3712]{1,0:T(8,128)(2,1)S(1)} collective-permute-done((bf16[20,3712]{1,0:T(8,128)(2,1)S(1)}, bf16[20,3712]{1,0:T(8,128)(2,1)S(1)}, u32[]{:S(2)}, u32[]{:S(2)}) %collective-permute-start.8) | collective-permute-done | bytes 148512 | tf_op jit(solution)/shard_map/ppermute | solution.py:197
  48.5 3.3 %all-to-all-done.mine_ref.refs_3_ = bf16[16,5,2,3584]{3,2,1,0:T(2,128)(2,1)S(1)} async-done(((bf16[16,5,2,3584]{3,2,1,0:T(2,128)(2,1)}), bf16[16,5,2,3584]{3,2,1,0:T(2,128)(2,1)S(1)}, u32[]{:S(2)}, u32[]{:S(2)}) %all-to-all-start) | async-done | bytes 1146912 | tf_op jit(solution)/shard_map/all_to_all | solution.py:203
  53.7 4.9 %all-to-all-start.1 = ((bf16[16,3,2,3584]{3,2,1,0:T(2,128)(2,1)}), bf16[16,3,2,3584]{3,2,1,0:T(2,128)(2,1)S(1)}, u32[]{:S(2)}, u32[]{:S(2)}) async-start(bf16[16,3,2,3584]{3,2,1,0:T(2,128)(2,1)} %shard_map.67), calls=%async_computation.1 | async-start | bytes 1376256 | tf_op jit(solution)/shard_map/all_to_all | solution.py:203
  58.5 9.8 %all-to-all-done.1.mine_ref = bf16[16,3,2,3584]{3,2,1,0:T(2,128)(2,1)S(1)} async-done(((bf16[16,3,2,3584]{3,2,1,0:T(2,128)(2,1)}), bf16[16,3,2,3584]{3,2,1,0:T(2,128)(2,1)S(1)}, u32[]{:S(2)}, u32[]{:S(2)}) %all-to-all-start.1) | async-done | bytes 688160 | tf_op jit(solution)/shard_map/all_to_all | solution.py:203
  76.6 3.9 %shard_map.68 = (bf16[16,3,2,3584]{3,2,1,0:T(2,128)(2,1)S(1)}, bf16[16,3,2,3584]{3,2,1,0:T(2,128)(2,1)S(1)}) custom-call(bf16[16,3,2,3584]{3,2,1,0:T(2,128)(2,1)S(1)} %all-to-all-done.1.mine_ref, bf16[16,3,2,3584]{3,2,1,0:T(2,128)(2,1)S(1)} %collective-permute-done.9.peer_ref, bf16[3584,512]{1,0:T(8,128)(2,1)S(1)} %bitcast.4, bf16[3584,512]{1,0:T(8,128)(2,1)S(1)} %bitcast.6, ...), custom_call_target="tpu_custom_call" | custom-call | flops 2113929216 | bytes 16777216 | tf_op jit(solution)/shard_map/pallas_call | solution.py:179
  80.8 5.4 %shard_map.66 = (bf16[16,5,2,3584]{3,2,1,0:T(2,128)(2,1)S(1)}, bf16[16,5,2,3584]{3,2,1,0:T(2,128)(2,1)S(1)}) custom-call(bf16[16,5,2,3584]{3,2,1,0:T(2,128)(2,1)S(1)} %all-to-all-done.mine_ref.refs_3_, bf16[16,5,2,3584]{3,2,1,0:T(2,128)(2,1)S(1)} %collective-permute-done.4.peer_ref, bf16[3584,512]{1,0:T(8,128)(2,1)S(1)} %bitcast.5, ...), custom_call_target="tpu_custom_call" | custom-call | flops 3523215360 | bytes 16777216 | tf_op jit(solution)/shard_map/pallas_call | solution.py:179
  87.4 16.7 %all_to_all.20.refs_3_ = bf16[16,3,2,3584]{3,2,1,0:T(2,128)(2,1)S(1)} all-to-all(bf16[16,3,2,3584]{3,2,1,0:T(2,128)(2,1)S(1)} %shard_map.69), channel_id=1, replica_groups=mesh['y'=4,'core'=2,'x'=4,'z'=8] {'x','y'}, dimensions={0} | all-to-all | bytes 1376256 | tf_op jit(solution)/shard_map/all_to_all | solution.py:203
  107.5 5.2 %all-to-all-start.3 = ((bf16[16,5,2,3584]{3,2,1,0:T(2,128)(2,1)}), bf16[16,5,2,3584]{3,2,1,0:T(2,128)(2,1)S(1)}, u32[]{:S(2)}, u32[]{:S(2)}) async-start(bf16[16,5,2,3584]{3,2,1,0:T(2,128)(2,1)} %shard_map.71), calls=%async_computation.3 | async-start | bytes 2293760 | tf_op jit(solution)/shard_map/all_to_all | solution.py:203
  112.7 2.2 %collective-permute-start.11 = (bf16[20,3584]{1,0:T(8,128)(2,1)S(1)}, bf16[20,3584]{1,0:T(8,128)(2,1)S(1)}, u32[]{:S(2)}, u32[]{:S(2)}) collective-permute-start(bf16[20,3584]{1,0:T(8,128)(2,1)S(1)} %get-tuple-element.21.refs_0_), channel_id=1, source_target_pairs={{0,7},{1,0},{2,1},{3,2},{4,3},{5,4},{6,5},{7,6},{8,15},{9,8},{10,9... | collective-permute-start | bytes 430088 | tf_op jit(solution)/shard_map/ppermute | solution.py:197
  117.1 3.6 %collective-permute-done.11.add_left = bf16[20,3584]{1,0:T(8,128)(2,1)S(1)} collective-permute-done((bf16[20,3584]{1,0:T(8,128)(2,1)S(1)}, bf16[20,3584]{1,0:T(8,128)(2,1)S(1)}, u32[]{:S(2)}, u32[]{:S(2)}) %collective-permute-start.11) | collective-permute-done | bytes 143392 | tf_op jit(solution)/shard_map/ppermute | solution.py:197
  121.5 4.2 %collective-permute-done.13.add_far = bf16[20,3584]{1,0:T(8,128)(2,1)S(1)} collective-permute-done((bf16[20,3584]{1,0:T(8,128)(2,1)S(1)}, bf16[20,3584]{1,0:T(8,128)(2,1)S(1)}, u32[]{:S(2)}, u32[]{:S(2)}) %collective-permute-start.13) | collective-permute-done | bytes 143392 | tf_op jit(solution)/shard_map/ppermute | solution.py:197
  125.8 3.2 %all-to-all-done.3.rows_ref = bf16[16,5,2,3584]{3,2,1,0:T(2,128)(2,1)S(1)} async-done(((bf16[16,5,2,3584]{3,2,1,0:T(2,128)(2,1)}), bf16[16,5,2,3584]{3,2,1,0:T(2,128)(2,1)S(1)}, u32[]{:S(2)}, u32[]{:S(2)}) %all-to-all-start.3) | async-done | bytes 1146912 | tf_op jit(solution)/shard_map/all_to_all | solution.py:203
  131.7 2.2 %collective-permute-start.14 = (bf16[20,3584]{1,0:T(8,128)(2,1)S(1)}, bf16[20,3584]{1,0:T(8,128)(2,1)S(1)}, u32[]{:S(2)}, u32[]{:S(2)}) collective-permute-start(bf16[20,3584]{1,0:T(8,128)(2,1)S(1)} %get-tuple-element.25), channel_id=1, source_target_pairs={{0,7},{1,0},{2,1},{3,2},{4,3},{5,4},{6,5},{7,6},{8,15},{9,8},{10,9... | collective-permute-start | bytes 430088 | tf_op jit(solution)/shard_map/ppermute | solution.py:197
  133.9 2.2 %collective-permute-start.16 = (bf16[20,3584]{1,0:T(8,128)(2,1)S(1)}, bf16[20,3584]{1,0:T(8,128)(2,1)S(1)}, u32[]{:S(2)}, u32[]{:S(2)}) collective-permute-start(bf16[20,3584]{1,0:T(8,128)(2,1)S(1)} %get-tuple-element.27), channel_id=1, source_target_pairs={{0,6},{1,7},{2,0},{3,1},{4,2},{5,3},{6,4},{7,5},{8,14},{9,15},{10,... | collective-permute-start | bytes 430088 | tf_op jit(solution)/shard_map/ppermute | solution.py:197
  136.8 4.3 %collective-permute-done.14.refs_0_ = bf16[20,3584]{1,0:T(8,128)(2,1)S(1)} collective-permute-done((bf16[20,3584]{1,0:T(8,128)(2,1)S(1)}, bf16[20,3584]{1,0:T(8,128)(2,1)S(1)}, u32[]{:S(2)}, u32[]{:S(2)}) %collective-permute-start.14) | collective-permute-done | bytes 143392 | tf_op jit(solution)/shard_map/ppermute | solution.py:197
  141.2 3.8 %collective-permute-done.15.refs_1_ = bf16[20,3584]{1,0:T(8,128)(2,1)S(1)} collective-permute-done((bf16[20,3584]{1,0:T(8,128)(2,1)S(1)}, bf16[20,3584]{1,0:T(8,128)(2,1)S(1)}, u32[]{:S(2)}, u32[]{:S(2)}) %collective-permute-start.15) | collective-permute-done | bytes 143392 | tf_op jit(solution)/shard_map/ppermute | solution.py:197
  (69 shorter events, 36.4 us)
Async XLA Ops:
  4.5 14.7 %collective-permute-start.2 = (bf16[20,3712]{1,0:T(8,128)(2,1)}, bf16[20,3712]{1,0:T(8,128)(2,1)S(1)}, u32[]{:S(2)}, u32[]{:S(2)}) collective-permute-start(bf16[20,3712]{1,0:T(8,128)(2,1)} %shard_map.64.refs_0_.own), channel_id=1, source_target_pairs={{0,2},{1,3},{2,4},{3,5},{4,6},{5,7},{6,0},{7,1},{8,10},{9,11},{10,... | collective-permute-start | bytes 445448 | tf_op jit(solution)/shard_map/ppermute | solution.py:197
  7.7 13.3 %collective-permute-start.3 = (bf16[20,3712]{1,0:T(8,128)(2,1)}, bf16[20,3712]{1,0:T(8,128)(2,1)S(1)}, u32[]{:S(2)}, u32[]{:S(2)}) collective-permute-start(bf16[20,3712]{1,0:T(8,128)(2,1)} %shard_map.64.refs_0_.own), channel_id=1, source_target_pairs={{0,6},{1,7},{2,0},{3,1},{4,2},{5,3},{6,4},{7,5},{8,14},{9,15},{10,... | collective-permute-start | bytes 445448 | tf_op jit(solution)/shard_map/ppermute | solution.py:197
  10.8 11.9 %collective-permute-start = (bf16[20,3712]{1,0:T(8,128)(2,1)}, bf16[20,3712]{1,0:T(8,128)(2,1)S(1)}, u32[]{:S(2)}, u32[]{:S(2)}) collective-permute-start(bf16[20,3712]{1,0:T(8,128)(2,1)} %shard_map.64.refs_0_.own), channel_id=1, source_target_pairs={{0,1},{1,2},{2,3},{3,4},{4,5},{5,6},{6,7},{7,0},{8,9},{9,10},{10,1... | collective-permute-start | bytes 445448 | tf_op jit(solution)/shard_map/ppermute | solution.py:197
  11.8 12.1 %collective-permute-start.1 = (bf16[20,3712]{1,0:T(8,128)(2,1)}, bf16[20,3712]{1,0:T(8,128)(2,1)S(1)}, u32[]{:S(2)}, u32[]{:S(2)}) collective-permute-start(bf16[20,3712]{1,0:T(8,128)(2,1)} %shard_map.64.refs_0_.own), channel_id=1, source_target_pairs={{0,7},{1,0},{2,1},{3,2},{4,3},{5,4},{6,5},{7,6},{8,15},{9,8},{10,9... | collective-permute-start | bytes 445448 | tf_op jit(solution)/shard_map/ppermute | solution.py:197
  27.4 24.5 %all-to-all-start = ((bf16[16,5,2,3584]{3,2,1,0:T(2,128)(2,1)}), bf16[16,5,2,3584]{3,2,1,0:T(2,128)(2,1)S(1)}, u32[]{:S(2)}, u32[]{:S(2)}) async-start(bf16[16,5,2,3584]{3,2,1,0:T(2,128)(2,1)} %shard_map.65), calls=%async_computation | async-start | bytes 2293760 | tf_op jit(solution)/shard_map/all_to_all | solution.py:203
  34.8 10.2 %collective-permute-start.6 = (bf16[20,3712]{1,0:T(8,128)(2,1)S(1)}, bf16[20,3712]{1,0:T(8,128)(2,1)S(1)}, u32[]{:S(2)}, u32[]{:S(2)}) collective-permute-start(bf16[20,3712]{1,0:T(8,128)(2,1)S(1)} %collective-permute-done.2.refs_3_.left2), channel_id=1, source_target_pairs={{0,1},{1,2},{2,3},{3,4},{4,5},{5,6},{6,7},{7,0},{8,9},{9,10},{10,1... | collective-permute-start | bytes 445448 | tf_op jit(solution)/shard_map/ppermute | solution.py:197
  35.8 12.7 %collective-permute-start.8 = (bf16[20,3712]{1,0:T(8,128)(2,1)S(1)}, bf16[20,3712]{1,0:T(8,128)(2,1)S(1)}, u32[]{:S(2)}, u32[]{:S(2)}) collective-permute-start(bf16[20,3712]{1,0:T(8,128)(2,1)S(1)} %collective-permute-done.2.refs_3_.left2), channel_id=1, source_target_pairs={{0,2},{1,3},{2,4},{3,5},{4,6},{5,7},{6,0},{7,1},{8,10},{9,11},{10,... | collective-permute-start | bytes 445448 | tf_op jit(solution)/shard_map/ppermute | solution.py:197
  39.6 8.9 %collective-permute-start.7 = (bf16[20,3712]{1,0:T(8,128)(2,1)S(1)}, bf16[20,3712]{1,0:T(8,128)(2,1)S(1)}, u32[]{:S(2)}, u32[]{:S(2)}) collective-permute-start(bf16[20,3712]{1,0:T(8,128)(2,1)S(1)} %collective-permute-done.3.refs_4_.right2), channel_id=1, source_target_pairs={{0,7},{1,0},{2,1},{3,2},{4,3},{5,4},{6,5},{7,6},{8,15},{9,8},{10,9... | collective-permute-start | bytes 445448 | tf_op jit(solution)/shard_map/ppermute | solution.py:197
  53.7 14.7 %all-to-all-start.1 = ((bf16[16,3,2,3584]{3,2,1,0:T(2,128)(2,1)}), bf16[16,3,2,3584]{3,2,1,0:T(2,128)(2,1)S(1)}, u32[]{:S(2)}, u32[]{:S(2)}) async-start(bf16[16,3,2,3584]{3,2,1,0:T(2,128)(2,1)} %shard_map.67), calls=%async_computation.1 | async-start | bytes 1376256 | tf_op jit(solution)/shard_map/all_to_all | solution.py:203
  58.5 22.2 %collective-permute-start.4 = (bf16[16,5,2,3584]{3,2,1,0:T(2,128)(2,1)S(1)}, bf16[16,5,2,3584]{3,2,1,0:T(2,128)(2,1)S(1)}, u32[]{:S(2)}, u32[]{:S(2)}) collective-permute-start(bf16[16,5,2,3584]{3,2,1,0:T(2,128)(2,1)S(1)} %all-to-all-done.mine_ref.refs_3_), channel_id=1, source_target_pairs={{0,32},{32,0},{1,33},{33,1},{2,34},{34,2},{3,35},{35,3},{4,36},{36... | collective-permute-start | bytes 3440648 | tf_op jit(solution)/shard_map/ppermute | solution.py:200
  68.4 2.1 %collective-permute-start.9 = (bf16[16,3,2,3584]{3,2,1,0:T(2,128)(2,1)S(1)}, bf16[16,3,2,3584]{3,2,1,0:T(2,128)(2,1)S(1)}, u32[]{:S(2)}, u32[]{:S(2)}) collective-permute-start(bf16[16,3,2,3584]{3,2,1,0:T(2,128)(2,1)S(1)} %all-to-all-done.1.mine_ref), channel_id=1, source_target_pairs={{0,32},{32,0},{1,33},{33,1},{2,34},{34,2},{3,35},{35,3},{4,36},{36... | collective-permute-start | bytes 2064392 | tf_op jit(solution)/shard_map/ppermute | solution.py:200
  80.5 6.3 %collective-permute-start.10 = (bf16[16,3,2,3584]{3,2,1,0:T(2,128)(2,1)S(1)}, bf16[16,3,2,3584]{3,2,1,0:T(2,128)(2,1)S(1)}, u32[]{:S(2)}, u32[]{:S(2)}) collective-permute-start(bf16[16,3,2,3584]{3,2,1,0:T(2,128)(2,1)S(1)} %get-tuple-element.20), channel_id=1, source_target_pairs={{0,32},{32,0},{1,33},{33,1},{2,34},{34,2},{3,35},{35,3},{4,36},{36... | collective-permute-start | bytes 2064392 | tf_op jit(solution)/shard_map/ppermute | solution.py:200
  86.1 19.3 %collective-permute-start.5 = (bf16[16,5,2,3584]{3,2,1,0:T(2,128)(2,1)S(1)}, bf16[16,5,2,3584]{3,2,1,0:T(2,128)(2,1)S(1)}, u32[]{:S(2)}, u32[]{:S(2)}) collective-permute-start(bf16[16,5,2,3584]{3,2,1,0:T(2,128)(2,1)S(1)} %get-tuple-element.18), channel_id=1, source_target_pairs={{0,32},{32,0},{1,33},{33,1},{2,34},{34,2},{3,35},{35,3},{4,36},{36... | collective-permute-start | bytes 3440648 | tf_op jit(solution)/shard_map/ppermute | solution.py:200
  87.4 16.7 %copy-start.9 = (bf16[20,3712]{1,0:T(8,128)(2,1)S(1)}, bf16[20,3712]{1,0:T(8,128)(2,1)}, u32[]{:S(2)}) copy-start(bf16[20,3712]{1,0:T(8,128)(2,1)} %copy-done.8) | copy-start | bytes 445444
  107.5 21.5 %copy-start.5 = (bf16[20,3712]{1,0:T(8,128)(2,1)S(1)}, bf16[20,3712]{1,0:T(8,128)(2,1)}, u32[]{:S(2)}) copy-start(bf16[20,3712]{1,0:T(8,128)(2,1)} %shard_map.64.refs_0_.own) | copy-start | bytes 445444
  107.5 21.5 %copy-start.7 = (bf16[20,3712]{1,0:T(8,128)(2,1)S(1)}, bf16[20,3712]{1,0:T(8,128)(2,1)}, u32[]{:S(2)}) copy-start(bf16[20,3712]{1,0:T(8,128)(2,1)} %copy-done.6) | copy-start | bytes 445444
  107.5 21.5 %all-to-all-start.3 = ((bf16[16,5,2,3584]{3,2,1,0:T(2,128)(2,1)}), bf16[16,5,2,3584]{3,2,1,0:T(2,128)(2,1)S(1)}, u32[]{:S(2)}, u32[]{:S(2)}) async-start(bf16[16,5,2,3584]{3,2,1,0:T(2,128)(2,1)} %shard_map.71), calls=%async_computation.3 | async-start | bytes 2293760 | tf_op jit(solution)/shard_map/all_to_all | solution.py:203
  112.7 8.0 %collective-permute-start.11 = (bf16[20,3584]{1,0:T(8,128)(2,1)S(1)}, bf16[20,3584]{1,0:T(8,128)(2,1)S(1)}, u32[]{:S(2)}, u32[]{:S(2)}) collective-permute-start(bf16[20,3584]{1,0:T(8,128)(2,1)S(1)} %get-tuple-element.21.refs_0_), channel_id=1, source_target_pairs={{0,7},{1,0},{2,1},{3,2},{4,3},{5,4},{6,5},{7,6},{8,15},{9,8},{10,9... | collective-permute-start | bytes 430088 | tf_op jit(solution)/shard_map/ppermute | solution.py:197
  114.9 6.6 %collective-permute-start.12 = (bf16[20,3584]{1,0:T(8,128)(2,1)S(1)}, bf16[20,3584]{1,0:T(8,128)(2,1)S(1)}, u32[]{:S(2)}, u32[]{:S(2)}) collective-permute-start(bf16[20,3584]{1,0:T(8,128)(2,1)S(1)} %get-tuple-element.22), channel_id=1, source_target_pairs={{0,1},{1,2},{2,3},{3,4},{4,5},{5,6},{6,7},{7,0},{8,9},{9,10},{10,1... | collective-permute-start | bytes 430088 | tf_op jit(solution)/shard_map/ppermute | solution.py:197
  114.9 10.9 %collective-permute-start.13 = (bf16[20,3584]{1,0:T(8,128)(2,1)S(1)}, bf16[20,3584]{1,0:T(8,128)(2,1)S(1)}, u32[]{:S(2)}, u32[]{:S(2)}) collective-permute-start(bf16[20,3584]{1,0:T(8,128)(2,1)S(1)} %get-tuple-element.23), channel_id=1, source_target_pairs={{0,6},{1,7},{2,0},{3,1},{4,2},{5,3},{6,4},{7,5},{8,14},{9,15},{10,... | collective-permute-start | bytes 430088 | tf_op jit(solution)/shard_map/ppermute | solution.py:197
  131.7 9.5 %collective-permute-start.14 = (bf16[20,3584]{1,0:T(8,128)(2,1)S(1)}, bf16[20,3584]{1,0:T(8,128)(2,1)S(1)}, u32[]{:S(2)}, u32[]{:S(2)}) collective-permute-start(bf16[20,3584]{1,0:T(8,128)(2,1)S(1)} %get-tuple-element.25), channel_id=1, source_target_pairs={{0,7},{1,0},{2,1},{3,2},{4,3},{5,4},{6,5},{7,6},{8,15},{9,8},{10,9... | collective-permute-start | bytes 430088 | tf_op jit(solution)/shard_map/ppermute | solution.py:197
  133.9 11.1 %collective-permute-start.15 = (bf16[20,3584]{1,0:T(8,128)(2,1)S(1)}, bf16[20,3584]{1,0:T(8,128)(2,1)S(1)}, u32[]{:S(2)}, u32[]{:S(2)}) collective-permute-start(bf16[20,3584]{1,0:T(8,128)(2,1)S(1)} %get-tuple-element.26), channel_id=1, source_target_pairs={{0,1},{1,2},{2,3},{3,4},{4,5},{5,6},{6,7},{7,0},{8,9},{9,10},{10,1... | collective-permute-start | bytes 430088 | tf_op jit(solution)/shard_map/ppermute | solution.py:197
  133.9 11.1 %collective-permute-start.16 = (bf16[20,3584]{1,0:T(8,128)(2,1)S(1)}, bf16[20,3584]{1,0:T(8,128)(2,1)S(1)}, u32[]{:S(2)}, u32[]{:S(2)}) collective-permute-start(bf16[20,3584]{1,0:T(8,128)(2,1)S(1)} %get-tuple-element.27), channel_id=1, source_target_pairs={{0,6},{1,7},{2,0},{3,1},{4,2},{5,3},{6,4},{7,5},{8,14},{9,15},{10,... | collective-permute-start | bytes 430088 | tf_op jit(solution)/shard_map/ppermute | solution.py:197
  136.1 8.9 %collective-permute-start.17 = (bf16[20,3584]{1,0:T(8,128)(2,1)S(1)}, bf16[20,3584]{1,0:T(8,128)(2,1)S(1)}, u32[]{:S(2)}, u32[]{:S(2)}) collective-permute-start(bf16[20,3584]{1,0:T(8,128)(2,1)S(1)} %get-tuple-element.28), channel_id=1, source_target_pairs={{0,2},{1,3},{2,4},{3,5},{4,6},{5,7},{6,0},{7,1},{8,10},{9,11},{10,... | collective-permute-start | bytes 430088 | tf_op jit(solution)/shard_map/ppermute | solution.py:197
  (16 other events, 74.0 us)

commit v3 on v0

v3 whole, which is shorter than its diff:
```python
import functools

import jax
import jax.numpy as jnp
from jax import lax
from jax.experimental import pallas as pl
from jax.experimental.pallas import tpu as pltpu
from jax.sharding import Mesh, PartitionSpec as P

F32, BF16 = jnp.float32, jnp.bfloat16
SLOTS = 2
AXES = ("y", "core", "x", "z")
CHIPS = ("x", "z", "y")
EXTENT = {"y": 4, "x": 4, "z": 8}
WEIGHT = {"y": 32, "x": 8, "z": 1}
CUT = 512
STRIDE = 32
VMEM = pl.BlockSpec(memory_space=pltpu.VMEM)
ANY = pl.BlockSpec(memory_space=pl.ANY)
PICK_MIB = 8
FFN_MIB = 28
LOAD_MIB = 16


def params(mib):
    return pltpu.CompilerParams(vmem_limit_bytes=mib << 20)


def cost(flops, read):
    return pl.CostEstimate(flops=flops, bytes_accessed=read, transcendentals=0)


def expert_at(place):
    expert, inner = 0, 1
    for axis in reversed(CHIPS):
        expert = expert + place // inner % EXTENT[axis] * WEIGHT[axis]
        inner *= EXTENT[axis]
    return expert


def upright(piece):
    size = piece.shape[0]
    same = lax.broadcasted_iota(jnp.int32, (size, size), 0) == lax.broadcasted_iota(jnp.int32, (size, size), 1)
    return lax.dot_general(
        piece.astype(BF16), same.astype(F32).astype(BF16), (((0,), (0,)), ((), ())), preferred_element_type=F32
    )


def slot_parts(ids, lanes):
    tokens, top = ids.shape
    lane = lax.broadcasted_iota(jnp.int32, (tokens, lanes), 1)
    expert = expert_at(lane // SLOTS).astype(F32)
    named = [ids[:, k : k + 1] == expert for k in range(top)]
    hits = functools.reduce(jnp.logical_or, named)
    row = lax.broadcasted_iota(jnp.int32, (tokens, tokens), 0)
    before = lax.broadcasted_iota(jnp.int32, (tokens, tokens), 1) < row
    rank = jnp.dot(before.astype(F32).astype(BF16), hits.astype(F32).astype(BF16), preferred_element_type=F32)
    return named, hits, rank == (lane % SLOTS).astype(F32)


def pick_kernel(ids_ref, tokens_ref, out_ref):
    experts, slots, features = out_ref.shape
    unused, hits, here = slot_parts(upright(ids_ref[...].astype(F32)), experts * slots)
    chosen = (hits & here).astype(F32).astype(BF16)
    for at in range(0, features, CUT):
        cols = slice(at, at + CUT)
        rows = lax.dot_general(chosen, tokens_ref[:, cols], (((0,), (0,)), ((), ())), preferred_element_type=F32)
        out_ref[:, :, cols] = rows.astype(BF16).reshape(experts, slots, CUT)


def table_kernel(ids_ref, weights_ref, unused_ref, out_ref):
    tokens = ids_ref.shape[1]
    named, unused, here = slot_parts(upright(ids_ref[...].astype(F32)), out_ref.shape[1])
    weights = weights_ref[...]
    high = weights.astype(BF16)
    rest = weights - high.astype(F32)
    mid = rest.astype(BF16)
    low = (rest - mid.astype(F32)).astype(BF16)
    out_ref[...] = jnp.zeros_like(out_ref)
    for place, piece in enumerate((high, mid, low)):
        piece = upright(piece.astype(F32))
        value = jnp.zeros(here.shape, F32)
        for k, hit in enumerate(named):
            value = value + jnp.where(hit & here, piece[:, k : k + 1], 0.0)
        out_ref[place * STRIDE : place * STRIDE + tokens] = value.astype(BF16)


def mix_kernel(table_ref, rows_ref, out_ref):
    tokens = out_ref.shape[0]
    experts, slots, features = rows_ref.shape
    tables = [table_ref[place * STRIDE : place * STRIDE + tokens] for place in range(3)]
    for at in range(0, features, CUT):
        rows = rows_ref[:, :, at : at + CUT].reshape(experts * slots, CUT)
        value = sum(jnp.dot(table, rows, preferred_element_type=F32) for table in tables)
        out_ref[:, at : at + CUT] = value.astype(BF16)


def join_kernel(mine_ref, other_ref, unused_ref, out):
    for at in range(0, out.shape[2], CUT):
        parts = [ref[:, :, at : at + CUT].reshape(-1, CUT).astype(F32) for ref in (mine_ref, other_ref)]
        out[:, :, at : at + CUT] = (parts[0] + parts[1]).astype(BF16).reshape(*out.shape[:2], CUT)


def join(mine, other, after):
    return pl.pallas_call(
        join_kernel,
        in_specs=[VMEM] * 2 + [ANY],
        out_shape=jax.ShapeDtypeStruct(mine.shape, BF16),
        compiler_params=params(8),
        cost_estimate=cost(1 << 20, 3 << 20),
    )(mine, other, after)


def expert_kernel(rows_ref, gate, up, down, out_ref, rows, hidden):
    count, features = rows.shape
    units = hidden.shape[1]
    rows[...] = rows_ref[...].reshape(count, features)
    for at in range(0, units, 256):
        cols = slice(at, at + 256)
        gate_act = jnp.dot(rows[...], gate[:, cols], preferred_element_type=F32)
        up_act = jnp.dot(rows[...], up[:, cols], preferred_element_type=F32)
        hidden[:, cols] = (gate_act / (1.0 + jnp.exp(-gate_act)) * up_act).astype(BF16)
    for at in range(0, features, 256):
        cols = slice(at, at + 256)
        part = jnp.dot(hidden[...], down[:, cols], preferred_element_type=F32).astype(BF16)
        out_ref[:, :, cols] = part.reshape(*out_ref.shape[:2], 256)


def load_kernel(*refs):
    count = (len(refs) - 2) // 2
    sources, targets, sems = refs[:count], refs[count + 1 : -1], refs[-1]
    copies = [pltpu.make_async_copy(a, b, sems.at[i]) for i, (a, b) in enumerate(zip(sources, targets))]
    for copy in copies:
        copy.start()
    for copy in copies:
        copy.wait()


def load(values, after):
    return pl.pallas_call(
        load_kernel,
        in_specs=[ANY] * (len(values) + 1),
        out_specs=[VMEM] * len(values),
        out_shape=[jax.ShapeDtypeStruct(v.shape, v.dtype) for v in values],
        scratch_shapes=[pltpu.SemaphoreType.DMA((len(values),))],
        compiler_params=params(LOAD_MIB),
        cost_estimate=cost(0, sum(v.size * 2 for v in values)),
    )(*values, after)


def run_expert(rows, gate, up, down):
    features, units = gate.shape
    count = rows.size // features
    return pl.pallas_call(
        expert_kernel,
        in_specs=[VMEM] * 4,
        out_specs=VMEM,
        out_shape=jax.ShapeDtypeStruct(rows.shape, BF16),
        scratch_shapes=[pltpu.VMEM((count, features), BF16), pltpu.VMEM((count, units), BF16)],
        compiler_params=params(FFN_MIB),
        cost_estimate=pl.CostEstimate(
            flops=6 * count * features * units, bytes_accessed=15 << 20, transcendentals=count * units
        ),
    )(rows, gate, up, down)


def on_device(tokens, expert_ids, route_weights, w_gate, w_up, w_down):
    experts = lax.axis_size("y") * lax.axis_size("x") * lax.axis_size("z")
    ids, weights = expert_ids.T, route_weights.T
    matrices = w_gate[0, 0], w_up[0, 0], w_down[0, 0]

    def swap(value):
        return lax.ppermute(value, "core", [(0, 1), (1, 0)])

    def spread(value):
        return lax.all_to_all(value, CHIPS, 0, 0, tiled=True)

    picked = pl.pallas_call(
        pick_kernel,
        out_shape=jax.ShapeDtypeStruct((experts, SLOTS, tokens.shape[1]), BF16),
        compiler_params=params(PICK_MIB),
        cost_estimate=cost(1 << 28, 4 << 20),
    )(ids, tokens)
    mine = spread(picked)
    peer = swap(mine)
    table = pl.pallas_call(
        table_kernel,
        in_specs=[VMEM] * 2 + [ANY],
        out_shape=jax.ShapeDtypeStruct((3 * STRIDE, experts * SLOTS), BF16),
        compiler_params=params(8),
        cost_estimate=cost(1 << 22, 1 << 18),
    )(ids, weights, mine)
    matrices = matrices[:1] + tuple(load(matrices[1:], mine))
    mine_part = run_expert(mine, *matrices)
    peer_part = run_expert(peer, *matrices)
    returned = spread(join(mine_part, swap(peer_part), table))
    return pl.pallas_call(
        mix_kernel,
        out_shape=jax.ShapeDtypeStruct(tokens.shape, BF16),
        compiler_params=params(8),
        cost_estimate=cost(1 << 29, 4 << 20),
    )(table, returned)


def solution(mesh):
    groups, members = mesh.devices.shape
    fine = Mesh(mesh.devices.reshape(groups // 2, 2, 4, members // 4), AXES)
    rows = P(AXES, None)
    weights = P(("y", "core"), ("x", "z"), None, None)
    return jax.shard_map(
        on_device, mesh=fine, in_specs=(rows, rows, rows, weights, weights, weights), out_specs=rows, check_vma=False
    )
```

time: 362 us -> 133 us (0.37)
  blocking collectives: 233 us -> 116 us
  local copies, waits for them, and re-layouts: 51.4 us -> 3.96 us
  waiting for transfers between devices: 42.6 us -> 1.22 us
  matrix products: 15.6 us -> 0 us
  Pallas kernels: 0 us -> 11.1 us
  other arithmetic: 10.8 us -> 0 us
  starting transfers between devices: 5.97 us -> 0.6 us
    all_to_all x3 -> x2, blocking collectives: 233 us -> 116 us  [spread(): return lax.all_to_all(value, CHIPS, 0, 0, tiled=True)]
    all_to_all x1 -> x0, waiting for transfers between devices: 42.6 us -> none  [on_device(): lax.all_to_all(returned, 'group', split_axis=0, concat_axis=0, tiled=True)]
    reshape x3 -> x0, local copies, waits for them, and re-layouts: 22.4 us -> none  [the longest x2 14 us: on_device(): partial_value.reshape(item_count, members, capacity, features)]
    dot_general x3 -> x0, matrix products: 15.6 us -> none  [the longest x1 10.1 us: on_device(): jnp.dot(hidden, down_rows, preferred_element_type=jnp.float32)]
    all_to_all x3 -> x0, local copies, waits for them, and re-layouts: 13.1 us -> none  [the longest x1 4.66 us: on_device(): lax.all_to_all(partial_value, 'expert', split_axis=1, concat_axis=1, tile...]
    pallas_call x0 -> x7, Pallas kernels: none -> 11.1 us  [the longest x2 6.22 us: run_expert(): pl.pallas_call(expert_kernel, in_specs=[VMEM] * 4, out_specs=VMEM, out_sh...]
    all_to_all x1 -> x0, starting transfers between devices: 5.97 us -> none  [on_device(): lax.all_to_all(returned, 'group', split_axis=0, concat_axis=0, tiled=True)]
    convert_element_type x2 -> x0, other arithmetic: 5.2 us -> none  [the longest x1 5.19 us: on_device(): (pair_parts[:, 0].astype(jnp.float32) + pair_parts[:, 1].astype(jnp.float...]
  transfers between devices with their start and end apart: 1 -> 2, of which waited for: 1 -> 1; matrix products, arithmetic and copies ran while one was open for 0% -> 0% of each run, Pallas kernels for 0% -> 3%
where the time goes in v3:
time: 133 us
  blocking collectives  116 us (87%)
  Pallas kernels  11.1 us (8%)
  local copies, waits for them, and re-layouts  3.96 us (3%)
    all_to_all x2, blocking collectives, spread(): return lax.all_to_all(value, CHIPS, 0, 0, tiled=True)  116 us
    pallas_call x2, Pallas kernels, run_expert(): pl.pallas_call(expert_kernel, in_specs=[VMEM] * 4, out_specs=VMEM, out_sh...  6.22 us
    unnamed x14, local copies, waits for them, and re-layouts  3.96 us
  transfers between devices with their start and end apart: 2, of which 1 were waited for; matrix products, arithmetic and copies ran while one was open for 0% of the time, Pallas kernels for 3%

profile of v3, /device:TPU:8, one launch (start us, length us, event | category | flops | bytes accessed | tf_op | source)
XLA Modules:
  0.0 132.6 jit_solution(13641268314019850948)
XLA Ops:
  0.0 0.0 copy-start.3
  0.0 0.9 copy-done.3
  0.9 0.0 copy-start.4
  0.9 0.7 copy-done.4
  1.6 1.1 shard_map.64
  2.7 0.0 copy-start.1
  2.7 61.6 %all_to_all.10.unused_ref.refs_2_.rows_ref = bf16[128,2,3584]{2,1,0:T(2,128)(2,1)S(1)} all-to-all(bf16[128,2,3584]{2,1,0:T(2,128)(2,1)S(1)} %shard_map.64), channel_id=1, replica_groups=mesh['y'=4,'core'=2,'x'=4,'z'=8] {'x','z','y'}, dimensions={0} | all-to-all | bytes 3670016 | tf_op jit(solution)/shard_map/all_to_all | solution.py:176
  64.3 0.0 collective-permute-start
  64.3 0.0 copy-done.1
  64.3 0.0 copy-start.2
  64.3 2.0 %copy-done.2 = bf16[1,1,512,3584]{3,2,1,0:T(8,128)(2,1)S(1)} copy-done((bf16[1,1,512,3584]{3,2,1,0:T(8,128)(2,1)S(1)}, bf16[1,1,512,3584]{3,2,1,0:T(8,128)(2,1)}, u32[]{:S(2)}) %copy-start.2) | copy-done | bytes 3670040
  66.4 0.5 shard_map.66
  66.9 1.2 collective-permute-done.rows_ref
  68.1 0.3 copy-done
  68.4 3.1 %shard_map.68 = bf16[128,2,3584]{2,1,0:T(2,128)(2,1)S(1)} custom-call(bf16[128,2,3584]{2,1,0:T(2,128)(2,1)S(1)} %collective-permute-done.rows_ref, bf16[3584,512]{1,0:T(8,128)(2,1)S(1)} %bitcast.5, bf16[3584,512]{1,0:T(8,128)(2,1)S(1)} %get-tuple-element.7.up, bf16[512,3584]{1,0:T(8,128)(2,1)S(1)} %get-tuple-element.8.down), custom_call_target="tpu_custom_call" | custom-call | flops 2818572288 | bytes 15728640 | tf_op jit(solution)/shard_map/pallas_call | solution.py:154
  71.5 0.6 collective-permute-start.1
  72.1 0.0 copy-done.5
  72.1 0.0 copy-done.6
  72.1 0.6 shard_map.65.unused_ref.table_ref
  72.7 3.1 %shard_map.67.mine_ref = bf16[128,2,3584]{2,1,0:T(2,128)(2,1)S(1)} custom-call(bf16[128,2,3584]{2,1,0:T(2,128)(2,1)S(1)} %all_to_all.10.unused_ref.refs_2_.rows_ref, bf16[3584,512]{1,0:T(8,128)(2,1)S(1)} %bitcast.6, bf16[3584,512]{1,0:T(8,128)(2,1)S(1)} %get-tuple-element.7.up, bf16[512,3584]{1,0:T(8,128)(2,1)S(1)} %get-tuple-element.8.down), custom_call_target="tpu_custom_call" | custom-call | flops 2818572288 | bytes 15728640 | tf_op jit(solution)/shard_map/pallas_call | solution.py:154
  75.8 0.0 collective-permute-done.1.other_ref
  75.8 1.0 shard_map.69
  76.9 54.0 %all_to_all.11.rows_ref = bf16[128,2,3584]{2,1,0:T(2,128)(2,1)S(1)} all-to-all(bf16[128,2,3584]{2,1,0:T(2,128)(2,1)S(1)} %shard_map.69), channel_id=1, replica_groups=mesh['y'=4,'core'=2,'x'=4,'z'=8] {'x','z','y'}, dimensions={0} | all-to-all | bytes 3670016 | tf_op jit(solution)/shard_map/all_to_all | solution.py:176
  130.9 1.7 %shard_map.70 = bf16[20,3584]{1,0:T(8,128)(2,1)} custom-call(bf16[96,256]{1,0:T(8,128)(2,1)S(1)} %shard_map.65.unused_ref.table_ref, bf16[128,2,3584]{2,1,0:T(2,128)(2,1)S(1)} %all_to_all.11.rows_ref), custom_call_target="tpu_custom_call" | custom-call | flops 536870912 | bytes 4194304 | tf_op jit(solution)/shard_map/pallas_call | solution.py:197
  (3 shorter events, 0.0 us)
Async XLA Ops:
  0.0 0.9 copy-start.3
  0.9 0.7 copy-start.4
  2.7 61.6 %copy-start.1 = (bf16[1,1,3584,512]{3,2,1,0:T(8,128)(2,1)S(1)}, bf16[1,1,3584,512]{3,2,1,0:T(8,128)(2,1)}, u32[]{:S(2)}) copy-start(bf16[1,1,3584,512]{3,2,1,0:T(8,128)(2,1)} %param.10) | copy-start | bytes 11010052
  64.3 3.8 %collective-permute-start = (bf16[128,2,3584]{2,1,0:T(2,128)(2,1)S(1)}, bf16[128,2,3584]{2,1,0:T(2,128)(2,1)S(1)}, u32[]{:S(2)}, u32[]{:S(2)}) collective-permute-start(bf16[128,2,3584]{2,1,0:T(2,128)(2,1)S(1)} %all_to_all.10.unused_ref.refs_2_.rows_ref), channel_id=1, source_target_pairs={{0,32},{32,0},{1,33},{33,1},{2,34},{34,2},{3,35},{35,3},{4,36},{36... | collective-permute-start | bytes 5505032 | tf_op jit(solution)/shard_map/ppermute | solution.py:173
  64.3 2.0 %copy-start.2 = (bf16[1,1,512,3584]{3,2,1,0:T(8,128)(2,1)S(1)}, bf16[1,1,512,3584]{3,2,1,0:T(8,128)(2,1)}, u32[]{:S(2)}) copy-start(bf16[1,1,512,3584]{3,2,1,0:T(8,128)(2,1)} %param.11) | copy-start | bytes 11010052
  66.4 2.0 %copy-start = (bf16[1,1,3584,512]{3,2,1,0:T(8,128)(2,1)S(1)}, bf16[1,1,3584,512]{3,2,1,0:T(8,128)(2,1)}, u32[]{:S(2)}) copy-start(bf16[1,1,3584,512]{3,2,1,0:T(8,128)(2,1)} %param.9) | copy-start | bytes 11010052
  68.4 3.7 %copy-start.5 = (s32[20,8]{0,1:T(8,128)S(1)}, s32[20,8]{0,1:T(8,128)}, u32[]{:S(2)}) copy-start(s32[20,8]{0,1:T(8,128)} %param.7) | copy-start | bytes 1924
  68.4 3.7 %copy-start.6 = (f32[20,8]{0,1:T(8,128)S(1)}, f32[20,8]{0,1:T(8,128)}, u32[]{:S(2)}) copy-start(f32[20,8]{0,1:T(8,128)} %param.8) | copy-start | bytes 1924
  71.5 4.3 %collective-permute-start.1 = (bf16[128,2,3584]{2,1,0:T(2,128)(2,1)S(1)}, bf16[128,2,3584]{2,1,0:T(2,128)(2,1)S(1)}, u32[]{:S(2)}, u32[]{:S(2)}) collective-permute-start(bf16[128,2,3584]{2,1,0:T(2,128)(2,1)S(1)} %shard_map.68), channel_id=1, source_target_pairs={{0,32},{32,0},{1,33},{33,1},{2,34},{34,2},{3,35},{35,3},{4,36},{36... | collective-permute-start | bytes 5505032 | tf_op jit(solution)/shard_map/ppermute | solution.py:173

commit v4 on v3

v4 whole, which is shorter than its diff:
```python
import functools

import jax
import jax.numpy as jnp
from jax import lax
from jax.experimental import pallas as pl
from jax.experimental.pallas import tpu as pltpu
from jax.sharding import Mesh, PartitionSpec as P

F32, BF16 = jnp.float32, jnp.bfloat16
SLOTS = 2
AXES = ("y", "core", "x", "z")
BLOCKS = 4
CUT = 512
STRIDE = 32
VMEM = pl.BlockSpec(memory_space=pltpu.VMEM)
SMEM = pl.BlockSpec(memory_space=pltpu.SMEM)
ANY = pl.BlockSpec(memory_space=pl.ANY)
PICK_MIB = 12
FFN_MIB = 28


def params(mib):
    return pltpu.CompilerParams(vmem_limit_bytes=mib << 20)


def cost(flops, read):
    return pl.CostEstimate(flops=flops, bytes_accessed=read, transcendentals=0)


def upright(piece):
    size = piece.shape[0]
    same = lax.broadcasted_iota(jnp.int32, (size, size), 0) == lax.broadcasted_iota(jnp.int32, (size, size), 1)
    return lax.dot_general(
        piece.astype(BF16), same.astype(F32).astype(BF16), (((0,), (0,)), ((), ())), preferred_element_type=F32
    )


def slot_parts(info, planes_ref, lanes, tokens):
    size, top = info.shape[0], info.shape[1] // 2
    lane = lax.broadcasted_iota(jnp.int32, (size, lanes), 1)
    row = lax.broadcasted_iota(jnp.int32, (size, lanes), 0)
    device = lane // (BLOCKS * SLOTS)
    plane = jnp.where(device // 4 % 2 == 0, planes_ref[0], planes_ref[1])
    expert = (device % 4 * 32 + device // 8 * 8 + plane).astype(F32)
    fits = (row // STRIDE == lane // SLOTS % BLOCKS) & (row % STRIDE < tokens)
    named = [(info[:, k : k + 1] == expert) & fits for k in range(top)]
    hits = functools.reduce(jnp.logical_or, named)
    first = lax.broadcasted_iota(jnp.int32, (size, size), 0)
    second = lax.broadcasted_iota(jnp.int32, (size, size), 1)
    before = (first // STRIDE == second // STRIDE) & (second < first)
    rank = jnp.dot(before.astype(F32).astype(BF16), hits.astype(F32).astype(BF16), preferred_element_type=F32)
    return named, hits, rank == (lane % SLOTS).astype(F32)


def gather_info(infos, scratch):
    scratch[...] = jnp.zeros_like(scratch)
    for b, ref in enumerate(infos):
        value = ref[...]
        high = value.astype(BF16)
        rest = value - high.astype(F32)
        mid = rest.astype(BF16)
        low = (rest - mid.astype(F32)).astype(BF16)
        for place, piece in enumerate((high, mid, low)):
            scratch[place, b * STRIDE : b * STRIDE + value.shape[1]] = upright(piece)


def pick_kernel(planes_ref, *refs):
    infos, blocks, (out_ref, info, table) = refs[:BLOCKS], refs[BLOCKS : 2 * BLOCKS], refs[2 * BLOCKS :]
    tokens = blocks[0].shape[0]
    devices, each, features = out_ref.shape
    table[...] = jnp.zeros_like(table)
    for b, block in enumerate(blocks):
        table[b * STRIDE : b * STRIDE + tokens] = block[...]
    gather_info(infos, info)
    unused, hits, here = slot_parts(info[0], planes_ref, devices * each, tokens)
    chosen = (hits & here).astype(F32).astype(BF16)
    for at in range(0, features, CUT):
        cols = slice(at, at + CUT)
        rows = lax.dot_general(chosen, table[:, cols], (((0,), (0,)), ((), ())), preferred_element_type=F32)
        out_ref[:, :, cols] = rows.astype(BF16).reshape(devices, each, CUT)


def pick(planes, infos, blocks, devices):
    tokens, features = blocks[0].shape
    return pl.pallas_call(
        pick_kernel,
        in_specs=[SMEM] + [VMEM] * (2 * BLOCKS),
        out_shape=jax.ShapeDtypeStruct((devices, BLOCKS * SLOTS, features), BF16),
        scratch_shapes=[
            pltpu.VMEM((3, BLOCKS * STRIDE, infos[0].shape[0]), F32),
            pltpu.VMEM((BLOCKS * STRIDE, features), BF16),
        ],
        compiler_params=params(PICK_MIB),
        cost_estimate=cost(1 << 35, 4 << 20),
    )(planes, *infos, *blocks)


def table_kernel(planes_ref, *refs):
    infos, (out_ref, info) = refs[:BLOCKS], refs[BLOCKS + 1 :]
    gather_info(infos, info)
    named, unused, here = slot_parts(info[0], planes_ref, out_ref.shape[2], infos[0].shape[1])
    top = len(named)
    for place in range(3):
        value = jnp.zeros(here.shape, F32)
        for k, hit in enumerate(named):
            value = value + jnp.where(hit & here, info[place, :, top + k : top + k + 1], 0.0)
        out_ref[place] = value.astype(BF16)


def make_table(planes, infos, devices, after):
    return pl.pallas_call(
        table_kernel,
        in_specs=[SMEM] + [VMEM] * BLOCKS + [ANY],
        out_shape=jax.ShapeDtypeStruct((3, BLOCKS * STRIDE, devices * BLOCKS * SLOTS), BF16),
        scratch_shapes=[pltpu.VMEM((3, BLOCKS * STRIDE, infos[0].shape[0]), F32)],
        compiler_params=params(8),
        cost_estimate=cost(1 << 22, 1 << 18),
    )(planes, *infos, after)


def mix_kernel(table_ref, rows_ref, *outs):
    tokens = outs[0].shape[0]
    devices, each, features = rows_ref.shape
    for at in range(0, features, CUT):
        cols = slice(at, at + CUT)
        rows = rows_ref[:, :, cols].reshape(devices * each, CUT)
        total = sum(jnp.dot(table_ref[place], rows, preferred_element_type=F32) for place in range(3))
        for b, out in enumerate(outs):
            out[:, cols] = total[b * STRIDE : b * STRIDE + tokens].astype(out.dtype)


def sum_kernel(own, *refs):
    total = own[...]
    for ref in refs[:-1]:
        total = total + ref[...].astype(F32)
    refs[-1][...] = total.astype(BF16)


def join_kernel(mine_ref, other_ref, unused_ref, out):
    for at in range(0, out.shape[2], CUT):
        parts = [ref[:, :, at : at + CUT].reshape(-1, CUT).astype(F32) for ref in (mine_ref, other_ref)]
        out[:, :, at : at + CUT] = (parts[0] + parts[1]).astype(BF16).reshape(*out.shape[:2], CUT)


def join(mine, other, after):
    return pl.pallas_call(
        join_kernel,
        in_specs=[VMEM] * 2 + [ANY],
        out_shape=jax.ShapeDtypeStruct(mine.shape, BF16),
        compiler_params=params(8),
        cost_estimate=cost(1 << 20, 3 << 20),
    )(mine, other, after)


def expert_kernel(rows_ref, gate, up, down, out_ref, rows, hidden):
    count, features = rows.shape
    units = hidden.shape[1]
    rows[...] = rows_ref[...].reshape(count, features)
    for at in range(0, units, 256):
        cols = slice(at, at + 256)
        gate_act = jnp.dot(rows[...], gate[:, cols], preferred_element_type=F32)
        up_act = jnp.dot(rows[...], up[:, cols], preferred_element_type=F32)
        hidden[:, cols] = (gate_act / (1.0 + jnp.exp(-gate_act)) * up_act).astype(BF16)
    for at in range(0, features, 256):
        cols = slice(at, at + 256)
        part = jnp.dot(hidden[...], down[:, cols], preferred_element_type=F32).astype(BF16)
        out_ref[:, :, cols] = part.reshape(*out_ref.shape[:2], 256)


def run_expert(rows, gate, up, down):
    features, units = gate.shape
    count = rows.size // features
    return pl.pallas_call(
        expert_kernel,
        in_specs=[VMEM] * 4,
        out_specs=VMEM,
        out_shape=jax.ShapeDtypeStruct(rows.shape, BF16),
        scratch_shapes=[pltpu.VMEM((count, features), BF16), pltpu.VMEM((count, units), BF16)],
        compiler_params=params(FFN_MIB),
        cost_estimate=pl.CostEstimate(
            flops=6 * count * features * units, bytes_accessed=15 << 20, transcendentals=count * units
        ),
    )(rows, gate, up, down)


def on_device(tokens, expert_ids, route_weights, w_gate, w_up, w_down):
    ring, depth, width = lax.axis_size("z"), lax.axis_size("x"), lax.axis_size("y")
    matrices = w_gate[0, 0], w_up[0, 0], w_down[0, 0]
    core, z = lax.axis_index("core"), lax.axis_index("z")
    pair = (z - core + ring) % ring // 2
    planes = jnp.stack([(2 * pair + member + core) % ring for member in range(2)]).astype(jnp.int32)

    def route(by, back):
        pairs = []
        for c in range(2):
            for s in range(ring):
                t = s + by if (s + by) % 2 == 0 else s - by
                pairs.append((c * ring + (s + c) % ring, c * ring + (t + c) % ring))
        return [(b, a) for a, b in pairs] if back else pairs

    def send(value, by, back=False):
        return lax.ppermute(value, ("core", "z"), route(by, back))

    groups = [
        [
            ((y * 2 + c) * depth + x) * ring + (2 * p + member + c) % ring
            for x in range(depth)
            for member in range(2)
            for y in range(width)
        ]
        for c in range(2)
        for p in range(ring // 2)
    ]

    def spread(value):
        return lax.all_to_all(value, AXES, 0, 0, axis_index_groups=groups, tiled=True)

    def swap(value):
        return lax.ppermute(value, "core", [(0, 1), (1, 0)])

    info = jnp.concatenate([expert_ids.T.astype(F32), route_weights.T], axis=0)
    blocks, infos = [tokens], [info]
    blocks += [send(tokens, by) for by in range(1, BLOCKS)]
    infos += [send(info, by) for by in range(1, BLOCKS)]
    devices = 2 * depth * width
    mine = spread(pick(planes, infos, blocks, devices))
    peer = swap(mine)
    table = make_table(planes, infos, devices, mine)
    mine_part = run_expert(mine, *matrices)
    peer_part = run_expert(peer, *matrices)
    returned = spread(join(mine_part, swap(peer_part), table))
    shape = tokens.shape
    own, *others = pl.pallas_call(
        mix_kernel,
        out_shape=[jax.ShapeDtypeStruct(shape, F32)] + [jax.ShapeDtypeStruct(shape, BF16)] * (BLOCKS - 1),
        compiler_params=params(8),
        cost_estimate=cost(1 << 29, 4 << 20),
    )(table, returned)
    arrived = [send(value, by, True) for by, value in enumerate(others, 1)]
    return pl.pallas_call(
        sum_kernel, out_shape=jax.ShapeDtypeStruct(shape, BF16), compiler_params=params(8)
    )(own, *arrived)


def solution(mesh):
    groups, members = mesh.devices.shape
    fine = Mesh(mesh.devices.reshape(groups // 2, 2, 4, members // 4), AXES)
    rows = P(AXES, None)
    weights = P(("y", "core"), ("x", "z"), None, None)
    return jax.shard_map(
        on_device, mesh=fine, in_specs=(rows, rows, rows, weights, weights, weights), out_specs=rows, check_vma=False
    )
```

time: 133 us -> 119 us (0.89)
  blocking collectives: 116 us -> 57.3 us
  waiting for transfers between devices: 1.22 us -> 26 us
  starting transfers between devices: 0.6 us -> 21.4 us
  local copies, waits for them, and re-layouts: 3.96 us -> 0.93 us
  other arithmetic: 0 us -> 1.45 us
    all_to_all x2, blocking collectives: 116 us -> 57.3 us  [spread(): lax.all_to_all(value, AXES, 0, 0, axis_index_groups=groups, tiled=True)]
    ppermute x0 -> x9, waiting for transfers between devices: none -> 22.2 us  [send(): return lax.ppermute(value, ('core', 'z'), route(by, back))]
    ppermute x0 -> x9, starting transfers between devices: none -> 21.1 us  [send(): return lax.ppermute(value, ('core', 'z'), route(by, back))]
    unnamed x14 -> x8, local copies, waits for them, and re-layouts: 3.96 us -> 0.93 us
    ppermute x2, waiting for transfers between devices: 1.22 us -> 3.78 us  [swap(): return lax.ppermute(value, 'core', [(0, 1), (1, 0)])]
  transfers between devices with their start and end apart: 2 -> 11, of which waited for: 1 -> 6; matrix products, arithmetic and copies ran while one was open for 0% -> 1% of each run, Pallas kernels for 3% -> 4%
where the time goes in v4:
time: 119 us; the launch traced here: 118 us
  blocking collectives  57.3 us (48%)
  waiting for transfers between devices  26 us (22%)
  starting transfers between devices  21.4 us (18%)
  Pallas kernels  11.3 us (9%)
  other arithmetic  1.45 us (1%)
    all_to_all x2, blocking collectives, spread(): lax.all_to_all(value, AXES, 0, 0, axis_index_groups=groups, tiled=True)  57.3 us
    ppermute x9, waiting for transfers between devices, send(): return lax.ppermute(value, ('core', 'z'), route(by, back))  22.2 us
    ppermute x9, starting transfers between devices, send(): return lax.ppermute(value, ('core', 'z'), route(by, back))  21.1 us
    pallas_call x2, Pallas kernels, run_expert(): pl.pallas_call(expert_kernel, in_specs=[VMEM] * 4, out_specs=VMEM, out_sh...  6.03 us
    ppermute x2, waiting for transfers between devices, swap(): return lax.ppermute(value, 'core', [(0, 1), (1, 0)])  3.78 us
  transfers between devices with their start and end apart: 11, of which 6 were waited for; matrix products, arithmetic and copies ran while one was open for 1% of the time, Pallas kernels for 4%

profile of v4, /device:TPU:8, one launch (start us, length us, event | category | flops | bytes accessed | tf_op | source)
XLA Modules:
  0.0 118.5 jit_solution(10031194220920585875)
XLA Ops:
  0.0 3.3 %collective-permute-start.4 = (bf16[20,3584]{1,0:T(8,128)(2,1)}, bf16[20,3584]{1,0:T(8,128)(2,1)S(1)}, u32[]{:S(2)}, u32[]{:S(2)}) collective-permute-start(bf16[20,3584]{1,0:T(8,128)(2,1)} %refs_4_.1), channel_id=1, source_target_pairs={{0,2},{1,7},{2,4},{3,1},{4,6},{5,3},{6,0},{7,5},{33,35},{34,32},{3... | collective-permute-start | bytes 430088 | tf_op jit(solution)/shard_map/ppermute | solution.py:203
  3.3 4.0 %collective-permute-start.3 = (bf16[20,3584]{1,0:T(8,128)(2,1)}, bf16[20,3584]{1,0:T(8,128)(2,1)S(1)}, u32[]{:S(2)}, u32[]{:S(2)}) collective-permute-start(bf16[20,3584]{1,0:T(8,128)(2,1)} %refs_4_.1), channel_id=1, source_target_pairs={{0,7},{1,2},{2,1},{3,4},{4,3},{5,6},{6,5},{7,0},{33,32},{34,35},{3... | collective-permute-start | bytes 430088 | tf_op jit(solution)/shard_map/ppermute | solution.py:203
  7.3 0.5 collective-permute-start.5
  7.8 0.7 convert_bitcast_fusion
  8.5 0.7 pad_maximum_fusion.refs_0_
  9.1 4.6 %collective-permute-start.2 = (f32[16,20]{1,0:T(8,128)S(1)}, f32[16,20]{1,0:T(8,128)S(1)}, u32[]{:S(2)}, u32[]{:S(2)}) collective-permute-start(f32[16,20]{1,0:T(8,128)S(1)} %pad_maximum_fusion.refs_0_), channel_id=1, source_target_pairs={{0,5},{1,4},{2,7},{3,6},{4,1},{5,0},{6,3},{7,2},{33,38},{34,37},{3... | collective-permute-start | bytes 3848 | tf_op jit(solution)/shard_map/ppermute | solution.py:203
  13.7 1.5 %collective-permute-start.1 = (f32[16,20]{1,0:T(8,128)S(1)}, f32[16,20]{1,0:T(8,128)S(1)}, u32[]{:S(2)}, u32[]{:S(2)}) collective-permute-start(f32[16,20]{1,0:T(8,128)S(1)} %pad_maximum_fusion.refs_0_), channel_id=1, source_target_pairs={{0,2},{1,7},{2,4},{3,1},{4,6},{5,3},{6,0},{7,5},{33,35},{34,32},{3... | collective-permute-start | bytes 3848 | tf_op jit(solution)/shard_map/ppermute | solution.py:203
  15.2 5.7 %collective-permute-done.2.refs_3_ = f32[16,20]{1,0:T(8,128)S(1)} collective-permute-done((f32[16,20]{1,0:T(8,128)S(1)}, f32[16,20]{1,0:T(8,128)S(1)}, u32[]{:S(2)}, u32[]{:S(2)}) %collective-permute-start.2) | collective-permute-done | bytes 1312 | tf_op jit(solution)/shard_map/ppermute | solution.py:203
  21.0 4.8 %collective-permute-done.refs_1_ = f32[16,20]{1,0:T(8,128)S(1)} collective-permute-done((f32[16,20]{1,0:T(8,128)S(1)}, f32[16,20]{1,0:T(8,128)S(1)}, u32[]{:S(2)}, u32[]{:S(2)}) %collective-permute-start) | collective-permute-done | bytes 1312 | tf_op jit(solution)/shard_map/ppermute | solution.py:203
  25.8 0.9 copy-done.3
  26.7 1.8 %shard_map.64 = bf16[32,8,3584]{2,1,0:T(8,128)(2,1)S(1)} custom-call(s32[2]{0:T(128)S(1)} %pad_add_fusion.planes_ref, f32[16,20]{1,0:T(8,128)S(1)} %pad_maximum_fusion.refs_0_, f32[16,20]{1,0:T(8,128)S(1)} %collective-permute-done.refs_1_, f32[16,20]{1,0:T(8,128)S(1)} %collective-permute-done.1.refs_2_, f32[16,20]{1,0:T(8,128)S(1)} %collective-permute-done.2.refs_3_, ...), custom_call_target="tpu_custom_call" | custom-call | flops 34359738368 | bytes 4194304 | tf_op jit(solution)/shard_map/pallas_call | solution.py:86
  28.5 29.8 %all_to_all.10.refs_4_.rows_ref = bf16[32,8,3584]{2,1,0:T(8,128)(2,1)S(1)} all-to-all(bf16[32,8,3584]{2,1,0:T(8,128)(2,1)S(1)} %shard_map.64), channel_id=1, replica_groups={{0,64,128,192,1,65,129,193,8,72,136,200,9,73,137,201,16,80,144,208,17,8..., dimensions={0} | all-to-all | bytes 3670016 | tf_op jit(solution)/shard_map/all_to_all | solution.py:217
  58.3 3.8 %collective-permute-done.6.rows_ref = bf16[32,8,3584]{2,1,0:T(8,128)(2,1)S(1)} collective-permute-done((bf16[32,8,3584]{2,1,0:T(8,128)(2,1)S(1)}, bf16[32,8,3584]{2,1,0:T(8,128)(2,1)S(1)}, u32[]{:S(2)}, u32[]{:S(2)}) %collective-permute-start.6) | collective-permute-done | bytes 1835040 | tf_op jit(solution)/shard_map/ppermute | solution.py:220
  62.1 3.0 %shard_map.67 = bf16[32,8,3584]{2,1,0:T(8,128)(2,1)S(1)} custom-call(bf16[32,8,3584]{2,1,0:T(8,128)(2,1)S(1)} %collective-permute-done.6.rows_ref, bf16[3584,512]{1,0:T(8,128)(2,1)S(1)} %bitcast.8, bf16[3584,512]{1,0:T(8,128)(2,1)S(1)} %bitcast.10, bf16[512,3584]{1,0:T(8,128)(2,1)S(1)} %bitcast.12), custom_call_target="tpu_custom_call" | custom-call | flops 2818572288 | bytes 15728640 | tf_op jit(solution)/shard_map/pallas_call | solution.py:174
  65.3 1.5 %shard_map.65.unused_ref.table_ref = bf16[3,128,256]{2,1,0:T(8,128)(2,1)S(1)} custom-call(s32[2]{0:T(128)S(1)} %pad_add_fusion.planes_ref, f32[16,20]{1,0:T(8,128)S(1)} %pad_maximum_fusion.refs_0_, f32[16,20]{1,0:T(8,128)S(1)} %collective-permute-done.refs_1_, f32[16,20]{1,0:T(8,128)S(1)} %collective-permute-done.1.refs_2_, ...), custom_call_target="tpu_custom_call" | custom-call | flops 4194304 | bytes 262144 | tf_op jit(solution)/shard_map/pallas_call | solution.py:112
  66.8 3.0 %shard_map.66.mine_ref = bf16[32,8,3584]{2,1,0:T(8,128)(2,1)S(1)} custom-call(bf16[32,8,3584]{2,1,0:T(8,128)(2,1)S(1)} %all_to_all.10.refs_4_.rows_ref, bf16[3584,512]{1,0:T(8,128)(2,1)S(1)} %bitcast.9, bf16[3584,512]{1,0:T(8,128)(2,1)S(1)} %bitcast.11, bf16[512,3584]{1,0:T(8,128)(2,1)S(1)} %bitcast.13), custom_call_target="tpu_custom_call" | custom-call | flops 2818572288 | bytes 15728640 | tf_op jit(solution)/shard_map/pallas_call | solution.py:174
  70.3 27.5 %all_to_all.11.rows_ref = bf16[32,8,3584]{2,1,0:T(8,128)(2,1)S(1)} all-to-all(bf16[32,8,3584]{2,1,0:T(8,128)(2,1)S(1)} %shard_map.68), channel_id=1, replica_groups={{0,64,128,192,1,65,129,193,8,72,136,200,9,73,137,201,16,80,144,208,17,8..., dimensions={0} | all-to-all | bytes 3670016 | tf_op jit(solution)/shard_map/all_to_all | solution.py:217
  97.7 0.9 shard_map.69
  98.6 4.9 %collective-permute-start.8 = (bf16[20,3584]{1,0:T(8,128)(2,1)S(1)}, bf16[20,3584]{1,0:T(8,128)(2,1)S(1)}, u32[]{:S(2)}, u32[]{:S(2)}) collective-permute-start(bf16[20,3584]{1,0:T(8,128)(2,1)S(1)} %get-tuple-element.10), channel_id=1, source_target_pairs={{7,0},{2,1},{1,2},{4,3},{3,4},{6,5},{5,6},{0,7},{32,33},{35,34},{3... | collective-permute-start | bytes 430088 | tf_op jit(solution)/shard_map/ppermute | solution.py:203
  103.8 2.2 %collective-permute-start.10 = (bf16[20,3584]{1,0:T(8,128)(2,1)S(1)}, bf16[20,3584]{1,0:T(8,128)(2,1)S(1)}, u32[]{:S(2)}, u32[]{:S(2)}) collective-permute-start(bf16[20,3584]{1,0:T(8,128)(2,1)S(1)} %get-tuple-element.12), channel_id=1, source_target_pairs={{5,0},{4,1},{7,2},{6,3},{1,4},{0,5},{3,6},{2,7},{38,33},{37,34},{3... | collective-permute-start | bytes 430088 | tf_op jit(solution)/shard_map/ppermute | solution.py:203
  106.0 2.8 %collective-permute-done.8.refs_0_ = bf16[20,3584]{1,0:T(8,128)(2,1)S(1)} collective-permute-done((bf16[20,3584]{1,0:T(8,128)(2,1)S(1)}, bf16[20,3584]{1,0:T(8,128)(2,1)S(1)}, u32[]{:S(2)}, u32[]{:S(2)}) %collective-permute-start.8) | collective-permute-done | bytes 143392 | tf_op jit(solution)/shard_map/ppermute | solution.py:203
  108.7 2.3 %collective-permute-done.9.refs_1_ = bf16[20,3584]{1,0:T(8,128)(2,1)S(1)} collective-permute-done((bf16[20,3584]{1,0:T(8,128)(2,1)S(1)}, bf16[20,3584]{1,0:T(8,128)(2,1)S(1)}, u32[]{:S(2)}, u32[]{:S(2)}) %collective-permute-start.9) | collective-permute-done | bytes 143392 | tf_op jit(solution)/shard_map/ppermute | solution.py:203
  111.1 6.7 %collective-permute-done.10.refs_2_ = bf16[20,3584]{1,0:T(8,128)(2,1)S(1)} collective-permute-done((bf16[20,3584]{1,0:T(8,128)(2,1)S(1)}, bf16[20,3584]{1,0:T(8,128)(2,1)S(1)}, u32[]{:S(2)}, u32[]{:S(2)}) %collective-permute-start.10) | collective-permute-done | bytes 143392 | tf_op jit(solution)/shard_map/ppermute | solution.py:203
  117.7 0.7 shard_map.70
  (18 shorter events, 1.0 us)
Async XLA Ops:
  0.0 25.7 %collective-permute-start.4 = (bf16[20,3584]{1,0:T(8,128)(2,1)}, bf16[20,3584]{1,0:T(8,128)(2,1)S(1)}, u32[]{:S(2)}, u32[]{:S(2)}) collective-permute-start(bf16[20,3584]{1,0:T(8,128)(2,1)} %refs_4_.1), channel_id=1, source_target_pairs={{0,2},{1,7},{2,4},{3,1},{4,6},{5,3},{6,0},{7,5},{33,35},{34,32},{3... | collective-permute-start | bytes 430088 | tf_op jit(solution)/shard_map/ppermute | solution.py:203
  3.3 22.5 %collective-permute-start.3 = (bf16[20,3584]{1,0:T(8,128)(2,1)}, bf16[20,3584]{1,0:T(8,128)(2,1)S(1)}, u32[]{:S(2)}, u32[]{:S(2)}) collective-permute-start(bf16[20,3584]{1,0:T(8,128)(2,1)} %refs_4_.1), channel_id=1, source_target_pairs={{0,7},{1,2},{2,1},{3,4},{4,3},{5,6},{6,5},{7,0},{33,32},{34,35},{3... | collective-permute-start | bytes 430088 | tf_op jit(solution)/shard_map/ppermute | solution.py:203
  7.3 18.4 %collective-permute-start.5 = (bf16[20,3584]{1,0:T(8,128)(2,1)}, bf16[20,3584]{1,0:T(8,128)(2,1)S(1)}, u32[]{:S(2)}, u32[]{:S(2)}) collective-permute-start(bf16[20,3584]{1,0:T(8,128)(2,1)} %refs_4_.1), channel_id=1, source_target_pairs={{0,5},{1,4},{2,7},{3,6},{4,1},{5,0},{6,3},{7,2},{33,38},{34,37},{3... | collective-permute-start | bytes 430088 | tf_op jit(solution)/shard_map/ppermute | solution.py:203
  9.1 11.7 %collective-permute-start.2 = (f32[16,20]{1,0:T(8,128)S(1)}, f32[16,20]{1,0:T(8,128)S(1)}, u32[]{:S(2)}, u32[]{:S(2)}) collective-permute-start(f32[16,20]{1,0:T(8,128)S(1)} %pad_maximum_fusion.refs_0_), channel_id=1, source_target_pairs={{0,5},{1,4},{2,7},{3,6},{4,1},{5,0},{6,3},{7,2},{33,38},{34,37},{3... | collective-permute-start | bytes 3848 | tf_op jit(solution)/shard_map/ppermute | solution.py:203
  13.7 7.2 %collective-permute-start.1 = (f32[16,20]{1,0:T(8,128)S(1)}, f32[16,20]{1,0:T(8,128)S(1)}, u32[]{:S(2)}, u32[]{:S(2)}) collective-permute-start(f32[16,20]{1,0:T(8,128)S(1)} %pad_maximum_fusion.refs_0_), channel_id=1, source_target_pairs={{0,2},{1,7},{2,4},{3,1},{4,6},{5,3},{6,0},{7,5},{33,35},{34,32},{3... | collective-permute-start | bytes 3848 | tf_op jit(solution)/shard_map/ppermute | solution.py:203
  20.9 4.9 %collective-permute-start = (f32[16,20]{1,0:T(8,128)S(1)}, f32[16,20]{1,0:T(8,128)S(1)}, u32[]{:S(2)}, u32[]{:S(2)}) collective-permute-start(f32[16,20]{1,0:T(8,128)S(1)} %pad_maximum_fusion.refs_0_), channel_id=1, source_target_pairs={{0,7},{1,2},{2,1},{3,4},{4,3},{5,6},{6,5},{7,0},{33,32},{34,35},{3... | collective-permute-start | bytes 3848 | tf_op jit(solution)/shard_map/ppermute | solution.py:203
  25.7 0.9 copy-start.3
  26.7 35.4 %copy-start.1 = (bf16[1,1,3584,512]{3,2,1,0:T(8,128)(2,1)S(1)}, bf16[1,1,3584,512]{3,2,1,0:T(8,128)(2,1)}, u32[]{:S(2)}) copy-start(bf16[1,1,3584,512]{3,2,1,0:T(8,128)(2,1)} %param.10) | copy-start | bytes 11010052
  26.7 35.4 %copy-start.2 = (bf16[1,1,512,3584]{3,2,1,0:T(8,128)(2,1)S(1)}, bf16[1,1,512,3584]{3,2,1,0:T(8,128)(2,1)}, u32[]{:S(2)}) copy-start(bf16[1,1,512,3584]{3,2,1,0:T(8,128)(2,1)} %param.11) | copy-start | bytes 11010052
  28.5 33.6 %copy-start = (bf16[1,1,3584,512]{3,2,1,0:T(8,128)(2,1)S(1)}, bf16[1,1,3584,512]{3,2,1,0:T(8,128)(2,1)}, u32[]{:S(2)}) copy-start(bf16[1,1,3584,512]{3,2,1,0:T(8,128)(2,1)} %param.9) | copy-start | bytes 11010052
  58.3 3.8 %collective-permute-start.6 = (bf16[32,8,3584]{2,1,0:T(8,128)(2,1)S(1)}, bf16[32,8,3584]{2,1,0:T(8,128)(2,1)S(1)}, u32[]{:S(2)}, u32[]{:S(2)}) collective-permute-start(bf16[32,8,3584]{2,1,0:T(8,128)(2,1)S(1)} %all_to_all.10.refs_4_.rows_ref), channel_id=1, source_target_pairs={{0,32},{32,0},{1,33},{33,1},{2,34},{34,2},{3,35},{35,3},{4,36},{36... | collective-permute-start | bytes 5505032 | tf_op jit(solution)/shard_map/ppermute | solution.py:220
  65.1 4.7 %collective-permute-start.7 = (bf16[32,8,3584]{2,1,0:T(8,128)(2,1)S(1)}, bf16[32,8,3584]{2,1,0:T(8,128)(2,1)S(1)}, u32[]{:S(2)}, u32[]{:S(2)}) collective-permute-start(bf16[32,8,3584]{2,1,0:T(8,128)(2,1)S(1)} %shard_map.67), channel_id=1, source_target_pairs={{0,32},{32,0},{1,33},{33,1},{2,34},{34,2},{3,35},{35,3},{4,36},{36... | collective-permute-start | bytes 5505032 | tf_op jit(solution)/shard_map/ppermute | solution.py:220
  98.6 10.1 %collective-permute-start.8 = (bf16[20,3584]{1,0:T(8,128)(2,1)S(1)}, bf16[20,3584]{1,0:T(8,128)(2,1)S(1)}, u32[]{:S(2)}, u32[]{:S(2)}) collective-permute-start(bf16[20,3584]{1,0:T(8,128)(2,1)S(1)} %get-tuple-element.10), channel_id=1, source_target_pairs={{7,0},{2,1},{1,2},{4,3},{3,4},{6,5},{5,6},{0,7},{32,33},{35,34},{3... | collective-permute-start | bytes 430088 | tf_op jit(solution)/shard_map/ppermute | solution.py:203
  103.5 7.6 %collective-permute-start.9 = (bf16[20,3584]{1,0:T(8,128)(2,1)S(1)}, bf16[20,3584]{1,0:T(8,128)(2,1)S(1)}, u32[]{:S(2)}, u32[]{:S(2)}) collective-permute-start(bf16[20,3584]{1,0:T(8,128)(2,1)S(1)} %get-tuple-element.11), channel_id=1, source_target_pairs={{2,0},{7,1},{4,2},{1,3},{6,4},{3,5},{0,6},{5,7},{35,33},{32,34},{3... | collective-permute-start | bytes 430088 | tf_op jit(solution)/shard_map/ppermute | solution.py:203
  103.8 14.0 %collective-permute-start.10 = (bf16[20,3584]{1,0:T(8,128)(2,1)S(1)}, bf16[20,3584]{1,0:T(8,128)(2,1)S(1)}, u32[]{:S(2)}, u32[]{:S(2)}) collective-permute-start(bf16[20,3584]{1,0:T(8,128)(2,1)S(1)} %get-tuple-element.12), channel_id=1, source_target_pairs={{5,0},{4,1},{7,2},{6,3},{1,4},{0,5},{3,6},{2,7},{38,33},{37,34},{3... | collective-permute-start | bytes 430088 | tf_op jit(solution)/shard_map/ppermute | solution.py:203

commit v5 on v4

--- a/solution.py
+++ b/solution.py
@@ -17,6 +17,7 @@
 SMEM = pl.BlockSpec(memory_space=pltpu.SMEM)
 ANY = pl.BlockSpec(memory_space=pl.ANY)
 PICK_MIB = 12
+PREPARE_MIB = 8
 FFN_MIB = 28
 
 
@@ -41,8 +42,8 @@
     lane = lax.broadcasted_iota(jnp.int32, (size, lanes), 1)
     row = lax.broadcasted_iota(jnp.int32, (size, lanes), 0)
     device = lane // (BLOCKS * SLOTS)
-    plane = jnp.where(device // 4 % 2 == 0, planes_ref[0], planes_ref[1])
-    expert = (device % 4 * 32 + device // 8 * 8 + plane).astype(F32)
+    plane = jnp.where(device // 1 % 2 == 0, planes_ref[0], planes_ref[1])
+    expert = (device // 2 % 4 * 32 + device // 8 % 4 * 8 + plane).astype(F32)
     fits = (row // STRIDE == lane // SLOTS % BLOCKS) & (row % STRIDE < tokens)
     named = [(info[:, k : k + 1] == expert) & fits for k in range(top)]
     hits = functools.reduce(jnp.logical_or, named)
@@ -53,7 +54,7 @@
     return named, hits, rank == (lane % SLOTS).astype(F32)
 
 
-def gather_info(infos, scratch):
+def gather_info(infos, scratch, terms):
     scratch[...] = jnp.zeros_like(scratch)
     for b, ref in enumerate(infos):
         value = ref[...]
@@ -61,62 +62,83 @@
         rest = value - high.astype(F32)
         mid = rest.astype(BF16)
         low = (rest - mid.astype(F32)).astype(BF16)
-        for place, piece in enumerate((high, mid, low)):
+        for place, piece in enumerate((high, mid, low)[:terms]):
             scratch[place, b * STRIDE : b * STRIDE + value.shape[1]] = upright(piece)
 
 
-def pick_kernel(planes_ref, *refs):
-    infos, blocks, (out_ref, info, table) = refs[:BLOCKS], refs[BLOCKS : 2 * BLOCKS], refs[2 * BLOCKS :]
+def prepare_kernel(ids_ref, weights_ref, tokens_ref, info_ref, own_ref):
+    top = ids_ref.shape[0]
+    info_ref[:top] = ids_ref[...].astype(F32)
+    info_ref[top:] = weights_ref[...]
+    own_ref[...] = tokens_ref[...]
+
+
+def prepare(ids, weights, tokens):
+    return pl.pallas_call(
+        prepare_kernel,
+        out_shape=[
+            jax.ShapeDtypeStruct((2 * ids.shape[0], ids.shape[1]), F32),
+            jax.ShapeDtypeStruct(tokens.shape, BF16),
+        ],
+        compiler_params=params(PREPARE_MIB),
+        cost_estimate=cost(0, 1 << 18),
+    )(ids, weights, tokens)
+
+
+def choose_kernel(planes_ref, *refs):
+    infos, (chosen_ref, info) = refs[:BLOCKS], refs[BLOCKS:]
+    gather_info(infos, info, 1)
+    unused, hits, here = slot_parts(info[0], planes_ref, chosen_ref.shape[1], infos[0].shape[1])
+    chosen_ref[...] = (hits & here).astype(F32).astype(BF16)
+
+
+def table_kernel(planes_ref, *refs):
+    infos, (table_ref, info) = refs[:BLOCKS], refs[BLOCKS + 1 :]
+    gather_info(infos, info, 3)
+    named, unused, here = slot_parts(info[0], planes_ref, table_ref.shape[2], infos[0].shape[1])
+    top = len(named)
+    for place in range(3):
+        value = jnp.zeros(here.shape, F32)
+        for k, hit in enumerate(named):
+            value = value + jnp.where(hit & here, info[place, :, top + k : top + k + 1], 0.0)
+        table_ref[place] = value.astype(BF16)
+
+
+def from_info(kernel, terms, lead, planes, infos, devices, after=()):
+    return pl.pallas_call(
+        kernel,
+        in_specs=[SMEM] + [VMEM] * BLOCKS + [ANY] * len(after),
+        out_shape=jax.ShapeDtypeStruct((*lead, BLOCKS * STRIDE, devices * BLOCKS * SLOTS), BF16),
+        scratch_shapes=[pltpu.VMEM((terms, BLOCKS * STRIDE, infos[0].shape[0]), F32)],
+        compiler_params=params(8),
+        cost_estimate=cost(1 << 22, 1 << 18),
+    )(planes, *infos, *after)
+
+
+def pick_kernel(chosen_ref, *refs):
+    blocks, (out_ref, table) = refs[:BLOCKS], refs[BLOCKS:]
     tokens = blocks[0].shape[0]
     devices, each, features = out_ref.shape
     table[...] = jnp.zeros_like(table)
     for b, block in enumerate(blocks):
         table[b * STRIDE : b * STRIDE + tokens] = block[...]
-    gather_info(infos, info)
-    unused, hits, here = slot_parts(info[0], planes_ref, devices * each, tokens)
-    chosen = (hits & here).astype(F32).astype(BF16)
     for at in range(0, features, CUT):
         cols = slice(at, at + CUT)
-        rows = lax.dot_general(chosen, table[:, cols], (((0,), (0,)), ((), ())), preferred_element_type=F32)
+        rows = lax.dot_general(
+            chosen_ref[...], table[:, cols], (((0,), (0,)), ((), ())), preferred_element_type=F32
+        )
         out_ref[:, :, cols] = rows.astype(BF16).reshape(devices, each, CUT)
 
 
-def pick(planes, infos, blocks, devices):
-    tokens, features = blocks[0].shape
+def pick(chosen, blocks, devices):
+    features = blocks[0].shape[1]
     return pl.pallas_call(
         pick_kernel,
-        in_specs=[SMEM] + [VMEM] * (2 * BLOCKS),
         out_shape=jax.ShapeDtypeStruct((devices, BLOCKS * SLOTS, features), BF16),
-        scratch_shapes=[
-            pltpu.VMEM((3, BLOCKS * STRIDE, infos[0].shape[0]), F32),
-            pltpu.VMEM((BLOCKS * STRIDE, features), BF16),
-        ],
+        scratch_shapes=[pltpu.VMEM((BLOCKS * STRIDE, features), BF16)],
         compiler_params=params(PICK_MIB),
         cost_estimate=cost(1 << 35, 4 << 20),
-    )(planes, *infos, *blocks)
-
-
-def table_kernel(planes_ref, *refs):
-    infos, (out_ref, info) = refs[:BLOCKS], refs[BLOCKS + 1 :]
-    gather_info(infos, info)
-    named, unused, here = slot_parts(info[0], planes_ref, out_ref.shape[2], infos[0].shape[1])
-    top = len(named)
-    for place in range(3):
-        value = jnp.zeros(here.shape, F32)
-        for k, hit in enumerate(named):
-            value = value + jnp.where(hit & here, info[place, :, top + k : top + k + 1], 0.0)
-        out_ref[place] = value.astype(BF16)
-
-
-def make_table(planes, infos, devices, after):
-    return pl.pallas_call(
-        table_kernel,
-        in_specs=[SMEM] + [VMEM] * BLOCKS + [ANY],
-        out_shape=jax.ShapeDtypeStruct((3, BLOCKS * STRIDE, devices * BLOCKS * SLOTS), BF16),
-        scratch_shapes=[pltpu.VMEM((3, BLOCKS * STRIDE, infos[0].shape[0]), F32)],
-        compiler_params=params(8),
-        cost_estimate=cost(1 << 22, 1 << 18),
-    )(planes, *infos, after)
+    )(chosen, *blocks)
 
 
 def mix_kernel(table_ref, rows_ref, *outs):
@@ -137,23 +159,23 @@
     refs[-1][...] = total.astype(BF16)
 
 
-def join_kernel(mine_ref, other_ref, unused_ref, out):
+def join_kernel(mine_ref, other_ref, out):
     for at in range(0, out.shape[2], CUT):
         parts = [ref[:, :, at : at + CUT].reshape(-1, CUT).astype(F32) for ref in (mine_ref, other_ref)]
         out[:, :, at : at + CUT] = (parts[0] + parts[1]).astype(BF16).reshape(*out.shape[:2], CUT)
 
 
-def join(mine, other, after):
+def join(mine, other):
     return pl.pallas_call(
         join_kernel,
-        in_specs=[VMEM] * 2 + [ANY],
         out_shape=jax.ShapeDtypeStruct(mine.shape, BF16),
         compiler_params=params(8),
         cost_estimate=cost(1 << 20, 3 << 20),
-    )(mine, other, after)
-
-
-def expert_kernel(rows_ref, gate, up, down, out_ref, rows, hidden):
+    )(mine, other)
+
+
+def expert_kernel(rows_ref, gate, up, down, *refs):
+    out_ref, rows, hidden = refs[-3:]
     count, features = rows.shape
     units = hidden.shape[1]
     rows[...] = rows_ref[...].reshape(count, features)
@@ -168,12 +190,12 @@
         out_ref[:, :, cols] = part.reshape(*out_ref.shape[:2], 256)
 
 
-def run_expert(rows, gate, up, down):
+def run_expert(rows, gate, up, down, after=()):
     features, units = gate.shape
     count = rows.size // features
     return pl.pallas_call(
         expert_kernel,
-        in_specs=[VMEM] * 4,
+        in_specs=[VMEM] * 4 + [ANY] * len(after),
         out_specs=VMEM,
         out_shape=jax.ShapeDtypeStruct(rows.shape, BF16),
         scratch_shapes=[pltpu.VMEM((count, features), BF16), pltpu.VMEM((count, units), BF16)],
@@ -181,7 +203,7 @@
         cost_estimate=pl.CostEstimate(
             flops=6 * count * features * units, bytes_accessed=15 << 20, transcendentals=count * units
         ),
-    )(rows, gate, up, down)
+    )(rows, gate, up, down, *after)
 
 
 def on_device(tokens, expert_ids, route_weights, w_gate, w_up, w_down):
@@ -206,8 +228,8 @@
         [
             ((y * 2 + c) * depth + x) * ring + (2 * p + member + c) % ring
             for x in range(depth)
+            for y in range(width)
             for member in range(2)
-            for y in range(width)
         ]
         for c in range(2)
         for p in range(ring // 2)
@@ -219,17 +241,18 @@
     def swap(value):
         return lax.ppermute(value, "core", [(0, 1), (1, 0)])
 
-    info = jnp.concatenate([expert_ids.T.astype(F32), route_weights.T], axis=0)
+    info, own = prepare(expert_ids.T, route_weights.T, tokens)
     blocks, infos = [tokens], [info]
     blocks += [send(tokens, by) for by in range(1, BLOCKS)]
     infos += [send(info, by) for by in range(1, BLOCKS)]
     devices = 2 * depth * width
-    mine = spread(pick(planes, infos, blocks, devices))
+    chosen = from_info(choose_kernel, 1, (), planes, infos, devices)
+    mine = spread(pick(chosen, [own] + blocks[1:], devices))
     peer = swap(mine)
-    table = make_table(planes, infos, devices, mine)
+    table = from_info(table_kernel, 3, (3,), planes, infos, devices, [mine])
     mine_part = run_expert(mine, *matrices)
-    peer_part = run_expert(peer, *matrices)
-    returned = spread(join(mine_part, swap(peer_part), table))
+    peer_part = run_expert(peer, *matrices, [table])
+    returned = spread(join(mine_part, swap(peer_part)))
     shape = tokens.shape
     own, *others = pl.pallas_call(
         mix_kernel,

time: 119 us -> 113 us (0.950)
  waiting for transfers between devices: 26 us -> 19.6 us
  local copies, waits for them, and re-layouts: 0.93 us -> 2.34 us
  other arithmetic: 1.45 us -> 0.07 us
    ppermute x9, waiting for transfers between devices: 22.2 us -> 16.7 us  [send(): return lax.ppermute(value, ('core', 'z'), route(by, back))]
    unnamed x8 -> x12, local copies, waits for them, and re-layouts: 0.93 us -> 2.34 us
    pallas_call x5 -> x7, Pallas kernels: 9.7 us -> 9.73 us  [the longest x2 6.02 us: run_expert(): pl.pallas_call(expert_kernel, in_specs=[VMEM] * 4 + [ANY] * len(after), o...]
  transfers between devices with their start and end apart: 11 -> 11, of which waited for: 6 -> 7; matrix products, arithmetic and copies ran while one was open for 1% -> 0% of each run, Pallas kernels for 4% -> 5%
where the time goes in v5:
time: 113 us; the launch traced here: 112 us
  blocking collectives  56.5 us (50%)
  starting transfers between devices  21.7 us (19%)
  waiting for transfers between devices  19.6 us (17%)
  Pallas kernels  11.4 us (10%)
  local copies, waits for them, and re-layouts  2.34 us (2%)
    all_to_all x2, blocking collectives, spread(): lax.all_to_all(value, AXES, 0, 0, axis_index_groups=groups, tiled=True)  56.5 us
    ppermute x9, starting transfers between devices, send(): return lax.ppermute(value, ('core', 'z'), route(by, back))  21.4 us
    ppermute x9, waiting for transfers between devices, send(): return lax.ppermute(value, ('core', 'z'), route(by, back))  16.7 us
    pallas_call x2, Pallas kernels, run_expert(): pl.pallas_call(expert_kernel, in_specs=[VMEM] * 4 + [ANY] * len(after), o...  6.02 us
    ppermute x2, waiting for transfers between devices, swap(): return lax.ppermute(value, 'core', [(0, 1), (1, 0)])  2.95 us
    pallas_call x2, Pallas kernels, from_info(): pl.pallas_call(kernel, in_specs=[SMEM] + [VMEM] * BLOCKS + [ANY] * len(af...  2.61 us
    unnamed x12, local copies, waits for them, and re-layouts  2.34 us
  transfers between devices with their start and end apart: 11, of which 7 were waited for; matrix products, arithmetic and copies ran while one was open for 0% of the time, Pallas kernels for 5%

profile of v5, /device:TPU:8, one launch (start us, length us, event | category | flops | bytes accessed | tf_op | source)
XLA Modules:
  0.0 111.7 jit_solution(18223880410192196954)
XLA Ops:
  0.0 5.9 %collective-permute-start.3 = (bf16[20,3584]{1,0:T(8,128)(2,1)}, bf16[20,3584]{1,0:T(8,128)(2,1)S(1)}, u32[]{:S(2)}, u32[]{:S(2)}) collective-permute-start(bf16[20,3584]{1,0:T(8,128)(2,1)} %tokens_ref.1), channel_id=1, source_target_pairs={{0,7},{1,2},{2,1},{3,4},{4,3},{5,6},{6,5},{7,0},{33,32},{34,35},{3... | collective-permute-start | bytes 430088 | tf_op jit(solution)/shard_map/ppermute | solution.py:225
  5.9 1.9 %collective-permute-start.5 = (bf16[20,3584]{1,0:T(8,128)(2,1)}, bf16[20,3584]{1,0:T(8,128)(2,1)S(1)}, u32[]{:S(2)}, u32[]{:S(2)}) collective-permute-start(bf16[20,3584]{1,0:T(8,128)(2,1)} %tokens_ref.1), channel_id=1, source_target_pairs={{0,5},{1,4},{2,7},{3,6},{4,1},{5,0},{6,3},{7,2},{33,38},{34,37},{3... | collective-permute-start | bytes 430088 | tf_op jit(solution)/shard_map/ppermute | solution.py:225
  8.2 0.9 copy-done.3
  9.2 0.7 copy-done.4
  9.9 0.7 copy-done.5
  10.6 4.2 %collective-permute-start.2 = (f32[16,20]{1,0:T(8,128)S(1)}, f32[16,20]{1,0:T(8,128)S(1)}, u32[]{:S(2)}, u32[]{:S(2)}) collective-permute-start(f32[16,20]{1,0:T(8,128)S(1)} %get-tuple-element.11.refs_0_), channel_id=1, source_target_pairs={{0,5},{1,4},{2,7},{3,6},{4,1},{5,0},{6,3},{7,2},{33,38},{34,37},{3... | collective-permute-start | bytes 3848 | tf_op jit(solution)/shard_map/ppermute | solution.py:225
  14.8 1.5 %collective-permute-start.1 = (f32[16,20]{1,0:T(8,128)S(1)}, f32[16,20]{1,0:T(8,128)S(1)}, u32[]{:S(2)}, u32[]{:S(2)}) collective-permute-start(f32[16,20]{1,0:T(8,128)S(1)} %get-tuple-element.11.refs_0_), channel_id=1, source_target_pairs={{0,2},{1,7},{2,4},{3,1},{4,6},{5,3},{6,0},{7,5},{33,35},{34,32},{3... | collective-permute-start | bytes 3848 | tf_op jit(solution)/shard_map/ppermute | solution.py:225
  16.3 2.8 %collective-permute-done.2.refs_3_ = f32[16,20]{1,0:T(8,128)S(1)} collective-permute-done((f32[16,20]{1,0:T(8,128)S(1)}, f32[16,20]{1,0:T(8,128)S(1)}, u32[]{:S(2)}, u32[]{:S(2)}) %collective-permute-start.2) | collective-permute-done | bytes 1312 | tf_op jit(solution)/shard_map/ppermute | solution.py:225
  19.0 1.9 %collective-permute-start = (f32[16,20]{1,0:T(8,128)S(1)}, f32[16,20]{1,0:T(8,128)S(1)}, u32[]{:S(2)}, u32[]{:S(2)}) collective-permute-start(f32[16,20]{1,0:T(8,128)S(1)} %get-tuple-element.11.refs_0_), channel_id=1, source_target_pairs={{0,7},{1,2},{2,1},{3,4},{4,3},{5,6},{6,5},{7,0},{33,32},{34,35},{3... | collective-permute-start | bytes 3848 | tf_op jit(solution)/shard_map/ppermute | solution.py:225
  20.9 2.9 %collective-permute-done.refs_1_ = f32[16,20]{1,0:T(8,128)S(1)} collective-permute-done((f32[16,20]{1,0:T(8,128)S(1)}, f32[16,20]{1,0:T(8,128)S(1)}, u32[]{:S(2)}, u32[]{:S(2)}) %collective-permute-start) | collective-permute-done | bytes 1312 | tf_op jit(solution)/shard_map/ppermute | solution.py:225
  23.9 1.1 %shard_map.65.chosen_ref = bf16[128,256]{1,0:T(8,128)(2,1)S(1)} custom-call(s32[2]{0:T(128)S(1)} %pad_add_fusion.planes_ref, f32[16,20]{1,0:T(8,128)S(1)} %get-tuple-element.11.refs_0_, f32[16,20]{1,0:T(8,128)S(1)} %collective-permute-done.refs_1_, f32[16,20]{1,0:T(8,128)S(1)} %collective-permute-done.1.refs_2_, f32[16,20]{1,0:T(8,128)S(1)} %collective-permute-done.2.refs_3_), custom_call_target="tpu_custom_call" | custom-call | flops 4194304 | bytes 262144 | tf_op jit(solution)/shard_map/pallas_call | solution.py:108
  25.8 28.3 %all_to_all.10.refs_4_.rows_ref = bf16[32,8,3584]{2,1,0:T(8,128)(2,1)S(1)} all-to-all(bf16[32,8,3584]{2,1,0:T(8,128)(2,1)S(1)} %shard_map.66), channel_id=1, replica_groups={{0,1,64,65,128,129,192,193,8,9,72,73,136,137,200,201,16,17,80,81,144,14..., dimensions={0} | all-to-all | bytes 3670016 | tf_op jit(solution)/shard_map/all_to_all | solution.py:239
  54.1 1.5 %shard_map.67.refs_0_.table_ref = bf16[3,128,256]{2,1,0:T(8,128)(2,1)S(1)} custom-call(s32[2]{0:T(128)S(1)} %pad_add_fusion.planes_ref, f32[16,20]{1,0:T(8,128)S(1)} %get-tuple-element.11.refs_0_, f32[16,20]{1,0:T(8,128)S(1)} %collective-permute-done.refs_1_, f32[16,20]{1,0:T(8,128)S(1)} %collective-permute-done.1.refs_2_, ...), custom_call_target="tpu_custom_call" | custom-call | flops 4194304 | bytes 262144 | tf_op jit(solution)/shard_map/pallas_call | solution.py:108
  55.5 2.3 %collective-permute-done.6.rows_ref = bf16[32,8,3584]{2,1,0:T(8,128)(2,1)S(1)} collective-permute-done((bf16[32,8,3584]{2,1,0:T(8,128)(2,1)S(1)}, bf16[32,8,3584]{2,1,0:T(8,128)(2,1)S(1)}, u32[]{:S(2)}, u32[]{:S(2)}) %collective-permute-start.6) | collective-permute-done | bytes 1835040 | tf_op jit(solution)/shard_map/ppermute | solution.py:242
  57.9 3.0 %shard_map.69 = bf16[32,8,3584]{2,1,0:T(8,128)(2,1)S(1)} custom-call(bf16[32,8,3584]{2,1,0:T(8,128)(2,1)S(1)} %collective-permute-done.6.rows_ref, bf16[3584,512]{1,0:T(8,128)(2,1)S(1)} %bitcast.7, bf16[3584,512]{1,0:T(8,128)(2,1)S(1)} %bitcast.9, bf16[512,3584]{1,0:T(8,128)(2,1)S(1)} %bitcast.11, bf16[3,128,256]{2,1,0:T(8,128)(2,1)S(1)} %shard_map.67.refs_0_.table_ref), custom_call_target="tpu_custom_call" | custom-call | flops 2818572288 | bytes 15728640 | tf_op jit(solution)/shard_map/pallas_call | solution.py:196
  61.1 3.0 %shard_map.68.mine_ref = bf16[32,8,3584]{2,1,0:T(8,128)(2,1)S(1)} custom-call(bf16[32,8,3584]{2,1,0:T(8,128)(2,1)S(1)} %all_to_all.10.refs_4_.rows_ref, bf16[3584,512]{1,0:T(8,128)(2,1)S(1)} %bitcast.8, bf16[3584,512]{1,0:T(8,128)(2,1)S(1)} %bitcast.10, bf16[512,3584]{1,0:T(8,128)(2,1)S(1)} %bitcast.12), custom_call_target="tpu_custom_call" | custom-call | flops 2818572288 | bytes 15728640 | tf_op jit(solution)/shard_map/pallas_call | solution.py:196
  65.2 28.2 %all_to_all.11.rows_ref = bf16[32,8,3584]{2,1,0:T(8,128)(2,1)S(1)} all-to-all(bf16[32,8,3584]{2,1,0:T(8,128)(2,1)S(1)} %shard_map.70), channel_id=1, replica_groups={{0,1,64,65,128,129,192,193,8,9,72,73,136,137,200,201,16,17,80,81,144,14..., dimensions={0} | all-to-all | bytes 3670016 | tf_op jit(solution)/shard_map/all_to_all | solution.py:239
  93.3 0.9 shard_map.71
  94.2 3.1 %collective-permute-start.8 = (bf16[20,3584]{1,0:T(8,128)(2,1)S(1)}, bf16[20,3584]{1,0:T(8,128)(2,1)S(1)}, u32[]{:S(2)}, u32[]{:S(2)}) collective-permute-start(bf16[20,3584]{1,0:T(8,128)(2,1)S(1)} %get-tuple-element.14), channel_id=1, source_target_pairs={{7,0},{2,1},{1,2},{4,3},{3,4},{6,5},{5,6},{0,7},{32,33},{35,34},{3... | collective-permute-start | bytes 430088 | tf_op jit(solution)/shard_map/ppermute | solution.py:225
  97.3 2.1 %collective-permute-start.9 = (bf16[20,3584]{1,0:T(8,128)(2,1)S(1)}, bf16[20,3584]{1,0:T(8,128)(2,1)S(1)}, u32[]{:S(2)}, u32[]{:S(2)}) collective-permute-start(bf16[20,3584]{1,0:T(8,128)(2,1)S(1)} %get-tuple-element.15), channel_id=1, source_target_pairs={{2,0},{7,1},{4,2},{1,3},{6,4},{3,5},{0,6},{5,7},{35,33},{32,34},{3... | collective-permute-start | bytes 430088 | tf_op jit(solution)/shard_map/ppermute | solution.py:225
  99.9 1.9 %collective-permute-done.8.refs_0_ = bf16[20,3584]{1,0:T(8,128)(2,1)S(1)} collective-permute-done((bf16[20,3584]{1,0:T(8,128)(2,1)S(1)}, bf16[20,3584]{1,0:T(8,128)(2,1)S(1)}, u32[]{:S(2)}, u32[]{:S(2)}) %collective-permute-start.8) | collective-permute-done | bytes 143392 | tf_op jit(solution)/shard_map/ppermute | solution.py:225
  101.8 4.0 %collective-permute-done.9.refs_1_ = bf16[20,3584]{1,0:T(8,128)(2,1)S(1)} collective-permute-done((bf16[20,3584]{1,0:T(8,128)(2,1)S(1)}, bf16[20,3584]{1,0:T(8,128)(2,1)S(1)}, u32[]{:S(2)}, u32[]{:S(2)}) %collective-permute-start.9) | collective-permute-done | bytes 143392 | tf_op jit(solution)/shard_map/ppermute | solution.py:225
  105.8 5.1 %collective-permute-done.10.refs_2_ = bf16[20,3584]{1,0:T(8,128)(2,1)S(1)} collective-permute-done((bf16[20,3584]{1,0:T(8,128)(2,1)S(1)}, bf16[20,3584]{1,0:T(8,128)(2,1)S(1)}, u32[]{:S(2)}, u32[]{:S(2)}) %collective-permute-start.10) | collective-permute-done | bytes 143392 | tf_op jit(solution)/shard_map/ppermute | solution.py:225
  110.9 0.7 shard_map.72
  (22 shorter events, 3.0 us)
Async XLA Ops:
  0.0 25.0 %collective-permute-start.3 = (bf16[20,3584]{1,0:T(8,128)(2,1)}, bf16[20,3584]{1,0:T(8,128)(2,1)S(1)}, u32[]{:S(2)}, u32[]{:S(2)}) collective-permute-start(bf16[20,3584]{1,0:T(8,128)(2,1)} %tokens_ref.1), channel_id=1, source_target_pairs={{0,7},{1,2},{2,1},{3,4},{4,3},{5,6},{6,5},{7,0},{33,32},{34,35},{3... | collective-permute-start | bytes 430088 | tf_op jit(solution)/shard_map/ppermute | solution.py:225
  5.9 19.2 %collective-permute-start.5 = (bf16[20,3584]{1,0:T(8,128)(2,1)}, bf16[20,3584]{1,0:T(8,128)(2,1)S(1)}, u32[]{:S(2)}, u32[]{:S(2)}) collective-permute-start(bf16[20,3584]{1,0:T(8,128)(2,1)} %tokens_ref.1), channel_id=1, source_target_pairs={{0,5},{1,4},{2,7},{3,6},{4,1},{5,0},{6,3},{7,2},{33,38},{34,37},{3... | collective-permute-start | bytes 430088 | tf_op jit(solution)/shard_map/ppermute | solution.py:225
  7.8 17.3 %collective-permute-start.4 = (bf16[20,3584]{1,0:T(8,128)(2,1)}, bf16[20,3584]{1,0:T(8,128)(2,1)S(1)}, u32[]{:S(2)}, u32[]{:S(2)}) collective-permute-start(bf16[20,3584]{1,0:T(8,128)(2,1)} %tokens_ref.1), channel_id=1, source_target_pairs={{0,2},{1,7},{2,4},{3,1},{4,6},{5,3},{6,0},{7,5},{33,35},{34,32},{3... | collective-permute-start | bytes 430088 | tf_op jit(solution)/shard_map/ppermute | solution.py:225
  8.2 1.0 copy-start.3
  9.2 0.7 copy-start.4
  9.9 0.7 copy-start.5
  10.6 8.4 %collective-permute-start.2 = (f32[16,20]{1,0:T(8,128)S(1)}, f32[16,20]{1,0:T(8,128)S(1)}, u32[]{:S(2)}, u32[]{:S(2)}) collective-permute-start(f32[16,20]{1,0:T(8,128)S(1)} %get-tuple-element.11.refs_0_), channel_id=1, source_target_pairs={{0,5},{1,4},{2,7},{3,6},{4,1},{5,0},{6,3},{7,2},{33,38},{34,37},{3... | collective-permute-start | bytes 3848 | tf_op jit(solution)/shard_map/ppermute | solution.py:225
  14.8 6.2 %collective-permute-start.1 = (f32[16,20]{1,0:T(8,128)S(1)}, f32[16,20]{1,0:T(8,128)S(1)}, u32[]{:S(2)}, u32[]{:S(2)}) collective-permute-start(f32[16,20]{1,0:T(8,128)S(1)} %get-tuple-element.11.refs_0_), channel_id=1, source_target_pairs={{0,2},{1,7},{2,4},{3,1},{4,6},{5,3},{6,0},{7,5},{33,35},{34,32},{3... | collective-permute-start | bytes 3848 | tf_op jit(solution)/shard_map/ppermute | solution.py:225
  19.0 4.9 %collective-permute-start = (f32[16,20]{1,0:T(8,128)S(1)}, f32[16,20]{1,0:T(8,128)S(1)}, u32[]{:S(2)}, u32[]{:S(2)}) collective-permute-start(f32[16,20]{1,0:T(8,128)S(1)} %get-tuple-element.11.refs_0_), channel_id=1, source_target_pairs={{0,7},{1,2},{2,1},{3,4},{4,3},{5,6},{6,5},{7,0},{33,32},{34,35},{3... | collective-permute-start | bytes 3848 | tf_op jit(solution)/shard_map/ppermute | solution.py:225
  25.1 32.8 %copy-start.1 = (bf16[1,1,3584,512]{3,2,1,0:T(8,128)(2,1)S(1)}, bf16[1,1,3584,512]{3,2,1,0:T(8,128)(2,1)}, u32[]{:S(2)}) copy-start(bf16[1,1,3584,512]{3,2,1,0:T(8,128)(2,1)} %param.10) | copy-start | bytes 11010052
  25.1 32.8 %copy-start.2 = (bf16[1,1,512,3584]{3,2,1,0:T(8,128)(2,1)S(1)}, bf16[1,1,512,3584]{3,2,1,0:T(8,128)(2,1)}, u32[]{:S(2)}) copy-start(bf16[1,1,512,3584]{3,2,1,0:T(8,128)(2,1)} %param.11) | copy-start | bytes 11010052
  25.8 32.1 %copy-start = (bf16[1,1,3584,512]{3,2,1,0:T(8,128)(2,1)S(1)}, bf16[1,1,3584,512]{3,2,1,0:T(8,128)(2,1)}, u32[]{:S(2)}) copy-start(bf16[1,1,3584,512]{3,2,1,0:T(8,128)(2,1)} %param.9) | copy-start | bytes 11010052
  54.1 3.8 %collective-permute-start.6 = (bf16[32,8,3584]{2,1,0:T(8,128)(2,1)S(1)}, bf16[32,8,3584]{2,1,0:T(8,128)(2,1)S(1)}, u32[]{:S(2)}, u32[]{:S(2)}) collective-permute-start(bf16[32,8,3584]{2,1,0:T(8,128)(2,1)S(1)} %all_to_all.10.refs_4_.rows_ref), channel_id=1, source_target_pairs={{0,32},{32,0},{1,33},{33,1},{2,34},{34,2},{3,35},{35,3},{4,36},{36... | collective-permute-start | bytes 5505032 | tf_op jit(solution)/shard_map/ppermute | solution.py:242
  60.9 3.9 %collective-permute-start.7 = (bf16[32,8,3584]{2,1,0:T(8,128)(2,1)S(1)}, bf16[32,8,3584]{2,1,0:T(8,128)(2,1)S(1)}, u32[]{:S(2)}, u32[]{:S(2)}) collective-permute-start(bf16[32,8,3584]{2,1,0:T(8,128)(2,1)S(1)} %shard_map.69), channel_id=1, source_target_pairs={{0,32},{32,0},{1,33},{33,1},{2,34},{34,2},{3,35},{35,3},{4,36},{36... | collective-permute-start | bytes 5505032 | tf_op jit(solution)/shard_map/ppermute | solution.py:242
  94.2 7.6 %collective-permute-start.8 = (bf16[20,3584]{1,0:T(8,128)(2,1)S(1)}, bf16[20,3584]{1,0:T(8,128)(2,1)S(1)}, u32[]{:S(2)}, u32[]{:S(2)}) collective-permute-start(bf16[20,3584]{1,0:T(8,128)(2,1)S(1)} %get-tuple-element.14), channel_id=1, source_target_pairs={{7,0},{2,1},{1,2},{4,3},{3,4},{6,5},{5,6},{0,7},{32,33},{35,34},{3... | collective-permute-start | bytes 430088 | tf_op jit(solution)/shard_map/ppermute | solution.py:225
  97.3 8.5 %collective-permute-start.9 = (bf16[20,3584]{1,0:T(8,128)(2,1)S(1)}, bf16[20,3584]{1,0:T(8,128)(2,1)S(1)}, u32[]{:S(2)}, u32[]{:S(2)}) collective-permute-start(bf16[20,3584]{1,0:T(8,128)(2,1)S(1)} %get-tuple-element.15), channel_id=1, source_target_pairs={{2,0},{7,1},{4,2},{1,3},{6,4},{3,5},{0,6},{5,7},{35,33},{32,34},{3... | collective-permute-start | bytes 430088 | tf_op jit(solution)/shard_map/ppermute | solution.py:225
  99.4 11.5 %collective-permute-start.10 = (bf16[20,3584]{1,0:T(8,128)(2,1)S(1)}, bf16[20,3584]{1,0:T(8,128)(2,1)S(1)}, u32[]{:S(2)}, u32[]{:S(2)}) collective-permute-start(bf16[20,3584]{1,0:T(8,128)(2,1)S(1)} %get-tuple-element.16), channel_id=1, source_target_pairs={{5,0},{4,1},{7,2},{6,3},{1,4},{0,5},{3,6},{2,7},{38,33},{37,34},{3... | collective-permute-start | bytes 430088 | tf_op jit(solution)/shard_map/ppermute | solution.py:225

commit v6 on v5

--- a/solution.py
+++ b/solution.py
@@ -11,6 +11,7 @@
 SLOTS = 2
 AXES = ("y", "core", "x", "z")
 BLOCKS = 4
+INFOS = 3
 CUT = 512
 STRIDE = 32
 VMEM = pl.BlockSpec(memory_space=pltpu.VMEM)
@@ -56,8 +57,8 @@
 
 def gather_info(infos, scratch, terms):
     scratch[...] = jnp.zeros_like(scratch)
-    for b, ref in enumerate(infos):
-        value = ref[...]
+    size = infos[0].shape[0]
+    for b, value in enumerate((infos[0][...], infos[1][...], infos[2][:size], infos[2][size:])):
         high = value.astype(BF16)
         rest = value - high.astype(F32)
         mid = rest.astype(BF16)
@@ -86,14 +87,14 @@
 
 
 def choose_kernel(planes_ref, *refs):
-    infos, (chosen_ref, info) = refs[:BLOCKS], refs[BLOCKS:]
+    infos, (chosen_ref, info) = refs[:INFOS], refs[INFOS:]
     gather_info(infos, info, 1)
     unused, hits, here = slot_parts(info[0], planes_ref, chosen_ref.shape[1], infos[0].shape[1])
     chosen_ref[...] = (hits & here).astype(F32).astype(BF16)
 
 
 def table_kernel(planes_ref, *refs):
-    infos, (table_ref, info) = refs[:BLOCKS], refs[BLOCKS + 1 :]
+    infos, (table_ref, info) = refs[:INFOS], refs[INFOS + 1 :]
     gather_info(infos, info, 3)
     named, unused, here = slot_parts(info[0], planes_ref, table_ref.shape[2], infos[0].shape[1])
     top = len(named)
@@ -107,7 +108,7 @@
 def from_info(kernel, terms, lead, planes, infos, devices, after=()):
     return pl.pallas_call(
         kernel,
-        in_specs=[SMEM] + [VMEM] * BLOCKS + [ANY] * len(after),
+        in_specs=[SMEM] + [VMEM] * INFOS + [ANY] * len(after),
         out_shape=jax.ShapeDtypeStruct((*lead, BLOCKS * STRIDE, devices * BLOCKS * SLOTS), BF16),
         scratch_shapes=[pltpu.VMEM((terms, BLOCKS * STRIDE, infos[0].shape[0]), F32)],
         compiler_params=params(8),
@@ -243,8 +244,10 @@
 
     info, own = prepare(expert_ids.T, route_weights.T, tokens)
     blocks, infos = [tokens], [info]
-    blocks += [send(tokens, by) for by in range(1, BLOCKS)]
-    infos += [send(info, by) for by in range(1, BLOCKS)]
+    blocks += [send(tokens, 1), send(tokens, 2)]
+    blocks += [send(blocks[1], 2)]
+    infos += [send(info, 1)]
+    infos += [send(jnp.concatenate(infos, axis=0), 2)]
     devices = 2 * depth * width
     chosen = from_info(choose_kernel, 1, (), planes, infos, devices)
     mine = spread(pick(chosen, [own] + blocks[1:], devices))
@@ -254,16 +257,20 @@
     peer_part = run_expert(peer, *matrices, [table])
     returned = spread(join(mine_part, swap(peer_part)))
     shape = tokens.shape
-    own, *others = pl.pallas_call(
+    own, next1, next2, next3 = pl.pallas_call(
         mix_kernel,
-        out_shape=[jax.ShapeDtypeStruct(shape, F32)] + [jax.ShapeDtypeStruct(shape, BF16)] * (BLOCKS - 1),
+        out_shape=[jax.ShapeDtypeStruct(shape, t) for t in (F32, F32, BF16, BF16)],
         compiler_params=params(8),
         cost_estimate=cost(1 << 29, 4 << 20),
     )(table, returned)
-    arrived = [send(value, by, True) for by, value in enumerate(others, 1)]
-    return pl.pallas_call(
-        sum_kernel, out_shape=jax.ShapeDtypeStruct(shape, BF16), compiler_params=params(8)
-    )(own, *arrived)
+
+    def add(*parts):
+        return pl.pallas_call(
+            sum_kernel, out_shape=jax.ShapeDtypeStruct(shape, BF16), compiler_params=params(8)
+        )(*parts)
+
+    next2, next3 = send(next2, 2, True), send(next3, 2, True)
+    return add(own, next2, send(add(next1, next3), 1, True))
 
 
 def solution(mesh):

time: 113 us -> 109 us (0.965)
  waiting for transfers between devices: 19.6 us -> 17.1 us
  starting transfers between devices: 21.7 us -> 20.4 us
    ppermute x9 -> x8, waiting for transfers between devices: 16.7 us -> 14.2 us  [send(): return lax.ppermute(value, ('core', 'z'), route(by, back))]
    ppermute x9 -> x8, starting transfers between devices: 21.4 us -> 20.2 us  [send(): return lax.ppermute(value, ('core', 'z'), route(by, back))]
    pallas_call x4 -> x5, Pallas kernels: 4.23 us -> 4.26 us  [the longest x2 2.6 us: from_info(): pl.pallas_call(kernel, in_specs=[SMEM] + [VMEM] * INFOS + [ANY] * len(aft...]
  transfers between devices with their start and end apart: 11 -> 10, of which waited for: 7 -> 7; matrix products, arithmetic and copies ran while one was open for 0% -> 0% of each run, Pallas kernels for 5% -> 5%
where the time goes in v6:
time: 109 us; the launch traced here: 108 us
  blocking collectives  56.3 us (52%)
  starting transfers between devices  20.4 us (19%)
  waiting for transfers between devices  17.1 us (16%)
  Pallas kernels  11.4 us (10%)
  local copies, waits for them, and re-layouts  2.38 us (2%)
    all_to_all x2, blocking collectives, spread(): lax.all_to_all(value, AXES, 0, 0, axis_index_groups=groups, tiled=True)  56.3 us
    ppermute x8, starting transfers between devices, send(): return lax.ppermute(value, ('core', 'z'), route(by, back))  20.2 us
    ppermute x8, waiting for transfers between devices, send(): return lax.ppermute(value, ('core', 'z'), route(by, back))  14.2 us
    pallas_call x2, Pallas kernels, run_expert(): pl.pallas_call(expert_kernel, in_specs=[VMEM] * 4 + [ANY] * len(after), o...  6.02 us
    ppermute x2, waiting for transfers between devices, swap(): return lax.ppermute(value, 'core', [(0, 1), (1, 0)])  2.95 us
    pallas_call x2, Pallas kernels, from_info(): pl.pallas_call(kernel, in_specs=[SMEM] + [VMEM] * INFOS + [ANY] * len(aft...  2.6 us
    unnamed x12, local copies, waits for them, and re-layouts  2.38 us
  transfers between devices with their start and end apart: 10, of which 7 were waited for; matrix products, arithmetic and copies ran while one was open for 0% of the time, Pallas kernels for 5%

profile of v6, /device:TPU:8, one launch (start us, length us, event | category | flops | bytes accessed | tf_op | source)
XLA Modules:
  0.0 107.8 jit_solution(1754457402651475938)
XLA Ops:
  0.0 5.9 %collective-permute-start.2 = (bf16[20,3584]{1,0:T(8,128)(2,1)}, bf16[20,3584]{1,0:T(8,128)(2,1)S(1)}, u32[]{:S(2)}, u32[]{:S(2)}) collective-permute-start(bf16[20,3584]{1,0:T(8,128)(2,1)} %tokens_ref.1), channel_id=1, source_target_pairs={{0,7},{1,2},{2,1},{3,4},{4,3},{5,6},{6,5},{7,0},{33,32},{34,35},{3... | collective-permute-start | bytes 430088 | tf_op jit(solution)/shard_map/ppermute | solution.py:226
  5.9 1.0 copy-done.3
  6.8 0.7 copy-done.4
  7.5 0.7 copy-done.5
  8.2 2.5 %collective-permute-start = (f32[16,20]{1,0:T(8,128)S(1)}, f32[16,20]{1,0:T(8,128)S(1)}, u32[]{:S(2)}, u32[]{:S(2)}) collective-permute-start(f32[16,20]{1,0:T(8,128)S(1)} %get-tuple-element.11.refs_0_), channel_id=1, source_target_pairs={{0,7},{1,2},{2,1},{3,4},{4,3},{5,6},{6,5},{7,0},{33,32},{34,35},{3... | collective-permute-start | bytes 3848 | tf_op jit(solution)/shard_map/ppermute | solution.py:226
  10.8 2.0 %collective-permute-done.2.refs_1_ = bf16[20,3584]{1,0:T(8,128)(2,1)S(1)} collective-permute-done((bf16[20,3584]{1,0:T(8,128)(2,1)}, bf16[20,3584]{1,0:T(8,128)(2,1)S(1)}, u32[]{:S(2)}, u32[]{:S(2)}) %collective-permute-start.2) | collective-permute-done | bytes 143392 | tf_op jit(solution)/shard_map/ppermute | solution.py:226
  12.7 0.8 collective-permute-done.refs_1_
  13.5 4.8 %collective-permute-start.1 = (f32[32,20]{1,0:T(8,128)S(1)}, f32[32,20]{1,0:T(8,128)S(1)}, u32[]{:S(2)}, u32[]{:S(2)}) collective-permute-start(f32[32,20]{1,0:T(8,128)S(1)} %pad_maximum_fusion), channel_id=1, source_target_pairs={{0,2},{1,7},{2,4},{3,1},{4,6},{5,3},{6,0},{7,5},{33,35},{34,32},{3... | collective-permute-start | bytes 7688 | tf_op jit(solution)/shard_map/ppermute | solution.py:226
  18.4 2.1 %collective-permute-done.1.refs_2_ = f32[32,20]{1,0:T(8,128)S(1)} collective-permute-done((f32[32,20]{1,0:T(8,128)S(1)}, f32[32,20]{1,0:T(8,128)S(1)}, u32[]{:S(2)}, u32[]{:S(2)}) %collective-permute-start.1) | collective-permute-done | bytes 2592 | tf_op jit(solution)/shard_map/ppermute | solution.py:226
  20.4 1.1 %shard_map.65.chosen_ref = bf16[128,256]{1,0:T(8,128)(2,1)S(1)} custom-call(s32[2]{0:T(128)S(1)} %pad_add_fusion.planes_ref, f32[16,20]{1,0:T(8,128)S(1)} %get-tuple-element.11.refs_0_, f32[16,20]{1,0:T(8,128)S(1)} %collective-permute-done.refs_1_, f32[32,20]{1,0:T(8,128)S(1)} %collective-permute-done.1.refs_2_), custom_call_target="tpu_custom_call" | custom-call | flops 4194304 | bytes 262144 | tf_op jit(solution)/shard_map/pallas_call | solution.py:109
  21.6 0.7 shard_map.66
  22.3 27.8 %all_to_all.10.refs_3_.rows_ref = bf16[32,8,3584]{2,1,0:T(8,128)(2,1)S(1)} all-to-all(bf16[32,8,3584]{2,1,0:T(8,128)(2,1)S(1)} %shard_map.66), channel_id=1, replica_groups={{0,1,64,65,128,129,192,193,8,9,72,73,136,137,200,201,16,17,80,81,144,14..., dimensions={0} | all-to-all | bytes 3670016 | tf_op jit(solution)/shard_map/all_to_all | solution.py:240
  50.1 1.5 %shard_map.67.refs_0_.table_ref = bf16[3,128,256]{2,1,0:T(8,128)(2,1)S(1)} custom-call(s32[2]{0:T(128)S(1)} %pad_add_fusion.planes_ref, f32[16,20]{1,0:T(8,128)S(1)} %get-tuple-element.11.refs_0_, f32[16,20]{1,0:T(8,128)S(1)} %collective-permute-done.refs_1_, f32[32,20]{1,0:T(8,128)S(1)} %collective-permute-done.1.refs_2_, ...), custom_call_target="tpu_custom_call" | custom-call | flops 4194304 | bytes 262144 | tf_op jit(solution)/shard_map/pallas_call | solution.py:109
  51.6 2.3 %collective-permute-done.5.rows_ref = bf16[32,8,3584]{2,1,0:T(8,128)(2,1)S(1)} collective-permute-done((bf16[32,8,3584]{2,1,0:T(8,128)(2,1)S(1)}, bf16[32,8,3584]{2,1,0:T(8,128)(2,1)S(1)}, u32[]{:S(2)}, u32[]{:S(2)}) %collective-permute-start.5) | collective-permute-done | bytes 1835040 | tf_op jit(solution)/shard_map/ppermute | solution.py:243
  53.9 3.0 %shard_map.69 = bf16[32,8,3584]{2,1,0:T(8,128)(2,1)S(1)} custom-call(bf16[32,8,3584]{2,1,0:T(8,128)(2,1)S(1)} %collective-permute-done.5.rows_ref, bf16[3584,512]{1,0:T(8,128)(2,1)S(1)} %bitcast.7, bf16[3584,512]{1,0:T(8,128)(2,1)S(1)} %bitcast.9, bf16[512,3584]{1,0:T(8,128)(2,1)S(1)} %bitcast.11, bf16[3,128,256]{2,1,0:T(8,128)(2,1)S(1)} %shard_map.67.refs_0_.table_ref), custom_call_target="tpu_custom_call" | custom-call | flops 2818572288 | bytes 15728640 | tf_op jit(solution)/shard_map/pallas_call | solution.py:197
  57.2 3.0 %shard_map.68.mine_ref = bf16[32,8,3584]{2,1,0:T(8,128)(2,1)S(1)} custom-call(bf16[32,8,3584]{2,1,0:T(8,128)(2,1)S(1)} %all_to_all.10.refs_3_.rows_ref, bf16[3584,512]{1,0:T(8,128)(2,1)S(1)} %bitcast.8, bf16[3584,512]{1,0:T(8,128)(2,1)S(1)} %bitcast.10, bf16[512,3584]{1,0:T(8,128)(2,1)S(1)} %bitcast.12), custom_call_target="tpu_custom_call" | custom-call | flops 2818572288 | bytes 15728640 | tf_op jit(solution)/shard_map/pallas_call | solution.py:197
  61.2 28.5 %all_to_all.11.rows_ref = bf16[32,8,3584]{2,1,0:T(8,128)(2,1)S(1)} all-to-all(bf16[32,8,3584]{2,1,0:T(8,128)(2,1)S(1)} %shard_map.70), channel_id=1, replica_groups={{0,1,64,65,128,129,192,193,8,9,72,73,136,137,200,201,16,17,80,81,144,14..., dimensions={0} | all-to-all | bytes 3670016 | tf_op jit(solution)/shard_map/all_to_all | solution.py:240
  89.8 0.9 shard_map.71
  90.7 3.4 %collective-permute-start.8 = (bf16[20,3584]{1,0:T(8,128)(2,1)S(1)}, bf16[20,3584]{1,0:T(8,128)(2,1)S(1)}, u32[]{:S(2)}, u32[]{:S(2)}) collective-permute-start(bf16[20,3584]{1,0:T(8,128)(2,1)S(1)} %get-tuple-element.16), channel_id=1, source_target_pairs={{2,0},{7,1},{4,2},{1,3},{6,4},{3,5},{0,6},{5,7},{35,33},{32,34},{3... | collective-permute-start | bytes 430088 | tf_op jit(solution)/shard_map/ppermute | solution.py:226
  94.1 0.8 collective-permute-start.7
  94.9 5.4 %collective-permute-done.8.refs_0_ = bf16[20,3584]{1,0:T(8,128)(2,1)S(1)} collective-permute-done((bf16[20,3584]{1,0:T(8,128)(2,1)S(1)}, bf16[20,3584]{1,0:T(8,128)(2,1)S(1)}, u32[]{:S(2)}, u32[]{:S(2)}) %collective-permute-start.8) | collective-permute-done | bytes 143392 | tf_op jit(solution)/shard_map/ppermute | solution.py:226
  100.3 2.8 %collective-permute-start.9 = (bf16[20,3584]{1,0:T(8,128)(2,1)S(1)}, bf16[20,3584]{1,0:T(8,128)(2,1)S(1)}, u32[]{:S(2)}, u32[]{:S(2)}) collective-permute-start(bf16[20,3584]{1,0:T(8,128)(2,1)S(1)} %shard_map.72), channel_id=1, source_target_pairs={{7,0},{2,1},{1,2},{4,3},{3,4},{6,5},{5,6},{0,7},{32,33},{35,34},{3... | collective-permute-start | bytes 430088 | tf_op jit(solution)/shard_map/ppermute | solution.py:226
  103.2 3.9 %collective-permute-done.9.refs_1_ = bf16[20,3584]{1,0:T(8,128)(2,1)S(1)} collective-permute-done((bf16[20,3584]{1,0:T(8,128)(2,1)S(1)}, bf16[20,3584]{1,0:T(8,128)(2,1)S(1)}, u32[]{:S(2)}, u32[]{:S(2)}) %collective-permute-start.9) | collective-permute-done | bytes 143392 | tf_op jit(solution)/shard_map/ppermute | solution.py:226
  107.1 0.7 shard_map.73
  (22 shorter events, 1.4 us)
Async XLA Ops:
  0.0 12.7 %collective-permute-start.2 = (bf16[20,3584]{1,0:T(8,128)(2,1)}, bf16[20,3584]{1,0:T(8,128)(2,1)S(1)}, u32[]{:S(2)}, u32[]{:S(2)}) collective-permute-start(bf16[20,3584]{1,0:T(8,128)(2,1)} %tokens_ref.1), channel_id=1, source_target_pairs={{0,7},{1,2},{2,1},{3,4},{4,3},{5,6},{6,5},{7,0},{33,32},{34,35},{3... | collective-permute-start | bytes 430088 | tf_op jit(solution)/shard_map/ppermute | solution.py:226
  5.9 15.7 %collective-permute-start.3 = (bf16[20,3584]{1,0:T(8,128)(2,1)}, bf16[20,3584]{1,0:T(8,128)(2,1)S(1)}, u32[]{:S(2)}, u32[]{:S(2)}) collective-permute-start(bf16[20,3584]{1,0:T(8,128)(2,1)} %tokens_ref.1), channel_id=1, source_target_pairs={{0,2},{1,7},{2,4},{3,1},{4,6},{5,3},{6,0},{7,5},{33,35},{34,32},{3... | collective-permute-start | bytes 430088 | tf_op jit(solution)/shard_map/ppermute | solution.py:226
  5.9 1.0 copy-start.3
  6.8 0.7 copy-start.4
  7.5 0.7 copy-start.5
  8.2 5.3 %collective-permute-start = (f32[16,20]{1,0:T(8,128)S(1)}, f32[16,20]{1,0:T(8,128)S(1)}, u32[]{:S(2)}, u32[]{:S(2)}) collective-permute-start(f32[16,20]{1,0:T(8,128)S(1)} %get-tuple-element.11.refs_0_), channel_id=1, source_target_pairs={{0,7},{1,2},{2,1},{3,4},{4,3},{5,6},{6,5},{7,0},{33,32},{34,35},{3... | collective-permute-start | bytes 3848 | tf_op jit(solution)/shard_map/ppermute | solution.py:226
  12.7 8.9 %collective-permute-start.4 = (bf16[20,3584]{1,0:T(8,128)(2,1)S(1)}, bf16[20,3584]{1,0:T(8,128)(2,1)S(1)}, u32[]{:S(2)}, u32[]{:S(2)}) collective-permute-start(bf16[20,3584]{1,0:T(8,128)(2,1)S(1)} %collective-permute-done.2.refs_1_), channel_id=1, source_target_pairs={{0,2},{1,7},{2,4},{3,1},{4,6},{5,3},{6,0},{7,5},{33,35},{34,32},{3... | collective-permute-start | bytes 430088 | tf_op jit(solution)/shard_map/ppermute | solution.py:226
  13.5 6.9 %collective-permute-start.1 = (f32[32,20]{1,0:T(8,128)S(1)}, f32[32,20]{1,0:T(8,128)S(1)}, u32[]{:S(2)}, u32[]{:S(2)}) collective-permute-start(f32[32,20]{1,0:T(8,128)S(1)} %pad_maximum_fusion), channel_id=1, source_target_pairs={{0,2},{1,7},{2,4},{3,1},{4,6},{5,3},{6,0},{7,5},{33,35},{34,32},{3... | collective-permute-start | bytes 7688 | tf_op jit(solution)/shard_map/ppermute | solution.py:226
  21.6 32.3 %copy-start.1 = (bf16[1,1,3584,512]{3,2,1,0:T(8,128)(2,1)S(1)}, bf16[1,1,3584,512]{3,2,1,0:T(8,128)(2,1)}, u32[]{:S(2)}) copy-start(bf16[1,1,3584,512]{3,2,1,0:T(8,128)(2,1)} %param.10) | copy-start | bytes 11010052
  21.6 32.3 %copy-start.2 = (bf16[1,1,512,3584]{3,2,1,0:T(8,128)(2,1)S(1)}, bf16[1,1,512,3584]{3,2,1,0:T(8,128)(2,1)}, u32[]{:S(2)}) copy-start(bf16[1,1,512,3584]{3,2,1,0:T(8,128)(2,1)} %param.11) | copy-start | bytes 11010052
  22.3 31.6 %copy-start = (bf16[1,1,3584,512]{3,2,1,0:T(8,128)(2,1)S(1)}, bf16[1,1,3584,512]{3,2,1,0:T(8,128)(2,1)}, u32[]{:S(2)}) copy-start(bf16[1,1,3584,512]{3,2,1,0:T(8,128)(2,1)} %param.9) | copy-start | bytes 11010052
  50.1 3.8 %collective-permute-start.5 = (bf16[32,8,3584]{2,1,0:T(8,128)(2,1)S(1)}, bf16[32,8,3584]{2,1,0:T(8,128)(2,1)S(1)}, u32[]{:S(2)}, u32[]{:S(2)}) collective-permute-start(bf16[32,8,3584]{2,1,0:T(8,128)(2,1)S(1)} %all_to_all.10.refs_3_.rows_ref), channel_id=1, source_target_pairs={{0,32},{32,0},{1,33},{33,1},{2,34},{34,2},{3,35},{35,3},{4,36},{36... | collective-permute-start | bytes 5505032 | tf_op jit(solution)/shard_map/ppermute | solution.py:243
  56.9 3.9 %collective-permute-start.6 = (bf16[32,8,3584]{2,1,0:T(8,128)(2,1)S(1)}, bf16[32,8,3584]{2,1,0:T(8,128)(2,1)S(1)}, u32[]{:S(2)}, u32[]{:S(2)}) collective-permute-start(bf16[32,8,3584]{2,1,0:T(8,128)(2,1)S(1)} %shard_map.69), channel_id=1, source_target_pairs={{0,32},{32,0},{1,33},{33,1},{2,34},{34,2},{3,35},{35,3},{4,36},{36... | collective-permute-start | bytes 5505032 | tf_op jit(solution)/shard_map/ppermute | solution.py:243
  90.7 9.6 %collective-permute-start.8 = (bf16[20,3584]{1,0:T(8,128)(2,1)S(1)}, bf16[20,3584]{1,0:T(8,128)(2,1)S(1)}, u32[]{:S(2)}, u32[]{:S(2)}) collective-permute-start(bf16[20,3584]{1,0:T(8,128)(2,1)S(1)} %get-tuple-element.16), channel_id=1, source_target_pairs={{2,0},{7,1},{4,2},{1,3},{6,4},{3,5},{0,6},{5,7},{35,33},{32,34},{3... | collective-permute-start | bytes 430088 | tf_op jit(solution)/shard_map/ppermute | solution.py:226
  94.1 9.1 %collective-permute-start.7 = (bf16[20,3584]{1,0:T(8,128)(2,1)S(1)}, bf16[20,3584]{1,0:T(8,128)(2,1)S(1)}, u32[]{:S(2)}, u32[]{:S(2)}) collective-permute-start(bf16[20,3584]{1,0:T(8,128)(2,1)S(1)} %get-tuple-element.14), channel_id=1, source_target_pairs={{2,0},{7,1},{4,2},{1,3},{6,4},{3,5},{0,6},{5,7},{35,33},{32,34},{3... | collective-permute-start | bytes 430088 | tf_op jit(solution)/shard_map/ppermute | solution.py:226
  100.3 6.7 %collective-permute-start.9 = (bf16[20,3584]{1,0:T(8,128)(2,1)S(1)}, bf16[20,3584]{1,0:T(8,128)(2,1)S(1)}, u32[]{:S(2)}, u32[]{:S(2)}) collective-permute-start(bf16[20,3584]{1,0:T(8,128)(2,1)S(1)} %shard_map.72), channel_id=1, source_target_pairs={{7,0},{2,1},{1,2},{4,3},{3,4},{6,5},{5,6},{0,7},{32,33},{35,34},{3... | collective-permute-start | bytes 430088 | tf_op jit(solution)/shard_map/ppermute | solution.py:226

commit v7 on v6

--- a/solution.py
+++ b/solution.py
@@ -67,23 +67,33 @@
             scratch[place, b * STRIDE : b * STRIDE + value.shape[1]] = upright(piece)
 
 
-def prepare_kernel(ids_ref, weights_ref, tokens_ref, info_ref, own_ref):
+def prepare_kernel(ids_ref, weights_ref, info_ref):
     top = ids_ref.shape[0]
     info_ref[:top] = ids_ref[...].astype(F32)
     info_ref[top:] = weights_ref[...]
-    own_ref[...] = tokens_ref[...]
-
-
-def prepare(ids, weights, tokens):
+
+
+def prepare(ids, weights):
     return pl.pallas_call(
         prepare_kernel,
-        out_shape=[
-            jax.ShapeDtypeStruct((2 * ids.shape[0], ids.shape[1]), F32),
-            jax.ShapeDtypeStruct(tokens.shape, BF16),
-        ],
+        out_shape=jax.ShapeDtypeStruct((2 * ids.shape[0], ids.shape[1]), F32),
         compiler_params=params(PREPARE_MIB),
         cost_estimate=cost(0, 1 << 18),
-    )(ids, weights, tokens)
+    )(ids, weights)
+
+
+def keep_kernel(tokens_ref, unused_ref, own_ref):
+    own_ref[...] = tokens_ref[...]
+
+
+def keep(tokens, after):
+    return pl.pallas_call(
+        keep_kernel,
+        in_specs=[VMEM, ANY],
+        out_shape=jax.ShapeDtypeStruct(tokens.shape, BF16),
+        compiler_params=params(PREPARE_MIB),
+        cost_estimate=cost(0, 1 << 18),
+    )(tokens, after)
 
 
 def choose_kernel(planes_ref, *refs):
@@ -242,7 +252,8 @@
     def swap(value):
         return lax.ppermute(value, "core", [(0, 1), (1, 0)])
 
-    info, own = prepare(expert_ids.T, route_weights.T, tokens)
+    info = prepare(expert_ids.T, route_weights.T)
+    own = keep(tokens, info)
     blocks, infos = [tokens], [info]
     blocks += [send(tokens, 1), send(tokens, 2)]
     blocks += [send(blocks[1], 2)]

time: 109 us -> 109 us (level)
  no operation moved by 1% of the time
where the time goes in v7:
time: 109 us; the launch traced here: 108 us
  blocking collectives  56 us (51%)
  starting transfers between devices  21.2 us (19%)
  waiting for transfers between devices  16.7 us (15%)
  Pallas kernels  11.4 us (10%)
  local copies, waits for them, and re-layouts  2.31 us (2%)
    all_to_all x2, blocking collectives, spread(): lax.all_to_all(value, AXES, 0, 0, axis_index_groups=groups, tiled=True)  56 us
    ppermute x8, starting transfers between devices, send(): return lax.ppermute(value, ('core', 'z'), route(by, back))  20.9 us
    ppermute x8, waiting for transfers between devices, send(): return lax.ppermute(value, ('core', 'z'), route(by, back))  13.7 us
    pallas_call x2, Pallas kernels, run_expert(): pl.pallas_call(expert_kernel, in_specs=[VMEM] * 4 + [ANY] * len(after), o...  6.02 us
    ppermute x2, waiting for transfers between devices, swap(): return lax.ppermute(value, 'core', [(0, 1), (1, 0)])  2.95 us
    pallas_call x2, Pallas kernels, from_info(): pl.pallas_call(kernel, in_specs=[SMEM] + [VMEM] * INFOS + [ANY] * len(aft...  2.6 us
    unnamed x12, local copies, waits for them, and re-layouts  2.31 us
  transfers between devices with their start and end apart: 10, of which 7 were waited for; matrix products, arithmetic and copies ran while one was open for 0% of the time, Pallas kernels for 5%

profile of v7, /device:TPU:8, one launch (start us, length us, event | category | flops | bytes accessed | tf_op | source)
XLA Modules:
  0.0 107.8 jit_solution(1964416518390764903)
XLA Ops:
  0.0 5.9 %collective-permute-start.2 = (bf16[20,3584]{1,0:T(8,128)(2,1)}, bf16[20,3584]{1,0:T(8,128)(2,1)S(1)}, u32[]{:S(2)}, u32[]{:S(2)}) collective-permute-start(bf16[20,3584]{1,0:T(8,128)(2,1)} %tokens_ref.1), channel_id=1, source_target_pairs={{0,7},{1,2},{2,1},{3,4},{4,3},{5,6},{6,5},{7,0},{33,32},{34,35},{3... | collective-permute-start | bytes 430088 | tf_op jit(solution)/shard_map/ppermute | solution.py:236
  5.9 0.7 copy-done.4
  6.6 0.7 copy-done.5
  7.2 2.5 %collective-permute-start = (f32[16,20]{1,0:T(8,128)S(1)}, f32[16,20]{1,0:T(8,128)S(1)}, u32[]{:S(2)}, u32[]{:S(2)}) collective-permute-start(f32[16,20]{1,0:T(8,128)S(1)} %shard_map.64.refs_0_.unused_ref), channel_id=1, source_target_pairs={{0,7},{1,2},{2,1},{3,4},{4,3},{5,6},{6,5},{7,0},{33,32},{34,35},{3... | collective-permute-start | bytes 3848 | tf_op jit(solution)/shard_map/ppermute | solution.py:236
  9.7 3.0 %collective-permute-done.2.refs_1_ = bf16[20,3584]{1,0:T(8,128)(2,1)S(1)} collective-permute-done((bf16[20,3584]{1,0:T(8,128)(2,1)}, bf16[20,3584]{1,0:T(8,128)(2,1)S(1)}, u32[]{:S(2)}, u32[]{:S(2)}) %collective-permute-start.2) | collective-permute-done | bytes 143392 | tf_op jit(solution)/shard_map/ppermute | solution.py:236
  12.8 5.5 %collective-permute-start.1 = (f32[32,20]{1,0:T(8,128)S(1)}, f32[32,20]{1,0:T(8,128)S(1)}, u32[]{:S(2)}, u32[]{:S(2)}) collective-permute-start(f32[32,20]{1,0:T(8,128)S(1)} %pad_maximum_fusion), channel_id=1, source_target_pairs={{0,2},{1,7},{2,4},{3,1},{4,6},{5,3},{6,0},{7,5},{33,35},{34,32},{3... | collective-permute-start | bytes 7688 | tf_op jit(solution)/shard_map/ppermute | solution.py:236
  18.4 0.9 copy-done.3
  19.3 1.1 %collective-permute-done.1.refs_2_ = f32[32,20]{1,0:T(8,128)S(1)} collective-permute-done((f32[32,20]{1,0:T(8,128)S(1)}, f32[32,20]{1,0:T(8,128)S(1)}, u32[]{:S(2)}, u32[]{:S(2)}) %collective-permute-start.1) | collective-permute-done | bytes 2592 | tf_op jit(solution)/shard_map/ppermute | solution.py:236
  20.4 1.1 %shard_map.65.chosen_ref = bf16[128,256]{1,0:T(8,128)(2,1)S(1)} custom-call(s32[2]{0:T(128)S(1)} %pad_add_fusion.planes_ref, f32[16,20]{1,0:T(8,128)S(1)} %shard_map.64.refs_0_.unused_ref, f32[16,20]{1,0:T(8,128)S(1)} %collective-permute-done.refs_1_, f32[32,20]{1,0:T(8,128)S(1)} %collective-permute-done.1.refs_2_), custom_call_target="tpu_custom_call" | custom-call | flops 4194304 | bytes 262144 | tf_op jit(solution)/shard_map/pallas_call | solution.py:119
  21.6 0.7 shard_map.67
  22.3 27.7 %all_to_all.10.refs_3_.rows_ref = bf16[32,8,3584]{2,1,0:T(8,128)(2,1)S(1)} all-to-all(bf16[32,8,3584]{2,1,0:T(8,128)(2,1)S(1)} %shard_map.67), channel_id=1, replica_groups={{0,1,64,65,128,129,192,193,8,9,72,73,136,137,200,201,16,17,80,81,144,14..., dimensions={0} | all-to-all | bytes 3670016 | tf_op jit(solution)/shard_map/all_to_all | solution.py:250
  50.0 1.5 %shard_map.68.refs_0_.table_ref = bf16[3,128,256]{2,1,0:T(8,128)(2,1)S(1)} custom-call(s32[2]{0:T(128)S(1)} %pad_add_fusion.planes_ref, f32[16,20]{1,0:T(8,128)S(1)} %shard_map.64.refs_0_.unused_ref, f32[16,20]{1,0:T(8,128)S(1)} %collective-permute-done.refs_1_, f32[32,20]{1,0:T(8,128)S(1)} %collective-permute-done.1.refs_2_, ...), custom_call_target="tpu_custom_call" | custom-call | flops 4194304 | bytes 262144 | tf_op jit(solution)/shard_map/pallas_call | solution.py:119
  51.5 2.3 %collective-permute-done.5.rows_ref = bf16[32,8,3584]{2,1,0:T(8,128)(2,1)S(1)} collective-permute-done((bf16[32,8,3584]{2,1,0:T(8,128)(2,1)S(1)}, bf16[32,8,3584]{2,1,0:T(8,128)(2,1)S(1)}, u32[]{:S(2)}, u32[]{:S(2)}) %collective-permute-start.5) | collective-permute-done | bytes 1835040 | tf_op jit(solution)/shard_map/ppermute | solution.py:253
  53.8 3.0 %shard_map.70 = bf16[32,8,3584]{2,1,0:T(8,128)(2,1)S(1)} custom-call(bf16[32,8,3584]{2,1,0:T(8,128)(2,1)S(1)} %collective-permute-done.5.rows_ref, bf16[3584,512]{1,0:T(8,128)(2,1)S(1)} %bitcast.7, bf16[3584,512]{1,0:T(8,128)(2,1)S(1)} %bitcast.9, bf16[512,3584]{1,0:T(8,128)(2,1)S(1)} %bitcast.11, bf16[3,128,256]{2,1,0:T(8,128)(2,1)S(1)} %shard_map.68.refs_0_.table_ref), custom_call_target="tpu_custom_call" | custom-call | flops 2818572288 | bytes 15728640 | tf_op jit(solution)/shard_map/pallas_call | solution.py:207
  57.0 3.0 %shard_map.69.mine_ref = bf16[32,8,3584]{2,1,0:T(8,128)(2,1)S(1)} custom-call(bf16[32,8,3584]{2,1,0:T(8,128)(2,1)S(1)} %all_to_all.10.refs_3_.rows_ref, bf16[3584,512]{1,0:T(8,128)(2,1)S(1)} %bitcast.8, bf16[3584,512]{1,0:T(8,128)(2,1)S(1)} %bitcast.10, bf16[512,3584]{1,0:T(8,128)(2,1)S(1)} %bitcast.12), custom_call_target="tpu_custom_call" | custom-call | flops 2818572288 | bytes 15728640 | tf_op jit(solution)/shard_map/pallas_call | solution.py:207
  60.1 0.6 collective-permute-done.6.other_ref
  61.1 28.4 %all_to_all.11.rows_ref = bf16[32,8,3584]{2,1,0:T(8,128)(2,1)S(1)} all-to-all(bf16[32,8,3584]{2,1,0:T(8,128)(2,1)S(1)} %shard_map.71), channel_id=1, replica_groups={{0,1,64,65,128,129,192,193,8,9,72,73,136,137,200,201,16,17,80,81,144,14..., dimensions={0} | all-to-all | bytes 3670016 | tf_op jit(solution)/shard_map/all_to_all | solution.py:250
  89.5 0.9 shard_map.72
  90.3 3.8 %collective-permute-start.8 = (bf16[20,3584]{1,0:T(8,128)(2,1)S(1)}, bf16[20,3584]{1,0:T(8,128)(2,1)S(1)}, u32[]{:S(2)}, u32[]{:S(2)}) collective-permute-start(bf16[20,3584]{1,0:T(8,128)(2,1)S(1)} %get-tuple-element.12), channel_id=1, source_target_pairs={{2,0},{7,1},{4,2},{1,3},{6,4},{3,5},{0,6},{5,7},{35,33},{32,34},{3... | collective-permute-start | bytes 430088 | tf_op jit(solution)/shard_map/ppermute | solution.py:236
  94.1 0.8 collective-permute-start.7
  94.9 5.4 %collective-permute-done.8.refs_0_ = bf16[20,3584]{1,0:T(8,128)(2,1)S(1)} collective-permute-done((bf16[20,3584]{1,0:T(8,128)(2,1)S(1)}, bf16[20,3584]{1,0:T(8,128)(2,1)S(1)}, u32[]{:S(2)}, u32[]{:S(2)}) %collective-permute-start.8) | collective-permute-done | bytes 143392 | tf_op jit(solution)/shard_map/ppermute | solution.py:236
  100.3 2.6 %collective-permute-start.9 = (bf16[20,3584]{1,0:T(8,128)(2,1)S(1)}, bf16[20,3584]{1,0:T(8,128)(2,1)S(1)}, u32[]{:S(2)}, u32[]{:S(2)}) collective-permute-start(bf16[20,3584]{1,0:T(8,128)(2,1)S(1)} %shard_map.73), channel_id=1, source_target_pairs={{7,0},{2,1},{1,2},{4,3},{3,4},{6,5},{5,6},{0,7},{32,33},{35,34},{3... | collective-permute-start | bytes 430088 | tf_op jit(solution)/shard_map/ppermute | solution.py:236
  103.0 4.1 %collective-permute-done.9.refs_1_ = bf16[20,3584]{1,0:T(8,128)(2,1)S(1)} collective-permute-done((bf16[20,3584]{1,0:T(8,128)(2,1)S(1)}, bf16[20,3584]{1,0:T(8,128)(2,1)S(1)}, u32[]{:S(2)}, u32[]{:S(2)}) %collective-permute-start.9) | collective-permute-done | bytes 143392 | tf_op jit(solution)/shard_map/ppermute | solution.py:236
  107.0 0.7 shard_map.74
  (23 shorter events, 0.9 us)
Async XLA Ops:
  0.0 12.7 %collective-permute-start.2 = (bf16[20,3584]{1,0:T(8,128)(2,1)}, bf16[20,3584]{1,0:T(8,128)(2,1)S(1)}, u32[]{:S(2)}, u32[]{:S(2)}) collective-permute-start(bf16[20,3584]{1,0:T(8,128)(2,1)} %tokens_ref.1), channel_id=1, source_target_pairs={{0,7},{1,2},{2,1},{3,4},{4,3},{5,6},{6,5},{7,0},{33,32},{34,35},{3... | collective-permute-start | bytes 430088 | tf_op jit(solution)/shard_map/ppermute | solution.py:236
  5.9 15.7 %collective-permute-start.3 = (bf16[20,3584]{1,0:T(8,128)(2,1)}, bf16[20,3584]{1,0:T(8,128)(2,1)S(1)}, u32[]{:S(2)}, u32[]{:S(2)}) collective-permute-start(bf16[20,3584]{1,0:T(8,128)(2,1)} %tokens_ref.1), channel_id=1, source_target_pairs={{0,2},{1,7},{2,4},{3,1},{4,6},{5,3},{6,0},{7,5},{33,35},{34,32},{3... | collective-permute-start | bytes 430088 | tf_op jit(solution)/shard_map/ppermute | solution.py:236
  5.9 0.7 copy-start.4
  6.5 0.7 copy-start.5
  7.2 5.6 %collective-permute-start = (f32[16,20]{1,0:T(8,128)S(1)}, f32[16,20]{1,0:T(8,128)S(1)}, u32[]{:S(2)}, u32[]{:S(2)}) collective-permute-start(f32[16,20]{1,0:T(8,128)S(1)} %shard_map.64.refs_0_.unused_ref), channel_id=1, source_target_pairs={{0,7},{1,2},{2,1},{3,4},{4,3},{5,6},{6,5},{7,0},{33,32},{34,35},{3... | collective-permute-start | bytes 3848 | tf_op jit(solution)/shard_map/ppermute | solution.py:236
  12.7 8.9 %collective-permute-start.4 = (bf16[20,3584]{1,0:T(8,128)(2,1)S(1)}, bf16[20,3584]{1,0:T(8,128)(2,1)S(1)}, u32[]{:S(2)}, u32[]{:S(2)}) collective-permute-start(bf16[20,3584]{1,0:T(8,128)(2,1)S(1)} %collective-permute-done.2.refs_1_), channel_id=1, source_target_pairs={{0,2},{1,7},{2,4},{3,1},{4,6},{5,3},{6,0},{7,5},{33,35},{34,32},{3... | collective-permute-start | bytes 430088 | tf_op jit(solution)/shard_map/ppermute | solution.py:236
  12.8 7.6 %collective-permute-start.1 = (f32[32,20]{1,0:T(8,128)S(1)}, f32[32,20]{1,0:T(8,128)S(1)}, u32[]{:S(2)}, u32[]{:S(2)}) collective-permute-start(f32[32,20]{1,0:T(8,128)S(1)} %pad_maximum_fusion), channel_id=1, source_target_pairs={{0,2},{1,7},{2,4},{3,1},{4,6},{5,3},{6,0},{7,5},{33,35},{34,32},{3... | collective-permute-start | bytes 7688 | tf_op jit(solution)/shard_map/ppermute | solution.py:236
  18.4 0.9 copy-start.3
  21.6 32.2 %copy-start.1 = (bf16[1,1,3584,512]{3,2,1,0:T(8,128)(2,1)S(1)}, bf16[1,1,3584,512]{3,2,1,0:T(8,128)(2,1)}, u32[]{:S(2)}) copy-start(bf16[1,1,3584,512]{3,2,1,0:T(8,128)(2,1)} %param.10) | copy-start | bytes 11010052
  21.6 32.2 %copy-start.2 = (bf16[1,1,512,3584]{3,2,1,0:T(8,128)(2,1)S(1)}, bf16[1,1,512,3584]{3,2,1,0:T(8,128)(2,1)}, u32[]{:S(2)}) copy-start(bf16[1,1,512,3584]{3,2,1,0:T(8,128)(2,1)} %param.11) | copy-start | bytes 11010052
  22.3 31.5 %copy-start = (bf16[1,1,3584,512]{3,2,1,0:T(8,128)(2,1)S(1)}, bf16[1,1,3584,512]{3,2,1,0:T(8,128)(2,1)}, u32[]{:S(2)}) copy-start(bf16[1,1,3584,512]{3,2,1,0:T(8,128)(2,1)} %param.9) | copy-start | bytes 11010052
  50.0 3.8 %collective-permute-start.5 = (bf16[32,8,3584]{2,1,0:T(8,128)(2,1)S(1)}, bf16[32,8,3584]{2,1,0:T(8,128)(2,1)S(1)}, u32[]{:S(2)}, u32[]{:S(2)}) collective-permute-start(bf16[32,8,3584]{2,1,0:T(8,128)(2,1)S(1)} %all_to_all.10.refs_3_.rows_ref), channel_id=1, source_target_pairs={{0,32},{32,0},{1,33},{33,1},{2,34},{34,2},{3,35},{35,3},{4,36},{36... | collective-permute-start | bytes 5505032 | tf_op jit(solution)/shard_map/ppermute | solution.py:253
  56.8 3.9 %collective-permute-start.6 = (bf16[32,8,3584]{2,1,0:T(8,128)(2,1)S(1)}, bf16[32,8,3584]{2,1,0:T(8,128)(2,1)S(1)}, u32[]{:S(2)}, u32[]{:S(2)}) collective-permute-start(bf16[32,8,3584]{2,1,0:T(8,128)(2,1)S(1)} %shard_map.70), channel_id=1, source_target_pairs={{0,32},{32,0},{1,33},{33,1},{2,34},{34,2},{3,35},{35,3},{4,36},{36... | collective-permute-start | bytes 5505032 | tf_op jit(solution)/shard_map/ppermute | solution.py:253
  90.3 9.9 %collective-permute-start.8 = (bf16[20,3584]{1,0:T(8,128)(2,1)S(1)}, bf16[20,3584]{1,0:T(8,128)(2,1)S(1)}, u32[]{:S(2)}, u32[]{:S(2)}) collective-permute-start(bf16[20,3584]{1,0:T(8,128)(2,1)S(1)} %get-tuple-element.12), channel_id=1, source_target_pairs={{2,0},{7,1},{4,2},{1,3},{6,4},{3,5},{0,6},{5,7},{35,33},{32,34},{3... | collective-permute-start | bytes 430088 | tf_op jit(solution)/shard_map/ppermute | solution.py:236
  94.1 8.9 %collective-permute-start.7 = (bf16[20,3584]{1,0:T(8,128)(2,1)S(1)}, bf16[20,3584]{1,0:T(8,128)(2,1)S(1)}, u32[]{:S(2)}, u32[]{:S(2)}) collective-permute-start(bf16[20,3584]{1,0:T(8,128)(2,1)S(1)} %get-tuple-element.10), channel_id=1, source_target_pairs={{2,0},{7,1},{4,2},{1,3},{6,4},{3,5},{0,6},{5,7},{35,33},{32,34},{3... | collective-permute-start | bytes 430088 | tf_op jit(solution)/shard_map/ppermute | solution.py:236
  100.3 6.7 %collective-permute-start.9 = (bf16[20,3584]{1,0:T(8,128)(2,1)S(1)}, bf16[20,3584]{1,0:T(8,128)(2,1)S(1)}, u32[]{:S(2)}, u32[]{:S(2)}) collective-permute-start(bf16[20,3584]{1,0:T(8,128)(2,1)S(1)} %shard_map.73), channel_id=1, source_target_pairs={{7,0},{2,1},{1,2},{4,3},{3,4},{6,5},{5,6},{0,7},{32,33},{35,34},{3... | collective-permute-start | bytes 430088 | tf_op jit(solution)/shard_map/ppermute | solution.py:236
